TPU v7x, 32 devices: a whole 2x2x4 slice. The times are simulated.
32 devices in a mesh: dp: 8 (over z, x), tensor: 4 (over y, core).
Axes of the slice: x: 2, y: 2, z: 4, core: 2. Of those that a mesh axis runs over, the one named last changes fastest.
Arguments:
- gradient_table: bfloat16 [512, 4096], P('dp', 'tensor'), may hold values from -384 to 384
- residual_input_rows: bfloat16 [512, 4096], P('dp', 'tensor'), may hold values from -6 to 6
- act: bfloat16 [8192, 7168], P('dp', 'tensor'), may hold values from -6 to 6
- down_weight: bfloat16 [7168, 4096], P('tensor'), may hold values from -0.0625 to 0.0625
- adapter_input_factor: bfloat16 [7168, 16], P('tensor'), may hold values from -0.0625 to 0.0625
- adapter_output_factor: bfloat16 [16, 4096], replicated, may hold values from -0.75 to 0.75
- lengths: int32 [8, 64], P('dp'), may hold values from 1 to 256, 1024 in all within a row
- owning_row_index: int32 [512], replicated, may hold values from 0 to 511, as said below
Outputs:
- activation_gradient: bfloat16 [512, 7168], P('dp', 'tensor')
- adapter_input_gradient: float32 [7168, 16], P('tensor')
- adapter_output_gradient: float32 [16, 4096], P(None, 'tensor')
Inputs may be any that keep to these rules, and one draw needn't show every extreme that they name: owning_row_index is a permutation of the passages; every loss owner block of 64 rows holds at most 8 passages of any one packed row, and exactly 8 for some row.
All inputs are finite; a program needn't handle non-finite values.
Results may differ from a plain program's by a relative error of at most 0.0054.
Values may be sent and summed in bfloat16 or wider, within the bound.
No kernel may reach another device: no remote copies, remote signals or barrier semaphores. Data moves between devices by JAX's collectives and lax.ppermute only.
A program may use at most 64 MiB of HBM per device.

v0:
```python
import jax
import jax.numpy as jnp
from jax import lax
from jax.sharding import PartitionSpec as P

ADAPTER_SCALE = 2.0
EPSILON = 1e-06


def local(
    gradient_table,
    residual_input_rows,
    act,
    down_weight,
    adapter_input_factor,
    adapter_output_factor,
    lengths,
    owning_row_index,
):
    devices = lax.axis_size("dp")
    device = lax.axis_index("dp")
    member = lax.axis_index("tensor")
    passes = lengths.shape[1]
    columns = gradient_table.shape[1]
    start_col = member * columns
    my_rows = lax.dynamic_slice_in_dim(owning_row_index, device * passes, passes)
    piece = lax.all_gather(gradient_table, "dp", axis=0, tiled=True)
    sources = jnp.arange(piece.shape[0], dtype=jnp.int32)
    picker = (my_rows[:, None] == sources[None, :]).astype(jnp.bfloat16)
    routed = jnp.dot(picker, piece, preferred_element_type=jnp.float32)
    positions = jnp.cumsum(lengths[0]) - 1
    pooled_embedding = act[positions]
    partial_result_value = jnp.dot(
        pooled_embedding, down_weight, preferred_element_type=jnp.float32
    )
    reduced_projection = jnp.dot(
        pooled_embedding, adapter_input_factor, preferred_element_type=jnp.float32
    )
    residual = residual_input_rows.astype(jnp.float32)
    own_part = lax.dynamic_slice_in_dim(partial_result_value, start_col, columns, 1) + residual
    partial_result_value = lax.dynamic_update_slice_in_dim(
        partial_result_value, own_part, start_col, 1
    )
    reduced_total, low_sum = lax.psum((partial_result_value, reduced_projection), "tensor")
    reduced_output_factor = low_sum.astype(jnp.bfloat16)
    hidden_output = reduced_total + ADAPTER_SCALE * jnp.dot(
        reduced_output_factor, adapter_output_factor, preferred_element_type=jnp.float32
    )
    grads = lax.all_gather(routed.astype(jnp.bfloat16), "tensor", axis=1, tiled=True).astype(
        jnp.float32
    )
    length = jnp.sqrt(jnp.sum(hidden_output * hidden_output, axis=1, keepdims=True) + EPSILON)
    unit = hidden_output / length
    along = jnp.sum(grads * unit, axis=1, keepdims=True)
    unit_direction = ((grads - along * unit) / length).astype(jnp.bfloat16)
    local_direction = lax.dynamic_slice_in_dim(unit_direction, start_col, columns, 1)
    broadcast_gradient = jnp.dot(
        unit_direction, adapter_output_factor.T, preferred_element_type=jnp.float32
    ).astype(jnp.bfloat16)
    activation_gradient = (
        jnp.dot(unit_direction, down_weight.T, preferred_element_type=jnp.float32)
        + ADAPTER_SCALE
        * jnp.dot(broadcast_gradient, adapter_input_factor.T, preferred_element_type=jnp.float32)
    ).astype(jnp.bfloat16)
    passage_count = passes * devices
    leading_gradient = (
        ADAPTER_SCALE
        * jnp.dot(pooled_embedding.T, broadcast_gradient, preferred_element_type=jnp.float32)
        / passage_count
    )
    second_grad = (
        ADAPTER_SCALE
        * jnp.dot(reduced_output_factor.T, local_direction, preferred_element_type=jnp.float32)
        / passage_count
    )
    leading_gradient, second_grad = lax.psum((leading_gradient, second_grad), "dp")
    return (activation_gradient, leading_gradient, second_grad)


def solution(mesh):
    placed = (
        P("dp", "tensor"),
        P("dp", "tensor"),
        P("dp", "tensor"),
        P("tensor", None),
        P("tensor", None),
        P(),
        P("dp", None),
        P(),
    )
    return jax.shard_map(
        local,
        mesh=mesh,
        in_specs=placed,
        out_specs=(P("dp", "tensor"), P("tensor", None), P(None, "tensor")),
        check_vma=False,
    )
```

profile of v0, /device:TPU:0, one launch (start us, length us, event | category | flops | bytes accessed | tf_op | source)
XLA Modules:
  0.0 156.9 jit_solution(2057049614634383343)
XLA Ops:
  8.1 0.8 copy.12
  9.0 0.1 fusion.7
  9.1 3.4 %gather_fusion = bf16[64,1792]{1,0:T(8,128)(2,1)S(1)} fusion(bf16[1024,1792]{1,0:T(8,128)(2,1)} %param.10, s32[1024]{0:T(1024)S(1)} %pad_clamp_fusion), kind=kCustom, calls=%fused_computation | custom fusion | bytes 459008 | tf_op jit(solution)/shard_map/gather | solution.py:32
  12.6 7.8 %fusion.11 = f32[64,4096]{1,0:T(8,128)S(1)} fusion(bf16[64,1792]{1,0:T(8,128)(2,1)S(1)} %gather_fusion, bf16[1792,4096]{1,0:T(8,128)(2,1)} %param.11), kind=kOutput, calls=%fused_computation.28 | convolution fusion | flops 939524096 | bytes 15958016 | tf_op jit(solution)/shard_map/dot_general | solution.py:33
  20.5 1.0 copy-done.1
  21.5 0.5 all-gather.2.cloned.1.call-update
  22.1 0.8 dynamic_slice.9
  22.9 0.1 fusion.12
  23.0 8.5 %psum.29 = bf16[64,16]{0,1:T(8,128)(2,1)S(1)} all-reduce(f32[64,16]{0,1:T(8,128)S(1)} %fusion.12), channel_id=1, replica_groups=mesh['dp'=8,'tensor'=4] {'tensor'}, use_global_device_ids=true, to_apply=%region_2.3 | all-reduce | flops 1024 | bytes 6144 | tf_op jit(solution)/shard_map/psum | solution.py:44
  31.5 28.8 %all-reduce.4.cloned.1.call-done = f32[64,4096]{1,0:T(8,128)} async-done(((f32[64,4096]{1,0:T(8,128)}), f32[64,4096]{1,0:T(8,128)}) %all-reduce.4.cloned.1.call-update) | async-done | bytes 1048592 | tf_op jit(solution)/shard_map/psum | solution.py:44
  60.4 1.6 %multiply_reduce_fusion = (f32[64]{0:T(128)S(1)}, f32[64,4096]{1,0:T(8,128)S(1)}) fusion(f32[64,4096]{1,0:T(8,128)} %all-reduce.4.cloned.1.call-done, bf16[64,16]{0,1:T(8,128)(2,1)S(1)} %psum.29, bf16[16,4096]{1,0:T(8,128)(2,1)S(1)} %copy-done), kind=kOutput, calls=%fused_computation.15 | convolution fusion | flops 9437120 | bytes 2230528 | tf_op jit(solution)/shard_map/dot_general | solution.py:46
  62.0 5.2 %all-gather.2.cloned.1.call-done = bf16[512,1024]{1,0:T(8,128)(2,1)} async-done(((bf16[64,1024]{1,0:T(8,128)(2,1)}), bf16[512,1024]{1,0:T(8,128)(2,1)}) %all-gather.2.cloned.1.call-update) | async-done | bytes 1048592 | tf_op jit(solution)/shard_map/all_gather | solution.py:27
  67.2 1.6 convolution_convert_fusion
  68.8 7.2 %all_gather.7 = bf16[64,4096]{1,0:T(8,128)(2,1)S(1)} all-gather(bf16[64,1024]{1,0:T(8,128)(2,1)S(1)} %convolution_convert_fusion), channel_id=1, replica_groups=mesh['dp'=8,'tensor'=4] {'tensor'}, dimensions={1}, use_global_device_ids=true | all-gather | bytes 655360 | tf_op jit(solution)/shard_map/all_gather | solution.py:49
  75.9 0.3 fusion.2
  76.3 0.3 fusion.4
  76.5 0.2 convolution_convert_fusion.1
  76.8 0.8 convolution_multiply_fusion.3
  77.6 0.8 convolution_multiply_fusion.2
  78.4 0.2 convolution_multiply_fusion.1
  78.6 10.5 %fusion.1 = bf16[64,1792]{1,0:T(8,128)(2,1)} fusion(f32[64,1792]{1,0:T(8,128)S(1)} %convolution_multiply_fusion.1, bf16[64,4096]{1,0:T(8,128)(2,1)S(1)} %fusion.4, bf16[1792,4096]{1,0:T(8,128)(2,1)} %param.11), kind=kOutput, calls=%fused_computation.5 | convolution fusion | flops 939753472 | bytes 15892480 | tf_op jit(solution)/shard_map/dot_general | solution.py:61
  89.1 57.4 %all-reduce.6.cloned.1.call-done = (f32[1792,16]{0,1:T(8,128)}, f32[16,1024]{1,0:T(8,128)}) async-done(((f32[1792,16]{0,1:T(8,128)}, f32[16,1024]{1,0:T(8,128)}), (f32[1792,16]{0,1:T(8,128)}, f32[16,1024]{1,0:T(8,128)})) %all-reduce.6.cloned.1.call-update) | async-done | bytes 180240 | tf_op jit(solution)/shard_map/psum | solution.py:76
  146.5 1.6 copy.17
  148.0 1.5 copy.18
  (16 shorter events, 0.3 us)
Async XLA Ops:
  8.0 52.4 %copy-start = (bf16[16,4096]{1,0:T(8,128)(2,1)S(1)}, bf16[16,4096]{1,0:T(8,128)(2,1)}, u32[]{:S(2)}) copy-start(bf16[16,4096]{1,0:T(8,128)(2,1)} %param.13) | copy-start | bytes 393220
  8.0 12.4 %copy-start.3 = (bf16[64,1024]{1,0:T(8,128)(2,1)S(1)}, bf16[64,1024]{1,0:T(8,128)(2,1)}, u32[]{:S(2)}) copy-start(bf16[64,1024]{1,0:T(8,128)(2,1)} %param.9) | copy-start | bytes 393220
  8.0 14.8 %copy-start.2 = (bf16[1792,16]{0,1:T(8,128)(2,1)S(1)}, bf16[1792,16]{0,1:T(8,128)(2,1)}, u32[]{:S(2)}) copy-start(bf16[1792,16]{0,1:T(8,128)(2,1)} %param.12) | copy-start | bytes 172036
  8.0 52.3 %all-reduce.4.cloned.1.call-start = ((), (), s32[]{:S(2)}) async-start(), calls=%async_computation.1 | async-start | bytes 2097152 | tf_op jit(solution)/shard_map/psum | solution.py:44
  20.5 1.0 copy-start.1
  21.5 45.8 %all-gather.2.cloned.1.call-start = ((), (), s32[]{:S(2)}) async-start(), calls=%async_computation | async-start | bytes 1179648 | tf_op jit(solution)/shard_map/all_gather | solution.py:27
  22.0 124.4 %all-reduce.6.cloned.1.call-start = ((), (), s32[]{:S(2)}) async-start(), calls=%async_computation.2 | async-start | bytes 360448 | tf_op jit(solution)/shard_map/psum | solution.py:76
Sparse Core Ops, SparseCore 0:
  21.6 38.7 all-reduce.3
Sparse Core Ops, SparseCore 1:
  24.1 43.1 all-gather.1
  78.7 67.7 all-reduce.5
where the time goes:
time: 157 us
  waiting for transfers between devices  91.9 us (59%)
  matrix products  23.7 us (15%)
  blocking collectives  15.7 us (10%)
  between operations  15.6 us (10%)
  local copies, waits for them, and re-layouts  9.02 us (6%)
    psum x1, waiting for transfers between devices, local(): lax.psum((leading_gradient, second_grad), 'dp')  57.4 us
    psum x1, waiting for transfers between devices, local(): lax.psum((partial_result_value, reduced_projection), 'tensor')  28.8 us
    dot_general x1, matrix products, local(): jnp.dot(unit_direction, down_weight.T, preferred_element_type=jnp.float32)  10.5 us
    psum x1, blocking collectives, local(): lax.psum((partial_result_value, reduced_projection), 'tensor')  8.53 us
    dot_general x1, matrix products, local(): jnp.dot(pooled_embedding, down_weight, preferred_element_type=jnp.float32)  7.83 us
    all_gather x1, blocking collectives, local(): lax.all_gather(routed.astype(jnp.bfloat16), 'tensor', axis=1, tiled=True)  7.16 us
    all_gather x1, waiting for transfers between devices, local(): piece = lax.all_gather(gradient_table, 'dp', axis=0, tiled=True)  5.17 us
    unnamed x10, local copies, waits for them, and re-layouts  4.02 us
  transfers between devices with their start and end apart: 3, of which 3 were waited for; matrix products, arithmetic and copies ran while one was open for 8% of the time, Pallas kernels for 0%

commit v1 on v0

v1 whole, which is shorter than its diff:
```python
import functools

import jax
import jax.numpy as jnp
from jax import lax
from jax.experimental import pallas as pl
from jax.experimental.pallas import tpu as pltpu
from jax.sharding import PartitionSpec as P

ADAPTER_SCALE = 2.0
EPSILON = 1e-06
F32, BF16 = jnp.float32, jnp.bfloat16
LANES = 128
ROWS = 256
VMEM = pl.BlockSpec(memory_space=pltpu.VMEM)
SMEM = pl.BlockSpec(memory_space=pltpu.SMEM)


def dot(a, b, dims=((1,), (0,))):
    return lax.dot_general(a, b, (dims, ((), ())), preferred_element_type=F32)


def call(body, outs, name, *args, near=(), far=(), after=(), scratch=(), flops=0, limit=24):
    size = sum(a.size * a.dtype.itemsize for a in args + near + far)
    specs = [SMEM if a.dtype == jnp.int32 and a.size == 1 else VMEM for a in args]
    specs += [pl.BlockSpec(memory_space=pltpu.HBM)] * (len(near) + len(far) + len(after))
    held = [pltpu.VMEM(a.shape, a.dtype) for a in near]
    held += [pltpu.SemaphoreType.DMA((len(near),))] if near else []

    def run(*refs):
        refs = list(refs)
        inputs = [refs.pop(0) for _ in args]
        distant = [refs.pop(0) for _ in near]
        inputs += [refs.pop(0) for _ in far]
        del refs[: len(after)]
        if near:
            sems = refs.pop()
            here = refs[len(refs) - len(near) :]
            del refs[len(refs) - len(near) :]
            copies = [pltpu.make_async_copy(a, b, sems.at[i]) for i, (a, b) in enumerate(zip(distant, here))]
            for copy in copies:
                copy.start()
            inputs = (inputs, here, copies)
            body(inputs, *refs)
        else:
            body(*inputs, *refs)

    return pl.pallas_call(
        run,
        out_shape=[jax.ShapeDtypeStruct(*s) for s in outs],
        in_specs=specs,
        out_specs=[VMEM] * len(outs),
        scratch_shapes=list(scratch) + held,
        compiler_params=pltpu.CompilerParams(vmem_limit_bytes=limit << 20),
        cost_estimate=pl.CostEstimate(flops=flops, bytes_accessed=size, transcendentals=0),
        name=name,
    )(*args, *[pltpu.with_memory_space_constraint(a, pltpu.HBM) for a in near + far + after])


def cuts(total, step):
    return [(at, min(step, total - at)) for at in range(0, total, step)]


def iota(shape, dim):
    return lax.broadcasted_iota(jnp.int32, shape, dim)


def turned(column):
    n = column.shape[0]
    return jnp.sum(jnp.where(iota((n, n), 0) == iota((n, n), 1), column, 0), axis=0, keepdims=True)


def route_body(passes, capacity, inputs, out_ref):
    (device_ref,), (index_ref, table_ref), copies = inputs
    rows, slots = table_ref.shape[0], out_ref.shape[0]
    copies[0].wait()
    index = index_ref[...]
    total = index.shape[1]
    mine = device_ref[0] * rows + iota((rows, total), 0)
    packed = iota((rows, total), 1) // passes
    dest = jnp.sum(jnp.where(index == mine, packed, 0), axis=1, keepdims=True)
    earlier = (dest == turned(dest)) & (iota((rows, rows), 1) < iota((rows, rows), 0))
    rank = jnp.sum(earlier.astype(jnp.int32), axis=1, keepdims=True)
    slot = turned(dest * capacity + rank)
    picker = (iota((slots, rows), 0) == slot).astype(F32).astype(BF16)
    copies[1].wait()
    out_ref[...] = dot(picker, table_ref[...]).astype(BF16)


def slot_picker(index_ref, owners, owned, capacity):
    row = index_ref[...]
    n = row.shape[1]
    column = jnp.sum(jnp.where(iota((n, n), 0) == iota((n, n), 1), row, 0), axis=1, keepdims=True)
    owner = column // owned
    earlier = (owner == row // owned) & (row < column)
    slot = owner * capacity + jnp.sum(earlier.astype(jnp.int32), axis=1, keepdims=True)
    return (slot == iota((n, owners * capacity), 1)).astype(F32).astype(BF16)


def start_all(source_ref, held_ref, sems, dim, step, offset=0, size=None):
    copies = []
    for i, (at, n) in enumerate(cuts(held_ref.shape[dim], step)):
        piece = slice(at, at + n)
        to = held_ref.at[piece] if dim == 0 else held_ref.at[:, piece]
        if dim == 1:
            source = source_ref.at[:, piece]
        else:
            source = source_ref.at[piece, pl.ds(pl.multiple_of(offset, LANES), size)]
        copies.append(pltpu.make_async_copy(source, to, sems.at[i]))
    return copies


def own_terms(half, member, residual_ref, out_ref):
    columns = residual_ref.shape[1]
    blocks = out_ref.shape[1] // columns
    for j in range(blocks):
        own = jnp.where(half * blocks + j == member, 1.0, 0.0)
        out_ref[:, j * columns : (j + 1) * columns] = own * residual_ref[...].astype(F32)
    out_ref[:, blocks * columns :] = jnp.zeros_like(out_ref[:, blocks * columns :])


def add_low(half, low, factor_ref, out_ref, width):
    columns = pl.ds(pl.multiple_of(half * width, LANES), width)
    out_ref[:, :width] += ADAPTER_SCALE * dot(low.astype(BF16), factor_ref[:, columns])
    out_ref[:, width : width + low.shape[1]] = low


def first_body(inputs, out_ref, pooled_ref, low_ref, act_held, weight_held, act_sems, sems):
    (member_ref, act_ref, weight_ref), (lengths_ref, residual_ref, input_factor_ref, factor_ref), copies = inputs
    member = member_ref[0]
    half = 1 - member % 2
    hidden, width = weight_held.shape
    acts = start_all(act_ref, act_held, act_sems, 1, ROWS)
    weights = start_all(weight_ref, weight_held, sems, 0, ROWS, half * width, width)
    for pair in zip(acts, weights):
        for copy in pair:
            copy.start()
    for copy in copies:
        copy.wait()
    lengths = lengths_ref[...]
    n = lengths.shape[1]
    upto = jnp.where(iota((n, n), 1) <= iota((n, n), 0), lengths, 0)
    last = jnp.sum(upto, axis=1, keepdims=True) - 1
    picker = (last == iota((n, act_ref.shape[0]), 1)).astype(F32).astype(BF16)
    own_terms(half, member, residual_ref, out_ref)
    low = jnp.zeros(low_ref.shape, F32)
    for (at, size), act_copy, weight_copy in zip(cuts(hidden, ROWS), acts, weights):
        piece = slice(at, at + size)
        act_copy.wait()
        pooled = dot(picker, act_held[:, piece]).astype(BF16)
        pooled_ref[:, piece] = pooled
        low += dot(pooled, input_factor_ref[:, piece], ((1,), (1,)))
        weight_copy.wait()
        out_ref[:, :width] += dot(pooled, weight_held[piece, :])
    low_ref[...] = low
    add_low(half, low, factor_ref, out_ref, width)


def second_body(inputs, out_ref, weight_held, sems):
    (member_ref, pooled_ref, low_ref, weight_ref), (residual_ref, factor_ref), copies = inputs
    member = member_ref[0]
    half = member % 2
    hidden, width = weight_held.shape
    weights = start_all(weight_ref, weight_held, sems, 0, ROWS, half * width, width)
    for copy in weights:
        copy.start()
    for copy in copies:
        copy.wait()
    own_terms(half, member, residual_ref, out_ref)
    add_low(half, low_ref[...], factor_ref, out_ref, width)
    for (at, size), copy in zip(cuts(hidden, ROWS), weights):
        piece = slice(at, at + size)
        copy.wait()
        out_ref[:, :width] += dot(pooled_ref[:, piece], weight_held[piece, :])


def sum_body(width, rank, *refs):
    *ins, sum_ref, out_ref = refs
    total = ins[0][...] + ins[1][...]
    sum_ref[...] = total
    out_ref[:, :width] = total[:, :width].astype(BF16)
    low = total[:, width : width + rank]
    high = low.astype(BF16)
    out_ref[:, width:] = jnp.zeros_like(out_ref[:, width:])
    out_ref[:, width : width + rank] = high
    out_ref[:, width + rank : width + 2 * rank] = (low - high.astype(F32)).astype(BF16)


def add_body(width, rank, sum_ref, got_ref, total_ref, out_ref):
    total = sum_ref[:, :width] + got_ref[:, :width].astype(F32)
    total_ref[:, :width] = total
    out_ref[:, :width] = total.astype(BF16)
    low = (
        sum_ref[:, width : width + rank]
        + got_ref[:, width : width + rank].astype(F32)
        + got_ref[:, width + rank : width + 2 * rank].astype(F32)
    )
    total_ref[:, width:] = jnp.zeros_like(total_ref[:, width:])
    total_ref[:, width : width + rank] = low
    high = low.astype(BF16)
    out_ref[:, width:] = jnp.zeros_like(out_ref[:, width:])
    out_ref[:, width : width + rank] = high
    out_ref[:, width + rank : width + 2 * rank] = (low - high.astype(F32)).astype(BF16)


def direction_body(owners, owned, capacity, count, member_ref, index_ref, mine_ref, other_ref, grads_ref, factor_ref,
                   pooled_ref, direction_ref, spread_ref, packed_ref):
    member = member_ref[0]
    core = member % 2
    width = other_ref.shape[1]
    rank, model = factor_ref.shape
    mine = mine_ref[:, :width]
    other = other_ref[...].astype(F32)
    low = mine_ref[:, width : width + rank].astype(BF16)
    squares = jnp.sum(mine * mine, axis=1, keepdims=True) + jnp.sum(other * other, axis=1, keepdims=True)
    length = jnp.sqrt(squares + EPSILON)
    picker = slot_picker(index_ref, owners, owned, capacity)
    first = jnp.where(core == 0, mine, other)
    second = jnp.where(core == 0, other, mine)
    unit = [first / length, second / length]
    grads = [dot(picker, grads_ref[:, i * width : (i + 1) * width]) for i in range(2)]
    along = sum(jnp.sum(g * u, axis=1, keepdims=True) for g, u in zip(grads, unit))
    for i in range(2):
        direction_ref[:, i * width : (i + 1) * width] = ((grads[i] - along * unit[i]) / length).astype(BF16)
    spread = dot(direction_ref[...], factor_ref[...], ((1,), (1,))).astype(BF16)
    spread_ref[...] = spread
    hidden = pooled_ref.shape[1]
    columns = packed_ref.shape[1] - hidden
    scale = ADAPTER_SCALE / count
    packed_ref[:, :hidden] = (scale * dot(spread, pooled_ref[...], ((0,), (0,)))).astype(BF16)
    own = direction_ref[:, pl.ds(pl.multiple_of(member * columns, LANES), columns)]
    packed_ref[:, hidden:] = (scale * dot(low, own, ((0,), (0,)))).astype(BF16)


def round_sum_body(own_ref, got_ref, *refs):
    refs[-1][...] = (own_ref[...].astype(F32) + got_ref[...].astype(F32)).astype(BF16)


def last_sum_body(own_ref, got_ref, *refs):
    first_ref, second_ref = refs[-2:]
    total = own_ref[...].astype(F32) + got_ref[...].astype(F32)
    hidden = first_ref.shape[1]
    first_ref[...] = total[:, :hidden]
    second_ref[...] = total[:, hidden:]


def activation_body(start, stop, *refs):
    direction_ref, spread_ref, input_factor_ref = refs[:3]
    weight_ref, out_ref, token_ref, held, sems = refs[-5:]
    token_ref[...] = jnp.zeros_like(token_ref)
    whole = (stop - start) // ROWS

    def load(i, at, size):
        to = held.at[i] if size == ROWS else held.at[i, :size]
        return pltpu.make_async_copy(weight_ref.at[pl.ds(at, size)], to, sems.at[i])

    def part(i, at, size):
        columns = pl.ds(at, size)
        value = ADAPTER_SCALE * dot(spread_ref[...], input_factor_ref[:, columns])
        load(i, at, size).wait()
        rows = held[i] if size == ROWS else held[i, :size]
        out_ref[:, columns] = (value + dot(direction_ref[...], rows, ((1,), (1,)))).astype(BF16)

    for i, (at, size) in enumerate(cuts(stop - start, ROWS)):
        load(i, start + at, size).start()
    if start:
        out_ref[:, :start] = refs[3][:, :start]

    @pl.loop(0, whole)
    def _(i):
        part(i, pl.multiple_of(start + i * ROWS, ROWS), ROWS)

    if whole * ROWS < stop - start:
        part(whole, start + whole * ROWS, stop - start - whole * ROWS)


def local(gradient_table, residual_input_rows, act, down_weight, adapter_input_factor, adapter_output_factor, lengths,
          owning_row_index):
    devices = lax.axis_size("dp")
    members = lax.axis_size("tensor")
    device = lax.axis_index("dp")
    member = lax.axis_index("tensor")
    passes = lengths.shape[1]
    owned, columns = gradient_table.shape
    rank, model = adapter_output_factor.shape
    hidden = act.shape[1]
    capacity = -(-passes // devices)
    slots = devices * capacity
    blocks = members // 2
    width = blocks * columns
    count = passes * devices
    dp_at = device.astype(jnp.int32).reshape(1)
    member_at = member.astype(jnp.int32).reshape(1)
    input_factor = adapter_input_factor.T

    def swap(x, axis, size, bit):
        return lax.ppermute(x, axis, [(i, i ^ bit) for i in range(size)])

    steps = []
    bit = 2
    while bit < members:
        steps.append(bit)
        bit *= 2

    index = owning_row_index.reshape(1, -1)
    (sent,) = call(functools.partial(route_body, passes, capacity), [((slots, columns), BF16)], "route",
                   dp_at, near=(index, gradient_table))
    routed = lax.all_to_all(sent, "dp", 0, 0, tiled=True)
    grads = routed
    parts = {0: routed}
    for bit in steps:
        parts.update({k ^ bit: swap(v, "tensor", members, bit) for k, v in list(parts.items())})
    parts.update({k ^ 1: swap(v, "tensor", members, 1) for k, v in list(parts.items())})

    half_shape = (passes, width + LANES)
    pieces = len(cuts(hidden, ROWS))
    holds = [pltpu.VMEM((hidden, width), BF16)]
    sems = [pltpu.SemaphoreType.DMA((pieces,))]
    out, pooled, low = call(
        first_body, [(half_shape, F32), ((passes, hidden), BF16), ((passes, rank), F32)], "project_away",
        member_at, near=(lengths, residual_input_rows, input_factor, adapter_output_factor), far=(act, down_weight),
        scratch=[pltpu.VMEM(act.shape, BF16), *holds, *sems, *sems],
        flops=passes * hidden * model, after=(sent,),
    )
    away = swap(out, "tensor", members, 1)
    (kept,) = call(
        second_body, [(half_shape, F32)], "project_own",
        member_at, pooled, low, near=(residual_input_rows, adapter_output_factor), far=(down_weight,),
        scratch=[*holds, *sems], flops=passes * hidden * model,
    )
    total, out = call(functools.partial(sum_body, width, rank), [(half_shape, F32), (half_shape, BF16)], "sum_cores",
                      kept, away)
    for bit in steps:
        got = swap(out, "tensor", members, bit)
        total, out = call(functools.partial(add_body, width, rank), [(half_shape, F32), (half_shape, BF16)],
                          "sum_chips", total, got)
    other = swap(out[:, :width], "tensor", members, 1)

    ordered = jnp.stack([parts[k] for k in range(members)])
    grads = jnp.concatenate(
        [lax.dynamic_index_in_dim(ordered, member ^ b, 0, keepdims=False) for b in range(members)], axis=1
    )
    my_index = lax.dynamic_slice_in_dim(owning_row_index, device * passes, passes).reshape(1, -1)
    direction, spread, packed = call(
        functools.partial(direction_body, devices, owned, capacity, count),
        [((passes, model), BF16), ((passes, rank), BF16), ((rank, hidden + columns), BF16)], "direction",
        member_at, my_index, total, other, grads, adapter_output_factor, pooled,
        flops=passes * model * 64,
    )
    parts = 3
    ends = [min(hidden, -(-pieces * (i + 1) // parts) * ROWS) for i in range(parts)]
    token = []
    activation = []

    def activate():
        start = ends[len(ends) - len(todo) - 1] if len(todo) < parts else 0
        stop = todo.pop(0)
        out, done = call(
            functools.partial(activation_body, start, stop), [((passes, hidden), BF16), ((8, LANES), F32)], "activation",
            direction, spread, input_factor, *activation, far=(down_weight,),
            scratch=[
                pltpu.VMEM((-(-(stop - start) // ROWS), ROWS, model), BF16),
                pltpu.SemaphoreType.DMA((-(-(stop - start) // ROWS),)),
            ],
            flops=passes * (stop - start) * model * 2,
        )
        activation[:] = [out]
        token[:] = [done]

    todo = list(ends)
    shapes = [((rank, hidden), F32), ((rank, columns), F32)]
    if devices & (devices - 1) == 0:
        bit = 1
        while bit < devices:
            got = swap(packed, "dp", devices, bit)
            bit *= 2
            if todo:
                activate()
            if bit < devices:
                (packed,) = call(round_sum_body, [(packed.shape, BF16)], "sum_pairs", packed, got, *token)
            else:
                sums = call(last_sum_body, shapes, "sum_last", packed, got, *token)
    else:
        packed = lax.psum(packed.astype(F32), "dp")
        sums = packed[:, :hidden], packed[:, hidden:]
    while todo:
        activate()
    return activation[0], sums[0].T, sums[1]


def solution(mesh):
    placed = (
        P("dp", "tensor"),
        P("dp", "tensor"),
        P("dp", "tensor"),
        P("tensor", None),
        P("tensor", None),
        P(),
        P("dp", None),
        P(),
    )
    return jax.shard_map(
        local,
        mesh=mesh,
        in_specs=placed,
        out_specs=(P("dp", "tensor"), P("tensor", None), P(None, "tensor")),
        check_vma=False,
    )
```

time: 157 us -> 64.4 us (0.41)
  waiting for transfers between devices: 91.9 us -> 13.7 us
  Pallas kernels: 0 us -> 27.7 us
  matrix products: 23.7 us -> 0 us
  between operations: 15.6 us -> 0.78 us
  local copies, waits for them, and re-layouts: 9.02 us -> 1.48 us
  starting transfers between devices: 0.12 us -> 6.09 us
    psum x2 -> x0, waiting for transfers between devices: 86.2 us -> none  [the longest x1 57.4 us: local(): lax.psum((leading_gradient, second_grad), 'dp')]
    pallas_call x0 -> x12, Pallas kernels: none -> 27.7 us  [call(): pl.pallas_call(run, out_shape=[jax.ShapeDtypeStruct(*s) for s in outs], i...]
    dot_general x9 -> x0, matrix products: 23.7 us -> none  [the longest x1 10.5 us: local(): jnp.dot(unit_direction, down_weight.T, preferred_element_type=jnp.float32)]
    all_to_all x0 -> x1, blocking collectives: none -> 14.2 us  [local(): routed = lax.all_to_all(sent, 'dp', 0, 0, tiled=True)]
    ppermute x0 -> x9, waiting for transfers between devices: none -> 13.7 us  [swap(): return lax.ppermute(x, axis, [(i, i ^ bit) for i in range(size)])]
    psum x1 -> x0, blocking collectives: 8.53 us -> none  [local(): lax.psum((partial_result_value, reduced_projection), 'tensor')]
    all_gather x1 -> x0, blocking collectives: 7.16 us -> none  [local(): lax.all_gather(routed.astype(jnp.bfloat16), 'tensor', axis=1, tiled=True)]
    ppermute x0 -> x9, starting transfers between devices: none -> 6.09 us  [swap(): return lax.ppermute(x, axis, [(i, i ^ bit) for i in range(size)])]
  transfers between devices with their start and end apart: 3 -> 9, of which waited for: 3 -> 6; matrix products, arithmetic and copies ran while one was open for 8% -> 1% of each run, Pallas kernels for 0% -> 25%
where the time goes in v1:
time: 64.4 us; the launch traced here: 64.1 us
  Pallas kernels  27.7 us (43%)
  blocking collectives  14.2 us (22%)
  waiting for transfers between devices  13.7 us (21%)
  starting transfers between devices  6.09 us (9%)
  local copies, waits for them, and re-layouts  1.48 us (2%)
  between operations  0.78 us (1%)
    pallas_call x12, Pallas kernels, call(): pl.pallas_call(run, out_shape=[jax.ShapeDtypeStruct(*s) for s in outs], i...  27.7 us
    all_to_all x1, blocking collectives, local(): routed = lax.all_to_all(sent, 'dp', 0, 0, tiled=True)  14.2 us
    ppermute x9, waiting for transfers between devices, swap(): return lax.ppermute(x, axis, [(i, i ^ bit) for i in range(size)])  13.7 us
    ppermute x9, starting transfers between devices, swap(): return lax.ppermute(x, axis, [(i, i ^ bit) for i in range(size)])  6.09 us
  transfers between devices with their start and end apart: 9, of which 6 were waited for; matrix products, arithmetic and copies ran while one was open for 1% of the time, Pallas kernels for 25%

profile of v1, /device:TPU:0, one launch (start us, length us, event | category | flops | bytes accessed | tf_op | source)
XLA Modules:
  0.0 64.1 jit_solution(13775027006030842893)
XLA Ops:
  0.6 1.1 %route.1.refs_7_ = bf16[64,1024]{1,0:T(8,128)(2,1)S(1)} custom-call(s32[1]{0:T(128)} %bitcast.3.refs_0_, s32[1,512]{1,0:T(1,128)} %bitcast.32, bf16[64,1024]{1,0:T(8,128)(2,1)} %refs_2_.2), custom_call_target="tpu_custom_call" | custom-call | bytes 133124 | tf_op jit(solution)/shard_map/route/pallas_call | solution.py:48
  1.8 0.6 %copy-done.1 = bf16[64,1024]{1,0:T(8,128)(2,1)} copy-done((bf16[64,1024]{1,0:T(8,128)(2,1)}, bf16[64,1024]{1,0:T(8,128)(2,1)S(1)}, u32[]{:S(2)}) %copy-start.1) | copy-done | bytes 131096
  2.4 8.1 %project_away.1 = (f32[64,2176]{1,0:T(8,128)S(1)}, bf16[64,1792]{1,0:T(8,128)(2,1)S(1)}, f32[64,16]{1,0:T(8,128)S(1)}) custom-call(s32[1]{0:T(128)} %bitcast.refs_0_, s32[1,64]{1,0:T(1,128)} %refs_1_.1, bf16[64,1024]{1,0:T(8,128)(2,1)} %refs_3_.2, bf16[16,1792]{1,0:T(8,128)(2,1)} %bitcast.22, bf16[16,4096]{1,0:T(8,128)(2,1)} %refs_5_.5, ...), custom_call_target="tpu_custom_call" | custom-call | flops 469762048 | bytes 18669828 | tf_op jit(solution)/shard_map/project_away/pallas_call | solution.py:48
  10.6 0.5 collective-permute-start
  11.1 14.2 %all_to_all.12 = bf16[8,8,1024]{2,1,0:T(8,128)(2,1)S(1)} all-to-all(bf16[8,8,1024]{2,1,0:T(8,128)(2,1)S(1)} %bitcast.21), channel_id=1, replica_groups=mesh['dp'=8,'tensor'=4] {'dp'}, dimensions={0} | all-to-all | bytes 262144 | tf_op jit(solution)/shard_map/all_to_all | solution.py:308
  25.4 1.5 %collective-permute-start.4 = (bf16[64,1024]{1,0:T(8,128)(2,1)S(1)}, bf16[64,1024]{1,0:T(8,128)(2,1)S(1)}, u32[]{:S(2)}, u32[]{:S(2)}) collective-permute-start(bf16[64,1024]{1,0:T(8,128)(2,1)S(1)} %bitcast.26), channel_id=1, source_target_pairs={{0,2},{1,3},{2,0},{3,1},{4,6},{5,7},{6,4},{7,5},{8,10},{9,11},{10,... | collective-permute-start | bytes 393224 | tf_op jit(solution)/shard_map/ppermute | solution.py:297
  26.9 3.5 %collective-permute-done.4 = bf16[64,1024]{1,0:T(8,128)(2,1)S(1)} collective-permute-done((bf16[64,1024]{1,0:T(8,128)(2,1)S(1)}, bf16[64,1024]{1,0:T(8,128)(2,1)S(1)}, u32[]{:S(2)}, u32[]{:S(2)}) %collective-permute-start.4) | collective-permute-done | bytes 131104 | tf_op jit(solution)/shard_map/ppermute | solution.py:297
  30.3 4.6 %project_own.1.refs_0_ = f32[64,2176]{1,0:T(8,128)S(1)} custom-call(s32[1]{0:T(128)} %bitcast.refs_0_, bf16[64,1792]{1,0:T(8,128)(2,1)S(1)} %get-tuple-element.21.refs_1_.refs_6_, f32[64,16]{1,0:T(8,128)S(1)} %get-tuple-element.22.refs_2_, bf16[64,1024]{1,0:T(8,128)(2,1)} %refs_3_.2, bf16[16,4096]{1,0:T(8,128)(2,1)} %refs_5_.5, bf16[1792,4096]{1,0:T(8,128)(2,1)} %refs_4_.7), custom_call_target="tpu_custom_call" | custom-call | flops 469762048 | bytes 15175684 | tf_op jit(solution)/shard_map/project_own/pallas_call | solution.py:48
  35.0 1.6 %collective-permute-start.1 = (bf16[64,2176]{1,0:T(8,128)(2,1)S(1)}, bf16[64,2176]{1,0:T(8,128)(2,1)S(1)}, u32[]{:S(2)}, u32[]{:S(2)}) collective-permute-start(bf16[64,2176]{1,0:T(8,128)(2,1)S(1)} %get-tuple-element.25), channel_id=1, source_target_pairs={{0,2},{1,3},{2,0},{3,1},{4,6},{5,7},{6,4},{7,5},{8,10},{9,11},{10,... | collective-permute-start | bytes 835592 | tf_op jit(solution)/shard_map/ppermute | solution.py:297
  36.6 0.8 %dynamic-slice_bitcast_fusion.4.refs_1_ = s32[1,64]{1,0:T(1,128)S(1)} fusion(s32[512]{0:T(512)} %param.15, s32[]{:T(128)S(6)} %select_n.16), kind=kLoop, calls=%fused_computation.6 | loop fusion | bytes 516 | tf_op jit(solution)/shard_map/reshape | solution.py:343
  37.5 6.7 %collective-permute-done.1.refs_1_ = bf16[64,2176]{1,0:T(8,128)(2,1)S(1)} collective-permute-done((bf16[64,2176]{1,0:T(8,128)(2,1)S(1)}, bf16[64,2176]{1,0:T(8,128)(2,1)S(1)}, u32[]{:S(2)}, u32[]{:S(2)}) %collective-permute-start.1) | collective-permute-done | bytes 278560 | tf_op jit(solution)/shard_map/ppermute | solution.py:297
  44.2 0.2 sum_chips.1
  44.5 1.5 %collective-permute-done.2.refs_3_ = bf16[64,2048]{1,0:T(8,128)(2,1)S(1)} collective-permute-done((bf16[64,2048]{1,0:T(8,128)(2,1)S(1)}, bf16[64,2048]{1,0:T(8,128)(2,1)S(1)}, u32[]{:S(2)}, u32[]{:S(2)}) %collective-permute-start.2) | collective-permute-done | bytes 262176 | tf_op jit(solution)/shard_map/ppermute | solution.py:297
  46.0 1.4 %direction.1 = (bf16[64,4096]{1,0:T(8,128)(2,1)S(1)}, bf16[64,16]{1,0:T(8,128)(2,1)S(1)}, bf16[16,2816]{1,0:T(8,128)(2,1)S(1)}) custom-call(s32[1]{0:T(128)} %bitcast.refs_0_, s32[1,64]{1,0:T(1,128)S(1)} %dynamic-slice_bitcast_fusion.4.refs_1_, f32[64,2176]{1,0:T(8,128)S(1)} %get-tuple-element.26.refs_2_, ...), custom_call_target="tpu_custom_call" | custom-call | flops 16777216 | bytes 1704196 | tf_op jit(solution)/shard_map/direction/pallas_call | solution.py:48
  47.5 0.3 collective-permute-start.6
  47.8 4.2 %activation.3 = (bf16[64,1792]{1,0:T(8,128)(2,1)S(1)}, f32[8,128]{1,0:T(8,128)S(1)}) custom-call(bf16[64,4096]{1,0:T(8,128)(2,1)S(1)} %get-tuple-element.28.refs_0_, bf16[64,16]{1,0:T(8,128)(2,1)S(1)} %get-tuple-element.29.refs_1_, bf16[16,1792]{1,0:T(8,128)(2,1)S(1)} %bitcast.23, bf16[1792,4096]{1,0:T(8,128)(2,1)} %refs_4_.7), custom_call_target="tpu_custom_call" | custom-call | flops 402653184 | bytes 15263744 | tf_op jit(solution)/shard_map/activation/pallas_call | solution.py:48
  52.0 0.2 collective-permute-done.6.refs_1_
  52.2 0.9 %collective-permute-start.7 = (bf16[16,2816]{1,0:T(8,128)(2,1)S(1)}, bf16[16,2816]{1,0:T(8,128)(2,1)S(1)}, u32[]{:S(2)}, u32[]{:S(2)}) collective-permute-start(bf16[16,2816]{1,0:T(8,128)(2,1)S(1)} %sum_pairs.2.refs_0_), channel_id=1, source_target_pairs={{0,8},{4,12},{8,0},{12,4},{16,24},{20,28},{24,16},{28,20},{1,9},{5... | collective-permute-start | bytes 270344 | tf_op jit(solution)/shard_map/ppermute | solution.py:297
  53.1 3.3 %activation.4 = (bf16[64,1792]{1,0:T(8,128)(2,1)S(1)}, f32[8,128]{1,0:T(8,128)S(1)}) custom-call(bf16[64,4096]{1,0:T(8,128)(2,1)S(1)} %get-tuple-element.28.refs_0_, bf16[64,16]{1,0:T(8,128)(2,1)S(1)} %get-tuple-element.29.refs_1_, bf16[16,1792]{1,0:T(8,128)(2,1)S(1)} %bitcast.24, bf16[64,1792]{1,0:T(8,128)(2,1)S(1)} %get-tuple-element.30.refs_3_, ...), custom_call_target="tpu_custom_call" | custom-call | flops 268435456 | bytes 15493120 | tf_op jit(solution)/shard_map/activation/pallas_call | solution.py:48
  56.4 0.4 collective-permute-done.7.refs_1_
  56.8 1.2 %collective-permute-start.8 = (bf16[16,2816]{1,0:T(8,128)(2,1)S(1)}, bf16[16,2816]{1,0:T(8,128)(2,1)S(1)}, u32[]{:S(2)}, u32[]{:S(2)}) collective-permute-start(bf16[16,2816]{1,0:T(8,128)(2,1)S(1)} %sum_pairs.3.refs_0_), channel_id=1, source_target_pairs={{0,16},{4,20},{8,24},{12,28},{16,0},{20,4},{24,8},{28,12},{1,17},{... | collective-permute-start | bytes 270344 | tf_op jit(solution)/shard_map/ppermute | solution.py:297
  58.0 4.0 %activation.5 = (bf16[64,1792]{1,0:T(8,128)(2,1)}, f32[8,128]{1,0:T(8,128)S(1)}) custom-call(bf16[64,4096]{1,0:T(8,128)(2,1)S(1)} %get-tuple-element.28.refs_0_, bf16[64,16]{1,0:T(8,128)(2,1)S(1)} %get-tuple-element.29.refs_1_, bf16[16,1792]{1,0:T(8,128)(2,1)S(1)} %bitcast.25, bf16[64,1792]{1,0:T(8,128)(2,1)S(1)} %get-tuple-element.31.refs_3_, ...), custom_call_target="tpu_custom_call" | custom-call | flops 268435456 | bytes 15493120 | tf_op jit(solution)/shard_map/activation/pallas_call | solution.py:48
  62.0 1.5 %collective-permute-done.8.refs_1_ = bf16[16,2816]{1,0:T(8,128)(2,1)S(1)} collective-permute-done((bf16[16,2816]{1,0:T(8,128)(2,1)S(1)}, bf16[16,2816]{1,0:T(8,128)(2,1)S(1)}, u32[]{:S(2)}, u32[]{:S(2)}) %collective-permute-start.8) | collective-permute-done | bytes 90144 | tf_op jit(solution)/shard_map/ppermute | solution.py:297
  63.5 0.7 %sum_last.1 = (f32[16,1792]{1,0:T(8,128)}, f32[16,1024]{1,0:T(8,128)}) custom-call(bf16[16,2816]{1,0:T(8,128)(2,1)S(1)} %sum_pairs.3.refs_0_, bf16[16,2816]{1,0:T(8,128)(2,1)S(1)} %collective-permute-done.8.refs_1_, f32[8,128]{1,0:T(8,128)S(1)} %get-tuple-element.36.refs_2_), custom_call_target="tpu_custom_call" | custom-call | bytes 184320 | tf_op jit(solution)/shard_map/sum_last/pallas_call | solution.py:48
  (20 shorter events, 0.4 us)
Async XLA Ops:
  1.7 0.7 %copy-start.1 = (bf16[64,1024]{1,0:T(8,128)(2,1)}, bf16[64,1024]{1,0:T(8,128)(2,1)S(1)}, u32[]{:S(2)}) copy-start(bf16[64,1024]{1,0:T(8,128)(2,1)S(1)} %route.1.refs_7_) | copy-start | bytes 393220
  2.4 8.7 %copy-start.2 = (bf16[64,1024]{1,0:T(8,128)(2,1)S(1)}, bf16[64,1024]{1,0:T(8,128)(2,1)}, u32[]{:S(2)}) copy-start(bf16[64,1024]{1,0:T(8,128)(2,1)} %copy-done.1) | copy-start | bytes 393220
  10.6 35.5 %copy-start = (bf16[16,4096]{1,0:T(8,128)(2,1)S(1)}, bf16[16,4096]{1,0:T(8,128)(2,1)}, u32[]{:S(2)}) copy-start(bf16[16,4096]{1,0:T(8,128)(2,1)} %refs_5_.5) | copy-start | bytes 393220
  10.6 37.2 %copy-start.3 = (bf16[1792,16]{0,1:T(8,128)(2,1)S(1)}, bf16[1792,16]{0,1:T(8,128)(2,1)}, u32[]{:S(2)}) copy-start(bf16[1792,16]{0,1:T(8,128)(2,1)} %param.12) | copy-start | bytes 172036
  10.6 24.4 %collective-permute-start = (f32[64,2176]{1,0:T(8,128)S(1)}, f32[64,2176]{1,0:T(8,128)S(1)}, u32[]{:S(2)}, u32[]{:S(2)}) collective-permute-start(f32[64,2176]{1,0:T(8,128)S(1)} %get-tuple-element.23), channel_id=1, source_target_pairs={{0,1},{1,0},{2,3},{3,2},{4,5},{5,4},{6,7},{7,6},{8,9},{9,8},{10,11... | collective-permute-start | bytes 1671176 | tf_op jit(solution)/shard_map/ppermute | solution.py:297
  25.4 5.0 %collective-permute-start.4 = (bf16[64,1024]{1,0:T(8,128)(2,1)S(1)}, bf16[64,1024]{1,0:T(8,128)(2,1)S(1)}, u32[]{:S(2)}, u32[]{:S(2)}) collective-permute-start(bf16[64,1024]{1,0:T(8,128)(2,1)S(1)} %bitcast.26), channel_id=1, source_target_pairs={{0,2},{1,3},{2,0},{3,1},{4,6},{5,7},{6,4},{7,5},{8,10},{9,11},{10,... | collective-permute-start | bytes 393224 | tf_op jit(solution)/shard_map/ppermute | solution.py:297
  26.9 10.5 %collective-permute-start.3 = (bf16[64,1024]{1,0:T(8,128)(2,1)S(1)}, bf16[64,1024]{1,0:T(8,128)(2,1)S(1)}, u32[]{:S(2)}, u32[]{:S(2)}) collective-permute-start(bf16[64,1024]{1,0:T(8,128)(2,1)S(1)} %bitcast.27), channel_id=1, source_target_pairs={{0,1},{1,0},{2,3},{3,2},{4,5},{5,4},{6,7},{7,6},{8,9},{9,8},{10,11... | collective-permute-start | bytes 393224 | tf_op jit(solution)/shard_map/ppermute | solution.py:297
  30.3 7.1 %collective-permute-start.5 = (bf16[64,1024]{1,0:T(8,128)(2,1)S(1)}, bf16[64,1024]{1,0:T(8,128)(2,1)S(1)}, u32[]{:S(2)}, u32[]{:S(2)}) collective-permute-start(bf16[64,1024]{1,0:T(8,128)(2,1)S(1)} %collective-permute-done.4), channel_id=1, source_target_pairs={{0,1},{1,0},{2,3},{3,2},{4,5},{5,4},{6,7},{7,6},{8,9},{9,8},{10,11... | collective-permute-start | bytes 393224 | tf_op jit(solution)/shard_map/ppermute | solution.py:297
  35.0 9.1 %collective-permute-start.1 = (bf16[64,2176]{1,0:T(8,128)(2,1)S(1)}, bf16[64,2176]{1,0:T(8,128)(2,1)S(1)}, u32[]{:S(2)}, u32[]{:S(2)}) collective-permute-start(bf16[64,2176]{1,0:T(8,128)(2,1)S(1)} %get-tuple-element.25), channel_id=1, source_target_pairs={{0,2},{1,3},{2,0},{3,1},{4,6},{5,7},{6,4},{7,5},{8,10},{9,11},{10,... | collective-permute-start | bytes 835592 | tf_op jit(solution)/shard_map/ppermute | solution.py:297
  44.4 1.6 %collective-permute-start.2 = (bf16[64,2048]{1,0:T(8,128)(2,1)S(1)}, bf16[64,2048]{1,0:T(8,128)(2,1)S(1)}, u32[]{:S(2)}, u32[]{:S(2)}) collective-permute-start(bf16[64,2048]{1,0:T(8,128)(2,1)S(1)} %slice.3), channel_id=1, source_target_pairs={{0,1},{1,0},{2,3},{3,2},{4,5},{5,4},{6,7},{7,6},{8,9},{9,8},{10,11... | collective-permute-start | bytes 786440 | tf_op jit(solution)/shard_map/ppermute | solution.py:297
  47.5 4.7 %collective-permute-start.6 = (bf16[16,2816]{1,0:T(8,128)(2,1)S(1)}, bf16[16,2816]{1,0:T(8,128)(2,1)S(1)}, u32[]{:S(2)}, u32[]{:S(2)}) collective-permute-start(bf16[16,2816]{1,0:T(8,128)(2,1)S(1)} %get-tuple-element.33.refs_0_), channel_id=1, source_target_pairs={{0,4},{4,0},{8,12},{12,8},{16,20},{20,16},{24,28},{28,24},{1,5},{5... | collective-permute-start | bytes 270344 | tf_op jit(solution)/shard_map/ppermute | solution.py:297
  52.2 4.6 %collective-permute-start.7 = (bf16[16,2816]{1,0:T(8,128)(2,1)S(1)}, bf16[16,2816]{1,0:T(8,128)(2,1)S(1)}, u32[]{:S(2)}, u32[]{:S(2)}) collective-permute-start(bf16[16,2816]{1,0:T(8,128)(2,1)S(1)} %sum_pairs.2.refs_0_), channel_id=1, source_target_pairs={{0,8},{4,12},{8,0},{12,4},{16,24},{20,28},{24,16},{28,20},{1,9},{5... | collective-permute-start | bytes 270344 | tf_op jit(solution)/shard_map/ppermute | solution.py:297
  56.8 6.6 %collective-permute-start.8 = (bf16[16,2816]{1,0:T(8,128)(2,1)S(1)}, bf16[16,2816]{1,0:T(8,128)(2,1)S(1)}, u32[]{:S(2)}, u32[]{:S(2)}) collective-permute-start(bf16[16,2816]{1,0:T(8,128)(2,1)S(1)} %sum_pairs.3.refs_0_), channel_id=1, source_target_pairs={{0,16},{4,20},{8,24},{12,28},{16,0},{20,4},{24,8},{28,12},{1,17},{... | collective-permute-start | bytes 270344 | tf_op jit(solution)/shard_map/ppermute | solution.py:297

commit v2 on v1

v2 whole, which is shorter than its diff:
```python
import functools

import jax
import jax.numpy as jnp
from jax import lax
from jax.experimental import pallas as pl
from jax.experimental.pallas import tpu as pltpu
from jax.sharding import PartitionSpec as P

ADAPTER_SCALE = 2.0
EPSILON = 1e-06
F32, BF16 = jnp.float32, jnp.bfloat16
LANES = 128
ROWS = 256
VMEM = pl.BlockSpec(memory_space=pltpu.VMEM)
SMEM = pl.BlockSpec(memory_space=pltpu.SMEM)


def dot(a, b, dims=((1,), (0,))):
    return lax.dot_general(a, b, (dims, ((), ())), preferred_element_type=F32)


def call(body, outs, name, *args, near=(), far=(), after=(), scratch=(), flops=0, limit=24):
    size = sum(a.size * a.dtype.itemsize for a in args + near + far)
    specs = [SMEM if a.dtype == jnp.int32 and a.size == 1 else VMEM for a in args]
    specs += [pl.BlockSpec(memory_space=pltpu.HBM)] * (len(near) + len(far) + len(after))
    held = [pltpu.VMEM(a.shape, a.dtype) for a in near]
    held += [pltpu.SemaphoreType.DMA((len(near),))] if near else []

    def run(*refs):
        refs = list(refs)
        inputs = [refs.pop(0) for _ in args]
        distant = [refs.pop(0) for _ in near]
        inputs += [refs.pop(0) for _ in far]
        del refs[: len(after)]
        if near:
            sems = refs.pop()
            here = refs[len(refs) - len(near) :]
            del refs[len(refs) - len(near) :]
            copies = [pltpu.make_async_copy(a, b, sems.at[i]) for i, (a, b) in enumerate(zip(distant, here))]
            for copy in copies:
                copy.start()
            inputs = (inputs, here, copies)
            body(inputs, *refs)
        else:
            body(*inputs, *refs)

    return pl.pallas_call(
        run,
        out_shape=[jax.ShapeDtypeStruct(*s) if isinstance(s, tuple) else s for s in outs],
        in_specs=specs,
        out_specs=[VMEM if isinstance(s, tuple) else pl.BlockSpec(memory_space=pltpu.HBM) for s in outs],
        scratch_shapes=list(scratch) + held,
        compiler_params=pltpu.CompilerParams(vmem_limit_bytes=limit << 20),
        cost_estimate=pl.CostEstimate(flops=flops, bytes_accessed=size, transcendentals=0),
        name=name,
    )(*args, *[pltpu.with_memory_space_constraint(a, pltpu.HBM) for a in near + far + after])


def cuts(total, step):
    return [(at, min(step, total - at)) for at in range(0, total, step)]


def iota(shape, dim):
    return lax.broadcasted_iota(jnp.int32, shape, dim)


def turned(column):
    n = column.shape[0]
    return jnp.sum(jnp.where(iota((n, n), 0) == iota((n, n), 1), column, 0), axis=0, keepdims=True)


def route_body(passes, capacity, inputs, out_ref):
    (device_ref,), (index_ref, table_ref), copies = inputs
    rows, slots = table_ref.shape[0], out_ref.shape[0]
    copies[0].wait()
    index = index_ref[...]
    total = index.shape[1]
    mine = device_ref[0] * rows + iota((rows, total), 0)
    packed = iota((rows, total), 1) // passes
    dest = jnp.sum(jnp.where(index == mine, packed, 0), axis=1, keepdims=True)
    earlier = (dest == turned(dest)) & (iota((rows, rows), 1) < iota((rows, rows), 0))
    rank = jnp.sum(earlier.astype(jnp.int32), axis=1, keepdims=True)
    slot = turned(dest * capacity + rank)
    picker = (iota((slots, rows), 0) == slot).astype(F32).astype(BF16)
    copies[1].wait()
    out_ref[...] = dot(picker, table_ref[...]).astype(BF16)


def slot_picker(index_ref, owners, owned, capacity):
    row = index_ref[...]
    n = row.shape[1]
    column = jnp.sum(jnp.where(iota((n, n), 0) == iota((n, n), 1), row, 0), axis=1, keepdims=True)
    owner = column // owned
    earlier = (owner == row // owned) & (row < column)
    slot = owner * capacity + jnp.sum(earlier.astype(jnp.int32), axis=1, keepdims=True)
    return (slot == iota((n, owners * capacity), 1)).astype(F32).astype(BF16)


def project_body(inputs, out_ref, pooled_ref, low_ref, act_held, weight_held, act_sems, sems):
    (member_ref, lengths_ref, act_ref, weight_ref), (residual_ref, input_factor_ref), copies = inputs
    hidden = weight_held.shape[0]
    pieces = []
    for i, (at, size) in enumerate(cuts(hidden, ROWS)):
        piece = slice(at, at + size)
        act_copy = pltpu.make_async_copy(act_ref.at[:, piece], act_held.at[:, piece], act_sems.at[i])
        act_copy.start()
        copy = pltpu.make_async_copy(weight_ref.at[piece], weight_held.at[piece], sems.at[i])
        copy.start()
        pieces.append((piece, act_copy, copy))
    lengths = lengths_ref[...]
    n = lengths.shape[1]
    upto = jnp.where(iota((n, n), 1) <= iota((n, n), 0), lengths, 0)
    last = jnp.sum(upto, axis=1, keepdims=True) - 1
    picker = (last == iota((n, act_ref.shape[0]), 1)).astype(F32).astype(BF16)
    for piece, act_copy, copy in pieces:
        act_copy.wait()
        pooled = dot(picker, act_held[:, piece]).astype(BF16)
        pooled_ref[:, piece] = pooled
        copy.wait()
        value = dot(pooled, weight_held[piece, :])
        if piece.start == 0:
            out_ref[...] = value
        else:
            out_ref[...] += value
    for copy in copies:
        copy.wait()
    low_ref[...] = dot(pooled_ref[...], input_factor_ref[...], ((1,), (1,)))
    columns = residual_ref.shape[1]
    own = pl.ds(pl.multiple_of(member_ref[0] * columns, LANES), columns)
    out_ref[:, own] += residual_ref[...].astype(F32)


def half_of(half, width, parts_ref, low_ref, factor_ref):
    columns = pl.ds(pl.multiple_of(half * width, LANES), width)
    return parts_ref[:, columns] + ADAPTER_SCALE * dot(low_ref[...].astype(BF16), factor_ref[:, columns])


def finish_body(owners, owned, capacity, member_ref, index_ref, routed_ref, parts_ref, low_ref, factor_ref, away_ref,
                grads_ref):
    width, rank = parts_ref.shape[1] // 2, low_ref.shape[1]
    away_ref[:, :width] = half_of(1 - member_ref[0] % 2, width, parts_ref, low_ref, factor_ref)
    away_ref[:, width:] = jnp.zeros_like(away_ref[:, width:])
    away_ref[:, width : width + rank] = low_ref[...]
    grads_ref[...] = dot(slot_picker(index_ref, owners, owned, capacity), routed_ref[...]).astype(BF16)


def put_low(low, at, out_ref):
    rank = low.shape[1]
    high = low.astype(BF16)
    out_ref[:, at:] = jnp.zeros_like(out_ref[:, at:])
    out_ref[:, at : at + rank] = high
    out_ref[:, at + rank : at + 2 * rank] = (low - high.astype(F32)).astype(BF16)


def sum_cores_body(member_ref, parts_ref, low_ref, away_ref, factor_ref, total_ref, low_total_ref, out_ref):
    width, rank = parts_ref.shape[1] // 2, low_ref.shape[1]
    total = half_of(member_ref[0] % 2, width, parts_ref, low_ref, factor_ref) + away_ref[:, :width]
    low = low_ref[...] + away_ref[:, width : width + rank]
    total_ref[...] = total
    low_total_ref[...] = low
    out_ref[:, :width] = total.astype(BF16)
    put_low(low, width, out_ref)


def sum_chips_body(last, total_ref, low_ref, got_ref, grads_ref, got_grads_ref, new_total_ref, new_low_ref, out_ref,
                   *more):
    width, rank = total_ref.shape[1], low_ref.shape[1]
    total = total_ref[...] + got_ref[:, :width].astype(F32)
    low = low_ref[...]
    for i in range(2):
        low += got_ref[:, width + i * rank : width + (i + 1) * rank].astype(F32)
    new_total_ref[...] = total
    new_low_ref[...] = low
    out_ref[:, :width] = total.astype(BF16)
    columns = grads_ref.shape[1]
    if last:
        joined_ref, at = out_ref, width
    else:
        put_low(low, width, out_ref)
        (joined_ref,), at = more, 0
    joined_ref[:, at : at + columns] = grads_ref[...]
    joined_ref[:, at + columns : at + 2 * columns] = got_grads_ref[...]


def direction_body(count, blocks, member_ref, total_ref, low_ref, mine_ref, other_ref, factor_ref, pooled_ref,
                   direction_ref, spread_ref, packed_ref):
    member = member_ref[0]
    width = total_ref.shape[1]
    columns = width // blocks

    def hidden_block(b):
        piece = slice(b % blocks * columns, (b % blocks + 1) * columns)
        return jnp.where(member % 2 == b // blocks, total_ref[:, piece], other_ref[:, piece].astype(F32))

    def grads_block(b):
        apart = member ^ b
        piece = pl.ds(pl.multiple_of(width + apart // 2 * columns, LANES), columns)
        return jnp.where(apart % 2 == 0, mine_ref[:, piece].astype(F32), other_ref[:, piece].astype(F32))

    squares = sum(jnp.sum(hidden_block(b) ** 2, axis=1, keepdims=True) for b in range(2 * blocks))
    length = jnp.sqrt(squares + EPSILON)
    along = sum(
        jnp.sum(grads_block(b) * (hidden_block(b) / length), axis=1, keepdims=True) for b in range(2 * blocks)
    )
    for b in range(2 * blocks):
        value = (grads_block(b) - along * (hidden_block(b) / length)) / length
        direction_ref[:, b * columns : (b + 1) * columns] = value.astype(BF16)
    spread = dot(direction_ref[...], factor_ref[...], ((1,), (1,))).astype(BF16)
    spread_ref[...] = spread
    hidden = pooled_ref.shape[1]
    scale = ADAPTER_SCALE / count
    packed_ref[:, :hidden] = (scale * dot(spread, pooled_ref[...], ((0,), (0,)))).astype(BF16)
    own = direction_ref[:, pl.ds(pl.multiple_of(member * columns, LANES), columns)]
    packed_ref[:, hidden:] = (scale * dot(low_ref[...].astype(BF16), own, ((0,), (0,)))).astype(BF16)


def round_sum_body(own_ref, got_ref, *refs):
    refs[-1][...] = (own_ref[...].astype(F32) + got_ref[...].astype(F32)).astype(BF16)


def last_sum_body(own_ref, got_ref, *refs):
    first_ref, second_ref = refs[-2:]
    total = own_ref[...].astype(F32) + got_ref[...].astype(F32)
    hidden = first_ref.shape[1]
    first_ref[...] = total[:, :hidden]
    second_ref[...] = total[:, hidden:]


def activation_body(start, stop, *refs):
    direction_ref, spread_ref, input_factor_ref = refs[:3]
    weight_ref, out_ref, token_ref, held, sems = refs[-5:]
    token_ref[...] = jnp.zeros_like(token_ref)
    whole = (stop - start) // ROWS

    def load(i, at, size):
        to = held.at[i] if size == ROWS else held.at[i, :size]
        return pltpu.make_async_copy(weight_ref.at[pl.ds(at, size)], to, sems.at[i])

    def part(i, at, size):
        columns = pl.ds(at, size)
        value = ADAPTER_SCALE * dot(spread_ref[...], input_factor_ref[:, columns])
        load(i, at, size).wait()
        rows = held[i] if size == ROWS else held[i, :size]
        out_ref[:, columns] = (value + dot(direction_ref[...], rows, ((1,), (1,)))).astype(BF16)

    for i, (at, size) in enumerate(cuts(stop - start, ROWS)):
        load(i, start + at, size).start()
    if start:
        out_ref[:, :start] = refs[3][:, :start]

    @pl.loop(0, whole)
    def _(i):
        part(i, pl.multiple_of(start + i * ROWS, ROWS), ROWS)

    if whole * ROWS < stop - start:
        part(whole, start + whole * ROWS, stop - start - whole * ROWS)


def local(gradient_table, residual_input_rows, act, down_weight, adapter_input_factor, adapter_output_factor, lengths,
          owning_row_index):
    devices = lax.axis_size("dp")
    members = lax.axis_size("tensor")
    device = lax.axis_index("dp")
    member = lax.axis_index("tensor")
    passes = lengths.shape[1]
    owned, columns = gradient_table.shape
    rank, model = adapter_output_factor.shape
    hidden = act.shape[1]
    capacity = -(-passes // devices)
    slots = devices * capacity
    blocks = members // 2
    width = blocks * columns
    count = passes * devices
    dp_at = device.astype(jnp.int32).reshape(1)
    member_at = member.astype(jnp.int32).reshape(1)
    input_factor = adapter_input_factor.T

    def swap(x, axis, size, bit):
        return lax.ppermute(x, axis, [(i, i ^ bit) for i in range(size)])

    steps = []
    bit = 2
    while bit < members:
        steps.append(bit)
        bit *= 2

    index = owning_row_index.reshape(1, -1)
    my_index = lax.dynamic_slice_in_dim(owning_row_index, device * passes, passes).reshape(1, -1)
    (sent,) = call(
        functools.partial(route_body, passes, capacity), [((slots, columns), BF16)], "route",
        dp_at, near=(index, gradient_table),
    )
    routed = lax.all_to_all(sent, "dp", 0, 0, tiled=True)
    pieces = len(cuts(hidden, ROWS))
    terms, pooled, low = call(
        project_body, [((passes, model), F32), ((passes, hidden), BF16), ((passes, rank), F32)], "project",
        member_at, lengths, near=(residual_input_rows, input_factor), far=(act, down_weight),
        scratch=[pltpu.VMEM(act.shape, BF16), pltpu.VMEM(down_weight.shape, BF16)]
        + [pltpu.SemaphoreType.DMA((pieces,))] * 2,
        flops=2 * passes * hidden * model, limit=32,
    )
    away, grads = call(
        functools.partial(finish_body, devices, owned, capacity),
        [((passes, width + LANES), F32), ((passes, columns), BF16)], "finish",
        member_at, my_index, routed, terms, low, adapter_output_factor,
    )
    away = swap(away, "tensor", members, 1)
    sums = [((passes, width), F32), ((passes, rank), F32)]
    total, low, out = call(
        sum_cores_body, [*sums, ((passes, width + LANES), BF16)], "sum_cores",
        member_at, terms, low, away, adapter_output_factor,
    )
    for bit in steps:
        got, got_grads = swap(out, "tensor", members, bit), swap(grads, "tensor", members, bit)
        joined = 2 * grads.shape[1]
        last = bit == steps[-1]
        outs = [((passes, width + joined), BF16)] if last else [(out.shape, BF16), ((passes, joined), BF16)]
        total, low, out, *more = call(
            functools.partial(sum_chips_body, last), [*sums, *outs], "sum_chips",
            total, low, got, grads, got_grads,
        )
        grads = more[0] if more else None
    other = swap(out, "tensor", members, 1)
    direction, spread, packed = call(
        functools.partial(direction_body, count, blocks),
        [((passes, model), BF16), ((passes, rank), BF16), ((rank, hidden + columns), BF16)], "direction",
        member_at, total, low, out, other, adapter_output_factor, pooled,
        flops=passes * model * 64,
    )
    parts = 3
    ends = [min(hidden, -(-pieces * (i + 1) // parts) * ROWS) for i in range(parts)]
    token = []
    activation = []

    def activate():
        start = ends[len(ends) - len(todo) - 1] if len(todo) < parts else 0
        stop = todo.pop(0)
        out, done = call(
            functools.partial(activation_body, start, stop), [((passes, hidden), BF16), ((8, LANES), F32)], "activation",
            direction, spread, input_factor, *activation, far=(down_weight,),
            scratch=[
                pltpu.VMEM((-(-(stop - start) // ROWS), ROWS, model), BF16),
                pltpu.SemaphoreType.DMA((-(-(stop - start) // ROWS),)),
            ],
            flops=passes * (stop - start) * model * 2,
        )
        activation[:] = [out]
        token[:] = [done]

    todo = list(ends)
    shapes = [((rank, hidden), F32), ((rank, columns), F32)]
    if devices & (devices - 1) == 0:
        bit = 1
        while bit < devices:
            got = swap(packed, "dp", devices, bit)
            bit *= 2
            if todo:
                activate()
            if bit < devices:
                (packed,) = call(round_sum_body, [(packed.shape, BF16)], "sum_pairs", packed, got, *token)
            else:
                sums = call(last_sum_body, shapes, "sum_last", packed, got, *token)
    else:
        packed = lax.psum(packed.astype(F32), "dp")
        sums = packed[:, :hidden], packed[:, hidden:]
    while todo:
        activate()
    return activation[0], sums[0].T, sums[1]


def solution(mesh):
    placed = (
        P("dp", "tensor"),
        P("dp", "tensor"),
        P("dp", "tensor"),
        P("tensor", None),
        P("tensor", None),
        P(),
        P("dp", None),
        P(),
    )
    return jax.shard_map(
        local,
        mesh=mesh,
        in_specs=placed,
        out_specs=(P("dp", "tensor"), P("tensor", None), P(None, "tensor")),
        check_vma=False,
    )
```

time: 64.4 us -> 55.1 us (0.86)
  blocking collectives: 14.2 us -> 0 us
  starting transfers between devices: 6.09 us -> 15.6 us
  Pallas kernels: 27.7 us -> 23.1 us
    all_to_all x1 -> x0, blocking collectives: 14.2 us -> none  [local(): routed = lax.all_to_all(sent, 'dp', 0, 0, tiled=True)]
    all_to_all x0 -> x1, starting transfers between devices: none -> 7.26 us  [local(): routed = lax.all_to_all(sent, 'dp', 0, 0, tiled=True)]
    pallas_call x12, Pallas kernels: 27.7 us -> 23.1 us  [call(): pl.pallas_call(run, out_shape=[jax.ShapeDtypeStruct(*s) if isinstance(s,...]
    ppermute x9 -> x7, starting transfers between devices: 6.09 us -> 8.29 us  [swap(): return lax.ppermute(x, axis, [(i, i ^ bit) for i in range(size)])]
    ppermute x9 -> x7, waiting for transfers between devices: 13.7 us -> 13.9 us  [swap(): return lax.ppermute(x, axis, [(i, i ^ bit) for i in range(size)])]
  transfers between devices with their start and end apart: 9 -> 8, of which waited for: 6 -> 4; matrix products, arithmetic and copies ran while one was open for 1% -> 1% of each run, Pallas kernels for 25% -> 34%
where the time goes in v2:
time: 55.1 us; the launch traced here: 54.7 us
  Pallas kernels  23.1 us (42%)
  starting transfers between devices  15.6 us (28%)
  waiting for transfers between devices  13.9 us (25%)
  local copies, waits for them, and re-layouts  1.42 us (3%)
  between operations  0.78 us (1%)
    pallas_call x12, Pallas kernels, call(): pl.pallas_call(run, out_shape=[jax.ShapeDtypeStruct(*s) if isinstance(s,...  23.1 us
    ppermute x7, waiting for transfers between devices, swap(): return lax.ppermute(x, axis, [(i, i ^ bit) for i in range(size)])  13.9 us
    ppermute x7, starting transfers between devices, swap(): return lax.ppermute(x, axis, [(i, i ^ bit) for i in range(size)])  8.29 us
    all_to_all x1, starting transfers between devices, local(): routed = lax.all_to_all(sent, 'dp', 0, 0, tiled=True)  7.26 us
  transfers between devices with their start and end apart: 8, of which 4 were waited for; matrix products, arithmetic and copies ran while one was open for 1% of the time, Pallas kernels for 34%

profile of v2, /device:TPU:0, one launch (start us, length us, event | category | flops | bytes accessed | tf_op | source)
XLA Modules:
  0.0 54.7 jit_solution(17899899447835800959)
XLA Ops:
  0.7 1.8 %route.1 = bf16[64,1024]{1,0:T(8,128)(2,1)} custom-call(s32[1]{0:T(128)} %bitcast.3.refs_0_, s32[1,512]{1,0:T(1,128)} %bitcast.14, bf16[64,1024]{1,0:T(8,128)(2,1)} %refs_2_.3), custom_call_target="tpu_custom_call" | custom-call | bytes 133124 | tf_op jit(solution)/shard_map/route/pallas_call | solution.py:48
  2.5 7.3 %all-to-all-start = ((bf16[8,8,1024]{2,1,0:T(8,128)(2,1)}), bf16[8,8,1024]{2,1,0:T(8,128)(2,1)S(1)}, u32[]{:S(2)}, u32[]{:S(2)}) async-start(bf16[8,8,1024]{2,1,0:T(8,128)(2,1)} %bitcast.5), calls=%async_computation | async-start | bytes 262144 | tf_op jit(solution)/shard_map/all_to_all | solution.py:294
  9.7 0.7 %copy-done.2 = s32[1,64]{1,0:T(1,128)S(1)} copy-done((s32[1,64]{1,0:T(1,128)S(1)}, s32[1,64]{1,0:T(1,128)}, u32[]{:S(2)}) %copy-start.2) | copy-done | bytes 280
  10.4 7.4 %project.1 = (f32[64,4096]{1,0:T(8,128)S(1)}, bf16[64,1792]{1,0:T(8,128)(2,1)S(1)}, f32[64,16]{1,0:T(8,128)S(1)}) custom-call(s32[1]{0:T(128)} %bitcast.refs_0_, s32[1,64]{1,0:T(1,128)S(1)} %copy-done.2, bf16[64,1024]{1,0:T(8,128)(2,1)} %refs_2_.2, bf16[16,1792]{1,0:T(8,128)(2,1)} %bitcast.9, bf16[1024,1792]{1,0:T(8,128)(2,1)} %refs_4_.4, ...), custom_call_target="tpu_custom_call" | custom-call | flops 939524096 | bytes 18538756 | tf_op jit(solution)/shard_map/project/pallas_call | solution.py:48
  17.8 0.8 %dynamic-slice_bitcast_fusion.refs_1_ = s32[1,64]{1,0:T(1,128)S(1)} fusion(s32[512]{0:T(512)} %param.15, s32[]{:T(128)S(6)} %select_n.3), kind=kLoop, calls=%fused_computation | loop fusion | bytes 516 | tf_op jit(solution)/shard_map/reshape | solution.py:289
  18.5 0.4 finish.1
  18.9 0.1 collective-permute-start
  19.0 1.9 %collective-permute-done.refs_3_ = f32[64,2176]{1,0:T(8,128)S(1)} collective-permute-done((f32[64,2176]{1,0:T(8,128)S(1)}, f32[64,2176]{1,0:T(8,128)S(1)}, u32[]{:S(2)}, u32[]{:S(2)}) %collective-permute-start) | collective-permute-done | bytes 557088 | tf_op jit(solution)/shard_map/ppermute | solution.py:280
  20.9 0.2 sum_cores.1
  21.1 1.6 %collective-permute-start.1 = (bf16[64,2176]{1,0:T(8,128)(2,1)S(1)}, bf16[64,2176]{1,0:T(8,128)(2,1)S(1)}, u32[]{:S(2)}, u32[]{:S(2)}) collective-permute-start(bf16[64,2176]{1,0:T(8,128)(2,1)S(1)} %get-tuple-element.30), channel_id=1, source_target_pairs={{0,2},{1,3},{2,0},{3,1},{4,6},{5,7},{6,4},{7,5},{8,10},{9,11},{10,... | collective-permute-start | bytes 835592 | tf_op jit(solution)/shard_map/ppermute | solution.py:280
  22.7 0.5 collective-permute-start.2
  23.2 9.5 %collective-permute-done.2.refs_4_ = bf16[64,1024]{1,0:T(8,128)(2,1)S(1)} collective-permute-done((bf16[64,1024]{1,0:T(8,128)(2,1)S(1)}, bf16[64,1024]{1,0:T(8,128)(2,1)S(1)}, u32[]{:S(2)}, u32[]{:S(2)}) %collective-permute-start.2) | collective-permute-done | bytes 131104 | tf_op jit(solution)/shard_map/ppermute | solution.py:280
  32.7 0.1 sum_chips.1
  32.8 0.1 collective-permute-start.3
  32.9 1.9 %collective-permute-done.3.refs_4_ = bf16[64,4096]{1,0:T(8,128)(2,1)S(1)} collective-permute-done((bf16[64,4096]{1,0:T(8,128)(2,1)S(1)}, bf16[64,4096]{1,0:T(8,128)(2,1)S(1)}, u32[]{:S(2)}, u32[]{:S(2)}) %collective-permute-start.3) | collective-permute-done | bytes 524320 | tf_op jit(solution)/shard_map/ppermute | solution.py:280
  34.8 1.1 %direction.1 = (bf16[64,4096]{1,0:T(8,128)(2,1)S(1)}, bf16[64,16]{1,0:T(8,128)(2,1)S(1)}, bf16[16,2816]{1,0:T(8,128)(2,1)S(1)}) custom-call(s32[1]{0:T(128)} %bitcast.refs_0_, f32[64,2048]{1,0:T(8,128)S(1)} %get-tuple-element.32.refs_1_, f32[64,16]{1,0:T(8,128)S(1)} %get-tuple-element.33.refs_2_, bf16[64,4096]{1,0:T(8,128)(2,1)S(1)} %get-tuple-element.34.refs_3_, ...), custom_call_target="tpu_custom_call" | custom-call | flops 16777216 | bytes 1937412 | tf_op jit(solution)/shard_map/direction/pallas_call | solution.py:48
  35.9 2.1 %collective-permute-start.4 = (bf16[16,2816]{1,0:T(8,128)(2,1)S(1)}, bf16[16,2816]{1,0:T(8,128)(2,1)S(1)}, u32[]{:S(2)}, u32[]{:S(2)}) collective-permute-start(bf16[16,2816]{1,0:T(8,128)(2,1)S(1)} %get-tuple-element.41.refs_0_), channel_id=1, source_target_pairs={{0,4},{4,0},{8,12},{12,8},{16,20},{20,16},{24,28},{28,24},{1,5},{5... | collective-permute-start | bytes 270344 | tf_op jit(solution)/shard_map/ppermute | solution.py:280
  38.0 4.2 %activation.3 = (bf16[64,1792]{1,0:T(8,128)(2,1)S(1)}, f32[8,128]{1,0:T(8,128)S(1)}) custom-call(bf16[64,4096]{1,0:T(8,128)(2,1)S(1)} %get-tuple-element.36.refs_0_, bf16[64,16]{1,0:T(8,128)(2,1)S(1)} %get-tuple-element.37.refs_1_, bf16[16,1792]{1,0:T(8,128)(2,1)S(1)} %bitcast.10, bf16[1792,4096]{1,0:T(8,128)(2,1)} %refs_4_.7), custom_call_target="tpu_custom_call" | custom-call | flops 402653184 | bytes 15263744 | tf_op jit(solution)/shard_map/activation/pallas_call | solution.py:48
  42.2 1.5 %collective-permute-start.5 = (bf16[16,2816]{1,0:T(8,128)(2,1)S(1)}, bf16[16,2816]{1,0:T(8,128)(2,1)S(1)}, u32[]{:S(2)}, u32[]{:S(2)}) collective-permute-start(bf16[16,2816]{1,0:T(8,128)(2,1)S(1)} %sum_pairs.2.refs_0_), channel_id=1, source_target_pairs={{0,8},{4,12},{8,0},{12,4},{16,24},{20,28},{24,16},{28,20},{1,9},{5... | collective-permute-start | bytes 270344 | tf_op jit(solution)/shard_map/ppermute | solution.py:280
  43.8 3.3 %activation.4 = (bf16[64,1792]{1,0:T(8,128)(2,1)S(1)}, f32[8,128]{1,0:T(8,128)S(1)}) custom-call(bf16[64,4096]{1,0:T(8,128)(2,1)S(1)} %get-tuple-element.36.refs_0_, bf16[64,16]{1,0:T(8,128)(2,1)S(1)} %get-tuple-element.37.refs_1_, bf16[16,1792]{1,0:T(8,128)(2,1)S(1)} %bitcast.11, bf16[64,1792]{1,0:T(8,128)(2,1)S(1)} %get-tuple-element.38.refs_3_, ...), custom_call_target="tpu_custom_call" | custom-call | flops 268435456 | bytes 15493120 | tf_op jit(solution)/shard_map/activation/pallas_call | solution.py:48
  47.1 2.4 %collective-permute-start.6 = (bf16[16,2816]{1,0:T(8,128)(2,1)S(1)}, bf16[16,2816]{1,0:T(8,128)(2,1)S(1)}, u32[]{:S(2)}, u32[]{:S(2)}) collective-permute-start(bf16[16,2816]{1,0:T(8,128)(2,1)S(1)} %sum_pairs.3.refs_0_), channel_id=1, source_target_pairs={{0,16},{4,20},{8,24},{12,28},{16,0},{20,4},{24,8},{28,12},{1,17},{... | collective-permute-start | bytes 270344 | tf_op jit(solution)/shard_map/ppermute | solution.py:280
  49.5 4.0 %activation.5 = (bf16[64,1792]{1,0:T(8,128)(2,1)}, f32[8,128]{1,0:T(8,128)S(1)}) custom-call(bf16[64,4096]{1,0:T(8,128)(2,1)S(1)} %get-tuple-element.36.refs_0_, bf16[64,16]{1,0:T(8,128)(2,1)S(1)} %get-tuple-element.37.refs_1_, bf16[16,1792]{1,0:T(8,128)(2,1)S(1)} %bitcast.12, bf16[64,1792]{1,0:T(8,128)(2,1)S(1)} %get-tuple-element.39.refs_3_, ...), custom_call_target="tpu_custom_call" | custom-call | flops 268435456 | bytes 15493120 | tf_op jit(solution)/shard_map/activation/pallas_call | solution.py:48
  53.5 0.6 %collective-permute-done.6.refs_1_ = bf16[16,2816]{1,0:T(8,128)(2,1)S(1)} collective-permute-done((bf16[16,2816]{1,0:T(8,128)(2,1)S(1)}, bf16[16,2816]{1,0:T(8,128)(2,1)S(1)}, u32[]{:S(2)}, u32[]{:S(2)}) %collective-permute-start.6) | collective-permute-done | bytes 90144 | tf_op jit(solution)/shard_map/ppermute | solution.py:280
  54.1 0.7 %sum_last.1 = (f32[16,1792]{1,0:T(8,128)}, f32[16,1024]{1,0:T(8,128)}) custom-call(bf16[16,2816]{1,0:T(8,128)(2,1)S(1)} %sum_pairs.3.refs_0_, bf16[16,2816]{1,0:T(8,128)(2,1)S(1)} %collective-permute-done.6.refs_1_, f32[8,128]{1,0:T(8,128)S(1)} %get-tuple-element.44.refs_2_), custom_call_target="tpu_custom_call" | custom-call | bytes 184320 | tf_op jit(solution)/shard_map/sum_last/pallas_call | solution.py:48
  (11 shorter events, 0.1 us)
Async XLA Ops:
  0.6 37.4 %copy-start.1 = (bf16[1792,16]{0,1:T(8,128)(2,1)S(1)}, bf16[1792,16]{0,1:T(8,128)(2,1)}, u32[]{:S(2)}) copy-start(bf16[1792,16]{0,1:T(8,128)(2,1)} %param.12) | copy-start | bytes 172036
  0.6 17.9 %copy-start = (bf16[16,4096]{1,0:T(8,128)(2,1)S(1)}, bf16[16,4096]{1,0:T(8,128)(2,1)}, u32[]{:S(2)}) copy-start(bf16[16,4096]{1,0:T(8,128)(2,1)} %refs_5_.5) | copy-start | bytes 393220
  2.5 16.0 %all-to-all-start = ((bf16[8,8,1024]{2,1,0:T(8,128)(2,1)}), bf16[8,8,1024]{2,1,0:T(8,128)(2,1)S(1)}, u32[]{:S(2)}, u32[]{:S(2)}) async-start(bf16[8,8,1024]{2,1,0:T(8,128)(2,1)} %bitcast.5), calls=%async_computation | async-start | bytes 262144 | tf_op jit(solution)/shard_map/all_to_all | solution.py:294
  9.7 0.7 %copy-start.2 = (s32[1,64]{1,0:T(1,128)S(1)}, s32[1,64]{1,0:T(1,128)}, u32[]{:S(2)}) copy-start(s32[1,64]{1,0:T(1,128)} %refs_1_.1) | copy-start | bytes 772
  18.9 2.0 %collective-permute-start = (f32[64,2176]{1,0:T(8,128)S(1)}, f32[64,2176]{1,0:T(8,128)S(1)}, u32[]{:S(2)}, u32[]{:S(2)}) collective-permute-start(f32[64,2176]{1,0:T(8,128)S(1)} %get-tuple-element.27), channel_id=1, source_target_pairs={{0,1},{1,0},{2,3},{3,2},{4,5},{5,4},{6,7},{7,6},{8,9},{9,8},{10,11... | collective-permute-start | bytes 1671176 | tf_op jit(solution)/shard_map/ppermute | solution.py:280
  21.1 11.6 %collective-permute-start.1 = (bf16[64,2176]{1,0:T(8,128)(2,1)S(1)}, bf16[64,2176]{1,0:T(8,128)(2,1)S(1)}, u32[]{:S(2)}, u32[]{:S(2)}) collective-permute-start(bf16[64,2176]{1,0:T(8,128)(2,1)S(1)} %get-tuple-element.30), channel_id=1, source_target_pairs={{0,2},{1,3},{2,0},{3,1},{4,6},{5,7},{6,4},{7,5},{8,10},{9,11},{10,... | collective-permute-start | bytes 835592 | tf_op jit(solution)/shard_map/ppermute | solution.py:280
  22.7 10.0 %collective-permute-start.2 = (bf16[64,1024]{1,0:T(8,128)(2,1)S(1)}, bf16[64,1024]{1,0:T(8,128)(2,1)S(1)}, u32[]{:S(2)}, u32[]{:S(2)}) collective-permute-start(bf16[64,1024]{1,0:T(8,128)(2,1)S(1)} %get-tuple-element.31.refs_3_), channel_id=1, source_target_pairs={{0,2},{1,3},{2,0},{3,1},{4,6},{5,7},{6,4},{7,5},{8,10},{9,11},{10,... | collective-permute-start | bytes 393224 | tf_op jit(solution)/shard_map/ppermute | solution.py:280
  32.8 2.0 %collective-permute-start.3 = (bf16[64,4096]{1,0:T(8,128)(2,1)S(1)}, bf16[64,4096]{1,0:T(8,128)(2,1)S(1)}, u32[]{:S(2)}, u32[]{:S(2)}) collective-permute-start(bf16[64,4096]{1,0:T(8,128)(2,1)S(1)} %get-tuple-element.34.refs_3_), channel_id=1, source_target_pairs={{0,1},{1,0},{2,3},{3,2},{4,5},{5,4},{6,7},{7,6},{8,9},{9,8},{10,11... | collective-permute-start | bytes 1572872 | tf_op jit(solution)/shard_map/ppermute | solution.py:280
  35.9 6.3 %collective-permute-start.4 = (bf16[16,2816]{1,0:T(8,128)(2,1)S(1)}, bf16[16,2816]{1,0:T(8,128)(2,1)S(1)}, u32[]{:S(2)}, u32[]{:S(2)}) collective-permute-start(bf16[16,2816]{1,0:T(8,128)(2,1)S(1)} %get-tuple-element.41.refs_0_), channel_id=1, source_target_pairs={{0,4},{4,0},{8,12},{12,8},{16,20},{20,16},{24,28},{28,24},{1,5},{5... | collective-permute-start | bytes 270344 | tf_op jit(solution)/shard_map/ppermute | solution.py:280
  42.2 4.8 %collective-permute-start.5 = (bf16[16,2816]{1,0:T(8,128)(2,1)S(1)}, bf16[16,2816]{1,0:T(8,128)(2,1)S(1)}, u32[]{:S(2)}, u32[]{:S(2)}) collective-permute-start(bf16[16,2816]{1,0:T(8,128)(2,1)S(1)} %sum_pairs.2.refs_0_), channel_id=1, source_target_pairs={{0,8},{4,12},{8,0},{12,4},{16,24},{20,28},{24,16},{28,20},{1,9},{5... | collective-permute-start | bytes 270344 | tf_op jit(solution)/shard_map/ppermute | solution.py:280
  47.1 7.0 %collective-permute-start.6 = (bf16[16,2816]{1,0:T(8,128)(2,1)S(1)}, bf16[16,2816]{1,0:T(8,128)(2,1)S(1)}, u32[]{:S(2)}, u32[]{:S(2)}) collective-permute-start(bf16[16,2816]{1,0:T(8,128)(2,1)S(1)} %sum_pairs.3.refs_0_), channel_id=1, source_target_pairs={{0,16},{4,20},{8,24},{12,28},{16,0},{20,4},{24,8},{28,12},{1,17},{... | collective-permute-start | bytes 270344 | tf_op jit(solution)/shard_map/ppermute | solution.py:280

commit v3 on v2

--- a/solution.py
+++ b/solution.py
@@ -12,6 +12,7 @@
 F32, BF16 = jnp.float32, jnp.bfloat16
 LANES = 128
 ROWS = 256
+WAIT = 5_000_000_000
 VMEM = pl.BlockSpec(memory_space=pltpu.VMEM)
 SMEM = pl.BlockSpec(memory_space=pltpu.SMEM)
 
@@ -20,10 +21,10 @@
     return lax.dot_general(a, b, (dims, ((), ())), preferred_element_type=F32)
 
 
-def call(body, outs, name, *args, near=(), far=(), after=(), scratch=(), flops=0, limit=24):
+def call(body, outs, name, *args, near=(), far=(), keep=(), scratch=(), flops=0, limit=24):
     size = sum(a.size * a.dtype.itemsize for a in args + near + far)
     specs = [SMEM if a.dtype == jnp.int32 and a.size == 1 else VMEM for a in args]
-    specs += [pl.BlockSpec(memory_space=pltpu.HBM)] * (len(near) + len(far) + len(after))
+    specs += [pl.BlockSpec(memory_space=pltpu.HBM)] * (len(near) + len(far)) + [VMEM] * len(keep)
     held = [pltpu.VMEM(a.shape, a.dtype) for a in near]
     held += [pltpu.SemaphoreType.DMA((len(near),))] if near else []
 
@@ -32,7 +33,7 @@
         inputs = [refs.pop(0) for _ in args]
         distant = [refs.pop(0) for _ in near]
         inputs += [refs.pop(0) for _ in far]
-        del refs[: len(after)]
+        del refs[: len(keep)]
         if near:
             sems = refs.pop()
             here = refs[len(refs) - len(near) :]
@@ -49,12 +50,12 @@
         run,
         out_shape=[jax.ShapeDtypeStruct(*s) if isinstance(s, tuple) else s for s in outs],
         in_specs=specs,
-        out_specs=[VMEM if isinstance(s, tuple) else pl.BlockSpec(memory_space=pltpu.HBM) for s in outs],
+        out_specs=[VMEM] * len(outs),
         scratch_shapes=list(scratch) + held,
         compiler_params=pltpu.CompilerParams(vmem_limit_bytes=limit << 20),
         cost_estimate=pl.CostEstimate(flops=flops, bytes_accessed=size, transcendentals=0),
         name=name,
-    )(*args, *[pltpu.with_memory_space_constraint(a, pltpu.HBM) for a in near + far + after])
+    )(*args, *[pltpu.with_memory_space_constraint(a, pltpu.HBM) for a in near + far], *keep)
 
 
 def cuts(total, step):
@@ -70,8 +71,8 @@
     return jnp.sum(jnp.where(iota((n, n), 0) == iota((n, n), 1), column, 0), axis=0, keepdims=True)
 
 
-def route_body(passes, capacity, inputs, out_ref):
-    (device_ref,), (index_ref, table_ref), copies = inputs
+def route_body(passes, capacity, inputs, out_ref, last_ref, mine_ref):
+    (device_ref,), (index_ref, lengths_ref, table_ref), copies = inputs
     rows, slots = table_ref.shape[0], out_ref.shape[0]
     copies[0].wait()
     index = index_ref[...]
@@ -83,14 +84,19 @@
     rank = jnp.sum(earlier.astype(jnp.int32), axis=1, keepdims=True)
     slot = turned(dest * capacity + rank)
     picker = (iota((slots, rows), 0) == slot).astype(F32).astype(BF16)
+    own = iota((passes, total), 1) == device_ref[0] * passes + iota((passes, total), 0)
+    mine_ref[...] = jnp.sum(jnp.where(own, index, 0), axis=1, keepdims=True)
     copies[1].wait()
+    upto = jnp.where(iota((passes, passes), 1) <= iota((passes, passes), 0), lengths_ref[...], 0)
+    last_ref[...] = jnp.sum(upto, axis=1, keepdims=True) - 1
+    copies[2].wait()
     out_ref[...] = dot(picker, table_ref[...]).astype(BF16)
 
 
 def slot_picker(index_ref, owners, owned, capacity):
-    row = index_ref[...]
-    n = row.shape[1]
-    column = jnp.sum(jnp.where(iota((n, n), 0) == iota((n, n), 1), row, 0), axis=1, keepdims=True)
+    column = index_ref[...]
+    n = column.shape[0]
+    row = turned(column)
     owner = column // owned
     earlier = (owner == row // owned) & (row < column)
     slot = owner * capacity + jnp.sum(earlier.astype(jnp.int32), axis=1, keepdims=True)
@@ -98,7 +104,7 @@
 
 
 def project_body(inputs, out_ref, pooled_ref, low_ref, act_held, weight_held, act_sems, sems):
-    (member_ref, lengths_ref, act_ref, weight_ref), (residual_ref, input_factor_ref), copies = inputs
+    (member_ref, last_ref, act_ref, weight_ref), (residual_ref, input_factor_ref), copies = inputs
     hidden = weight_held.shape[0]
     pieces = []
     for i, (at, size) in enumerate(cuts(hidden, ROWS)):
@@ -108,11 +114,7 @@
         copy = pltpu.make_async_copy(weight_ref.at[piece], weight_held.at[piece], sems.at[i])
         copy.start()
         pieces.append((piece, act_copy, copy))
-    lengths = lengths_ref[...]
-    n = lengths.shape[1]
-    upto = jnp.where(iota((n, n), 1) <= iota((n, n), 0), lengths, 0)
-    last = jnp.sum(upto, axis=1, keepdims=True) - 1
-    picker = (last == iota((n, act_ref.shape[0]), 1)).astype(F32).astype(BF16)
+    picker = (last_ref[...] == iota((last_ref.shape[0], act_ref.shape[0]), 1)).astype(F32).astype(BF16)
     for piece, act_copy, copy in pieces:
         act_copy.wait()
         pooled = dot(picker, act_held[:, piece]).astype(BF16)
@@ -227,34 +229,26 @@
     second_ref[...] = total[:, hidden:]
 
 
-def activation_body(start, stop, *refs):
-    direction_ref, spread_ref, input_factor_ref = refs[:3]
-    weight_ref, out_ref, token_ref, held, sems = refs[-5:]
+def activation_body(start, stop, direction_ref, spread_ref, input_factor_ref, weight_ref, *refs):
+    *before, out_ref, token_ref = refs
     token_ref[...] = jnp.zeros_like(token_ref)
-    whole = (stop - start) // ROWS
-
-    def load(i, at, size):
-        to = held.at[i] if size == ROWS else held.at[i, :size]
-        return pltpu.make_async_copy(weight_ref.at[pl.ds(at, size)], to, sems.at[i])
-
-    def part(i, at, size):
+    for ref in before:
+        out_ref[:, :start] = ref[:, :start]
+
+    def part(at, size):
         columns = pl.ds(at, size)
         value = ADAPTER_SCALE * dot(spread_ref[...], input_factor_ref[:, columns])
-        load(i, at, size).wait()
-        rows = held[i] if size == ROWS else held[i, :size]
-        out_ref[:, columns] = (value + dot(direction_ref[...], rows, ((1,), (1,)))).astype(BF16)
-
-    for i, (at, size) in enumerate(cuts(stop - start, ROWS)):
-        load(i, start + at, size).start()
-    if start:
-        out_ref[:, :start] = refs[3][:, :start]
+        value += dot(direction_ref[...], weight_ref[columns, :], ((1,), (1,)))
+        out_ref[:, columns] = value.astype(BF16)
+
+    whole = (stop - start) // ROWS
 
     @pl.loop(0, whole)
     def _(i):
-        part(i, pl.multiple_of(start + i * ROWS, ROWS), ROWS)
+        part(pl.multiple_of(start + i * ROWS, ROWS), ROWS)
 
     if whole * ROWS < stop - start:
-        part(whole, start + whole * ROWS, stop - start - whole * ROWS)
+        part(start + whole * ROWS, stop - start - whole * ROWS)
 
 
 def local(gradient_table, residual_input_rows, act, down_weight, adapter_input_factor, adapter_output_factor, lengths,
@@ -286,19 +280,19 @@
         bit *= 2
 
     index = owning_row_index.reshape(1, -1)
-    my_index = lax.dynamic_slice_in_dim(owning_row_index, device * passes, passes).reshape(1, -1)
-    (sent,) = call(
-        functools.partial(route_body, passes, capacity), [((slots, columns), BF16)], "route",
-        dp_at, near=(index, gradient_table),
+    sent, last, my_index = call(
+        functools.partial(route_body, passes, capacity),
+        [((slots, columns), BF16), ((passes, 1), jnp.int32), ((passes, 1), jnp.int32)], "route",
+        dp_at, near=(index, lengths, gradient_table),
     )
     routed = lax.all_to_all(sent, "dp", 0, 0, tiled=True)
     pieces = len(cuts(hidden, ROWS))
     terms, pooled, low = call(
         project_body, [((passes, model), F32), ((passes, hidden), BF16), ((passes, rank), F32)], "project",
-        member_at, lengths, near=(residual_input_rows, input_factor), far=(act, down_weight),
+        member_at, last, near=(residual_input_rows, input_factor), far=(act, down_weight),
         scratch=[pltpu.VMEM(act.shape, BF16), pltpu.VMEM(down_weight.shape, BF16)]
         + [pltpu.SemaphoreType.DMA((pieces,))] * 2,
-        flops=2 * passes * hidden * model, limit=32,
+        flops=2 * passes * hidden * model,
     )
     away, grads = call(
         functools.partial(finish_body, devices, owned, capacity),
@@ -311,6 +305,7 @@
         sum_cores_body, [*sums, ((passes, width + LANES), BF16)], "sum_cores",
         member_at, terms, low, away, adapter_output_factor,
     )
+    weight = pltpu.with_memory_space_constraint(down_weight, pltpu.VMEM)
     for bit in steps:
         got, got_grads = swap(out, "tensor", members, bit), swap(grads, "tensor", members, bit)
         joined = 2 * grads.shape[1]
@@ -318,15 +313,14 @@
         outs = [((passes, width + joined), BF16)] if last else [(out.shape, BF16), ((passes, joined), BF16)]
         total, low, out, *more = call(
             functools.partial(sum_chips_body, last), [*sums, *outs], "sum_chips",
-            total, low, got, grads, got_grads,
+            total, low, got, grads, got_grads, flops=WAIT,
         )
         grads = more[0] if more else None
     other = swap(out, "tensor", members, 1)
     direction, spread, packed = call(
         functools.partial(direction_body, count, blocks),
         [((passes, model), BF16), ((passes, rank), BF16), ((rank, hidden + columns), BF16)], "direction",
-        member_at, total, low, out, other, adapter_output_factor, pooled,
-        flops=passes * model * 64,
+        member_at, total, low, out, other, adapter_output_factor, pooled, flops=WAIT,
     )
     parts = 3
     ends = [min(hidden, -(-pieces * (i + 1) // parts) * ROWS) for i in range(parts)]
@@ -338,11 +332,7 @@
         stop = todo.pop(0)
         out, done = call(
             functools.partial(activation_body, start, stop), [((passes, hidden), BF16), ((8, LANES), F32)], "activation",
-            direction, spread, input_factor, *activation, far=(down_weight,),
-            scratch=[
-                pltpu.VMEM((-(-(stop - start) // ROWS), ROWS, model), BF16),
-                pltpu.SemaphoreType.DMA((-(-(stop - start) // ROWS),)),
-            ],
+            direction, spread, input_factor, weight, *activation,
             flops=passes * (stop - start) * model * 2,
         )
         activation[:] = [out]
@@ -358,7 +348,7 @@
             if todo:
                 activate()
             if bit < devices:
-                (packed,) = call(round_sum_body, [(packed.shape, BF16)], "sum_pairs", packed, got, *token)
+                (packed,) = call(round_sum_body, [(packed.shape, BF16)], "sum_pairs", packed, got, *token, keep=(weight,))
             else:
                 sums = call(last_sum_body, shapes, "sum_last", packed, got, *token)
     else:

time: 55.1 us -> 50.7 us (0.920)
  Pallas kernels: 23.1 us -> 17.8 us
  waiting for transfers between devices: 13.9 us -> 15.6 us
  local copies, waits for them, and re-layouts: 1.42 us -> 0.2 us
    pallas_call x12, Pallas kernels: 23.1 us -> 17.8 us  [call(): pl.pallas_call(run, out_shape=[jax.ShapeDtypeStruct(*s) if isinstance(s,...]
    ppermute x7, waiting for transfers between devices: 13.9 us -> 15.6 us  [swap(): return lax.ppermute(x, axis, [(i, i ^ bit) for i in range(size)])]
    reshape x1 -> x0, local copies, waits for them, and re-layouts: 0.76 us -> none  [local(): lax.dynamic_slice_in_dim(owning_row_index, device * passes, passes)]
  transfers between devices with their start and end apart: 8 -> 8, of which waited for: 4 -> 6; matrix products, arithmetic and copies ran while one was open for 1% -> 0% of each run, Pallas kernels for 34% -> 26%
where the time goes in v3:
time: 50.7 us; the launch traced here: 50.5 us
  Pallas kernels  17.8 us (35%)
  starting transfers between devices  16.1 us (32%)
  waiting for transfers between devices  15.6 us (31%)
  between operations  0.76 us (1%)
    pallas_call x12, Pallas kernels, call(): pl.pallas_call(run, out_shape=[jax.ShapeDtypeStruct(*s) if isinstance(s,...  17.8 us
    ppermute x7, waiting for transfers between devices, swap(): return lax.ppermute(x, axis, [(i, i ^ bit) for i in range(size)])  15.6 us
    ppermute x7, starting transfers between devices, swap(): return lax.ppermute(x, axis, [(i, i ^ bit) for i in range(size)])  8.82 us
    all_to_all x1, starting transfers between devices, local(): routed = lax.all_to_all(sent, 'dp', 0, 0, tiled=True)  7.26 us
  transfers between devices with their start and end apart: 8, of which 6 were waited for; matrix products, arithmetic and copies ran while one was open for 0% of the time, Pallas kernels for 26%

profile of v3, /device:TPU:0, one launch (start us, length us, event | category | flops | bytes accessed | tf_op | source)
XLA Modules:
  0.0 50.5 jit_solution(11385646113944097888)
XLA Ops:
  0.6 1.9 %route.1 = (bf16[64,1024]{1,0:T(8,128)(2,1)}, s32[64,1]{1,0:T(8,128)S(1)}, s32[64,1]{1,0:T(8,128)S(1)}) custom-call(s32[1]{0:T(128)} %bitcast.1.refs_0_, s32[1,512]{1,0:T(1,128)} %bitcast.14, s32[1,64]{1,0:T(1,128)} %refs_2_.2, bf16[64,1024]{1,0:T(8,128)(2,1)} %refs_3_.6), custom_call_target="tpu_custom_call" | custom-call | bytes 133380 | tf_op jit(solution)/shard_map/route/pallas_call | solution.py:49
  2.5 7.3 %all-to-all-start = ((bf16[8,8,1024]{2,1,0:T(8,128)(2,1)}), bf16[8,8,1024]{2,1,0:T(8,128)(2,1)S(1)}, u32[]{:S(2)}, u32[]{:S(2)}) async-start(bf16[8,8,1024]{2,1,0:T(8,128)(2,1)} %bitcast.4), calls=%async_computation | async-start | bytes 262144 | tf_op jit(solution)/shard_map/all_to_all | solution.py:288
  9.8 7.4 %project.1 = (f32[64,4096]{1,0:T(8,128)S(1)}, bf16[64,1792]{1,0:T(8,128)(2,1)S(1)}, f32[64,16]{1,0:T(8,128)S(1)}) custom-call(s32[1]{0:T(128)} %bitcast.refs_0_, s32[64,1]{1,0:T(8,128)S(1)} %get-tuple-element.28.refs_1_, bf16[64,1024]{1,0:T(8,128)(2,1)} %refs_2_.3, bf16[16,1792]{1,0:T(8,128)(2,1)} %bitcast.9, bf16[1024,1792]{1,0:T(8,128)(2,1)} %refs_4_.2, ...), custom_call_target="tpu_custom_call" | custom-call | flops 939524096 | bytes 18538756 | tf_op jit(solution)/shard_map/project/pallas_call | solution.py:49
  17.2 0.4 finish.1
  17.6 0.1 collective-permute-start
  17.7 1.9 %collective-permute-done.refs_3_ = f32[64,2176]{1,0:T(8,128)S(1)} collective-permute-done((f32[64,2176]{1,0:T(8,128)S(1)}, f32[64,2176]{1,0:T(8,128)S(1)}, u32[]{:S(2)}, u32[]{:S(2)}) %collective-permute-start) | collective-permute-done | bytes 557088 | tf_op jit(solution)/shard_map/ppermute | solution.py:274
  19.6 0.2 sum_cores.1
  19.9 1.6 %collective-permute-start.1 = (bf16[64,2176]{1,0:T(8,128)(2,1)S(1)}, bf16[64,2176]{1,0:T(8,128)(2,1)S(1)}, u32[]{:S(2)}, u32[]{:S(2)}) collective-permute-start(bf16[64,2176]{1,0:T(8,128)(2,1)S(1)} %get-tuple-element.36), channel_id=1, source_target_pairs={{0,2},{1,3},{2,0},{3,1},{4,6},{5,7},{6,4},{7,5},{8,10},{9,11},{10,... | collective-permute-start | bytes 835592 | tf_op jit(solution)/shard_map/ppermute | solution.py:274
  21.5 0.5 collective-permute-start.2
  21.9 9.5 %collective-permute-done.2.refs_4_ = bf16[64,1024]{1,0:T(8,128)(2,1)S(1)} collective-permute-done((bf16[64,1024]{1,0:T(8,128)(2,1)S(1)}, bf16[64,1024]{1,0:T(8,128)(2,1)S(1)}, u32[]{:S(2)}, u32[]{:S(2)}) %collective-permute-start.2) | collective-permute-done | bytes 131104 | tf_op jit(solution)/shard_map/ppermute | solution.py:274
  31.4 0.1 sum_chips.1
  31.6 1.9 %collective-permute-done.3.refs_4_ = bf16[64,4096]{1,0:T(8,128)(2,1)S(1)} collective-permute-done((bf16[64,4096]{1,0:T(8,128)(2,1)S(1)}, bf16[64,4096]{1,0:T(8,128)(2,1)S(1)}, u32[]{:S(2)}, u32[]{:S(2)}) %collective-permute-start.3) | collective-permute-done | bytes 524320 | tf_op jit(solution)/shard_map/ppermute | solution.py:274
  33.5 1.1 %direction.1 = (bf16[64,4096]{1,0:T(8,128)(2,1)S(1)}, bf16[64,16]{1,0:T(8,128)(2,1)S(1)}, bf16[16,2816]{1,0:T(8,128)(2,1)S(1)}) custom-call(s32[1]{0:T(128)} %bitcast.refs_0_, f32[64,2048]{1,0:T(8,128)S(1)} %get-tuple-element.38.refs_1_, f32[64,16]{1,0:T(8,128)S(1)} %get-tuple-element.39.refs_2_, bf16[64,4096]{1,0:T(8,128)(2,1)S(1)} %get-tuple-element.40.refs_3_, ...), custom_call_target="tpu_custom_call" | custom-call | flops 5000000000 | bytes 1937412 | tf_op jit(solution)/shard_map/direction/pallas_call | solution.py:49
  34.6 2.1 %collective-permute-start.4 = (bf16[16,2816]{1,0:T(8,128)(2,1)S(1)}, bf16[16,2816]{1,0:T(8,128)(2,1)S(1)}, u32[]{:S(2)}, u32[]{:S(2)}) collective-permute-start(bf16[16,2816]{1,0:T(8,128)(2,1)S(1)} %get-tuple-element.47.refs_0_), channel_id=1, source_target_pairs={{0,4},{4,0},{8,12},{12,8},{16,20},{20,16},{24,28},{28,24},{1,5},{5... | collective-permute-start | bytes 270344 | tf_op jit(solution)/shard_map/ppermute | solution.py:274
  36.7 0.2 slice-done.3
  36.9 2.3 %activation.3 = (bf16[64,1792]{1,0:T(8,128)(2,1)S(1)}, f32[8,128]{1,0:T(8,128)S(1)}) custom-call(bf16[64,4096]{1,0:T(8,128)(2,1)S(1)} %get-tuple-element.42.refs_0_, bf16[64,16]{1,0:T(8,128)(2,1)S(1)} %get-tuple-element.43.refs_1_, bf16[16,1792]{1,0:T(8,128)(2,1)S(1)} %bitcast.10, bf16[1792,4096]{1,0:T(8,128)(2,1)S(1)} %bitcast.8), custom_call_target="tpu_custom_call" | custom-call | flops 402653184 | bytes 15263744 | tf_op jit(solution)/shard_map/activation/pallas_call | solution.py:49
  39.2 0.4 collective-permute-done.4.refs_1_
  39.7 1.8 %collective-permute-start.5 = (bf16[16,2816]{1,0:T(8,128)(2,1)S(1)}, bf16[16,2816]{1,0:T(8,128)(2,1)S(1)}, u32[]{:S(2)}, u32[]{:S(2)}) collective-permute-start(bf16[16,2816]{1,0:T(8,128)(2,1)S(1)} %sum_pairs.2.refs_0_), channel_id=1, source_target_pairs={{0,8},{4,12},{8,0},{12,4},{16,24},{20,28},{24,16},{28,20},{1,9},{5... | collective-permute-start | bytes 270344 | tf_op jit(solution)/shard_map/ppermute | solution.py:274
  41.5 1.5 %activation.4 = (bf16[64,1792]{1,0:T(8,128)(2,1)S(1)}, f32[8,128]{1,0:T(8,128)S(1)}) custom-call(bf16[64,4096]{1,0:T(8,128)(2,1)S(1)} %get-tuple-element.42.refs_0_, bf16[64,16]{1,0:T(8,128)(2,1)S(1)} %get-tuple-element.43.refs_1_, bf16[16,1792]{1,0:T(8,128)(2,1)S(1)} %bitcast.11, bf16[1792,4096]{1,0:T(8,128)(2,1)S(1)} %bitcast.8, ...), custom_call_target="tpu_custom_call" | custom-call | flops 268435456 | bytes 15493120 | tf_op jit(solution)/shard_map/activation/pallas_call | solution.py:49
  43.0 1.3 %collective-permute-done.5.refs_1_ = bf16[16,2816]{1,0:T(8,128)(2,1)S(1)} collective-permute-done((bf16[16,2816]{1,0:T(8,128)(2,1)S(1)}, bf16[16,2816]{1,0:T(8,128)(2,1)S(1)}, u32[]{:S(2)}, u32[]{:S(2)}) %collective-permute-start.5) | collective-permute-done | bytes 90144 | tf_op jit(solution)/shard_map/ppermute | solution.py:274
  44.3 2.7 %collective-permute-start.6 = (bf16[16,2816]{1,0:T(8,128)(2,1)S(1)}, bf16[16,2816]{1,0:T(8,128)(2,1)S(1)}, u32[]{:S(2)}, u32[]{:S(2)}) collective-permute-start(bf16[16,2816]{1,0:T(8,128)(2,1)S(1)} %sum_pairs.3.refs_0_), channel_id=1, source_target_pairs={{0,16},{4,20},{8,24},{12,28},{16,0},{20,4},{24,8},{28,12},{1,17},{... | collective-permute-start | bytes 270344 | tf_op jit(solution)/shard_map/ppermute | solution.py:274
  47.0 2.2 %activation.5 = (bf16[64,1792]{1,0:T(8,128)(2,1)}, f32[8,128]{1,0:T(8,128)S(1)}) custom-call(bf16[64,4096]{1,0:T(8,128)(2,1)S(1)} %get-tuple-element.42.refs_0_, bf16[64,16]{1,0:T(8,128)(2,1)S(1)} %get-tuple-element.43.refs_1_, bf16[16,1792]{1,0:T(8,128)(2,1)S(1)} %bitcast.12, bf16[1792,4096]{1,0:T(8,128)(2,1)S(1)} %bitcast.8, ...), custom_call_target="tpu_custom_call" | custom-call | flops 268435456 | bytes 15493120 | tf_op jit(solution)/shard_map/activation/pallas_call | solution.py:49
  49.2 0.6 %collective-permute-done.6.refs_1_ = bf16[16,2816]{1,0:T(8,128)(2,1)S(1)} collective-permute-done((bf16[16,2816]{1,0:T(8,128)(2,1)S(1)}, bf16[16,2816]{1,0:T(8,128)(2,1)S(1)}, u32[]{:S(2)}, u32[]{:S(2)}) %collective-permute-start.6) | collective-permute-done | bytes 90144 | tf_op jit(solution)/shard_map/ppermute | solution.py:274
  49.8 0.7 %sum_last.1 = (f32[16,1792]{1,0:T(8,128)}, f32[16,1024]{1,0:T(8,128)}) custom-call(bf16[16,2816]{1,0:T(8,128)(2,1)S(1)} %sum_pairs.3.refs_0_, bf16[16,2816]{1,0:T(8,128)(2,1)S(1)} %collective-permute-done.6.refs_1_, f32[8,128]{1,0:T(8,128)S(1)} %get-tuple-element.50.refs_2_), custom_call_target="tpu_custom_call" | custom-call | bytes 184320 | tf_op jit(solution)/shard_map/sum_last/pallas_call | solution.py:49
  (17 shorter events, 0.1 us)
Async XLA Ops:
  0.6 16.6 %copy-start.1 = (bf16[16,4096]{1,0:T(8,128)(2,1)S(1)}, bf16[16,4096]{1,0:T(8,128)(2,1)}, u32[]{:S(2)}) copy-start(bf16[16,4096]{1,0:T(8,128)(2,1)} %refs_5_.5) | copy-start | bytes 393220
  2.5 14.6 %all-to-all-start = ((bf16[8,8,1024]{2,1,0:T(8,128)(2,1)}), bf16[8,8,1024]{2,1,0:T(8,128)(2,1)S(1)}, u32[]{:S(2)}, u32[]{:S(2)}) async-start(bf16[8,8,1024]{2,1,0:T(8,128)(2,1)} %bitcast.4), calls=%async_computation | async-start | bytes 262144 | tf_op jit(solution)/shard_map/all_to_all | solution.py:288
  17.6 2.0 %collective-permute-start = (f32[64,2176]{1,0:T(8,128)S(1)}, f32[64,2176]{1,0:T(8,128)S(1)}, u32[]{:S(2)}, u32[]{:S(2)}) collective-permute-start(f32[64,2176]{1,0:T(8,128)S(1)} %get-tuple-element.33), channel_id=1, source_target_pairs={{0,1},{1,0},{2,3},{3,2},{4,5},{5,4},{6,7},{7,6},{8,9},{9,8},{10,11... | collective-permute-start | bytes 1671176 | tf_op jit(solution)/shard_map/ppermute | solution.py:274
  19.9 11.6 %collective-permute-start.1 = (bf16[64,2176]{1,0:T(8,128)(2,1)S(1)}, bf16[64,2176]{1,0:T(8,128)(2,1)S(1)}, u32[]{:S(2)}, u32[]{:S(2)}) collective-permute-start(bf16[64,2176]{1,0:T(8,128)(2,1)S(1)} %get-tuple-element.36), channel_id=1, source_target_pairs={{0,2},{1,3},{2,0},{3,1},{4,6},{5,7},{6,4},{7,5},{8,10},{9,11},{10,... | collective-permute-start | bytes 835592 | tf_op jit(solution)/shard_map/ppermute | solution.py:274
  21.5 10.0 %collective-permute-start.2 = (bf16[64,1024]{1,0:T(8,128)(2,1)S(1)}, bf16[64,1024]{1,0:T(8,128)(2,1)S(1)}, u32[]{:S(2)}, u32[]{:S(2)}) collective-permute-start(bf16[64,1024]{1,0:T(8,128)(2,1)S(1)} %get-tuple-element.37.refs_3_), channel_id=1, source_target_pairs={{0,2},{1,3},{2,0},{3,1},{4,6},{5,7},{6,4},{7,5},{8,10},{9,11},{10,... | collective-permute-start | bytes 393224 | tf_op jit(solution)/shard_map/ppermute | solution.py:274
  31.4 5.3 %slice-start = ((s8[14680064]{0:T(1024)(128)(4,1)}), s8[4194304]{0:T(1024)(128)(4,1)S(1)}, s32[]{:S(2)}) async-start(s8[14680064]{0:T(1024)(128)(4,1)} %bitcast.7), calls=%async_computation.1 | async-start | bytes 8388608
  31.4 5.3 %slice-start.1 = ((s8[14680064]{0:T(1024)(128)(4,1)}), s8[4194304]{0:T(1024)(128)(4,1)S(1)}, s32[]{:S(2)}) async-start(s8[14680064]{0:T(1024)(128)(4,1)} %bitcast.7), calls=%async_computation.2 | async-start | bytes 8388608
  31.4 5.3 %copy-start = (bf16[1792,16]{0,1:T(8,128)(2,1)S(1)}, bf16[1792,16]{0,1:T(8,128)(2,1)}, u32[]{:S(2)}) copy-start(bf16[1792,16]{0,1:T(8,128)(2,1)} %param.12) | copy-start | bytes 172036
  31.6 2.0 %collective-permute-start.3 = (bf16[64,4096]{1,0:T(8,128)(2,1)S(1)}, bf16[64,4096]{1,0:T(8,128)(2,1)S(1)}, u32[]{:S(2)}, u32[]{:S(2)}) collective-permute-start(bf16[64,4096]{1,0:T(8,128)(2,1)S(1)} %get-tuple-element.40.refs_3_), channel_id=1, source_target_pairs={{0,1},{1,0},{2,3},{3,2},{4,5},{5,4},{6,7},{7,6},{8,9},{9,8},{10,11... | collective-permute-start | bytes 1572872 | tf_op jit(solution)/shard_map/ppermute | solution.py:274
  33.5 3.2 %slice-start.2 = ((s8[14680064]{0:T(1024)(128)(4,1)}), s8[4194304]{0:T(1024)(128)(4,1)S(1)}, s32[]{:S(2)}) async-start(s8[14680064]{0:T(1024)(128)(4,1)} %bitcast.7), calls=%async_computation.3 | async-start | bytes 8388608
  33.5 3.4 %slice-start.3 = ((s8[14680064]{0:T(1024)(128)(4,1)}), s8[2097152]{0:T(1024)(128)(4,1)S(1)}, s32[]{:S(2)}) async-start(s8[14680064]{0:T(1024)(128)(4,1)} %bitcast.7), calls=%async_computation.4 | async-start | bytes 4194304
  34.6 5.0 %collective-permute-start.4 = (bf16[16,2816]{1,0:T(8,128)(2,1)S(1)}, bf16[16,2816]{1,0:T(8,128)(2,1)S(1)}, u32[]{:S(2)}, u32[]{:S(2)}) collective-permute-start(bf16[16,2816]{1,0:T(8,128)(2,1)S(1)} %get-tuple-element.47.refs_0_), channel_id=1, source_target_pairs={{0,4},{4,0},{8,12},{12,8},{16,20},{20,16},{24,28},{28,24},{1,5},{5... | collective-permute-start | bytes 270344 | tf_op jit(solution)/shard_map/ppermute | solution.py:274
  39.7 4.6 %collective-permute-start.5 = (bf16[16,2816]{1,0:T(8,128)(2,1)S(1)}, bf16[16,2816]{1,0:T(8,128)(2,1)S(1)}, u32[]{:S(2)}, u32[]{:S(2)}) collective-permute-start(bf16[16,2816]{1,0:T(8,128)(2,1)S(1)} %sum_pairs.2.refs_0_), channel_id=1, source_target_pairs={{0,8},{4,12},{8,0},{12,4},{16,24},{20,28},{24,16},{28,20},{1,9},{5... | collective-permute-start | bytes 270344 | tf_op jit(solution)/shard_map/ppermute | solution.py:274
  44.3 5.5 %collective-permute-start.6 = (bf16[16,2816]{1,0:T(8,128)(2,1)S(1)}, bf16[16,2816]{1,0:T(8,128)(2,1)S(1)}, u32[]{:S(2)}, u32[]{:S(2)}) collective-permute-start(bf16[16,2816]{1,0:T(8,128)(2,1)S(1)} %sum_pairs.3.refs_0_), channel_id=1, source_target_pairs={{0,16},{4,20},{8,24},{12,28},{16,0},{20,4},{24,8},{28,12},{1,17},{... | collective-permute-start | bytes 270344 | tf_op jit(solution)/shard_map/ppermute | solution.py:274

commit v4 on v3

--- a/solution.py
+++ b/solution.py
@@ -133,88 +133,83 @@
     out_ref[:, own] += residual_ref[...].astype(F32)
 
 
-def half_of(half, width, parts_ref, low_ref, factor_ref):
-    columns = pl.ds(pl.multiple_of(half * width, LANES), width)
-    return parts_ref[:, columns] + ADAPTER_SCALE * dot(low_ref[...].astype(BF16), factor_ref[:, columns])
+def term_of(block, columns, parts_ref, low_ref, factor_ref):
+    at = pl.ds(pl.multiple_of(block * columns, LANES), columns)
+    return parts_ref[:, at] + ADAPTER_SCALE * dot(low_ref[...].astype(BF16), factor_ref[:, at])
 
 
 def finish_body(owners, owned, capacity, member_ref, index_ref, routed_ref, parts_ref, low_ref, factor_ref, away_ref,
                 grads_ref):
-    width, rank = parts_ref.shape[1] // 2, low_ref.shape[1]
-    away_ref[:, :width] = half_of(1 - member_ref[0] % 2, width, parts_ref, low_ref, factor_ref)
-    away_ref[:, width:] = jnp.zeros_like(away_ref[:, width:])
-    away_ref[:, width : width + rank] = low_ref[...]
+    columns = grads_ref.shape[1]
+    for j in range(away_ref.shape[1] // columns):
+        block = 2 * j + 1 - member_ref[0] % 2
+        away_ref[:, j * columns : (j + 1) * columns] = term_of(block, columns, parts_ref, low_ref, factor_ref)
     grads_ref[...] = dot(slot_picker(index_ref, owners, owned, capacity), routed_ref[...]).astype(BF16)
 
 
-def put_low(low, at, out_ref):
-    rank = low.shape[1]
-    high = low.astype(BF16)
-    out_ref[:, at:] = jnp.zeros_like(out_ref[:, at:])
-    out_ref[:, at : at + rank] = high
-    out_ref[:, at + rank : at + 2 * rank] = (low - high.astype(F32)).astype(BF16)
-
-
-def sum_cores_body(member_ref, parts_ref, low_ref, away_ref, factor_ref, total_ref, low_total_ref, out_ref):
-    width, rank = parts_ref.shape[1] // 2, low_ref.shape[1]
-    total = half_of(member_ref[0] % 2, width, parts_ref, low_ref, factor_ref) + away_ref[:, :width]
-    low = low_ref[...] + away_ref[:, width : width + rank]
-    total_ref[...] = total
-    low_total_ref[...] = low
-    out_ref[:, :width] = total.astype(BF16)
-    put_low(low, width, out_ref)
-
-
-def sum_chips_body(last, total_ref, low_ref, got_ref, grads_ref, got_grads_ref, new_total_ref, new_low_ref, out_ref,
-                   *more):
-    width, rank = total_ref.shape[1], low_ref.shape[1]
-    total = total_ref[...] + got_ref[:, :width].astype(F32)
-    low = low_ref[...]
-    for i in range(2):
-        low += got_ref[:, width + i * rank : width + (i + 1) * rank].astype(F32)
-    new_total_ref[...] = total
-    new_low_ref[...] = low
-    out_ref[:, :width] = total.astype(BF16)
+def sum_cores_body(columns, member_ref, parts_ref, low_ref, away_ref, factor_ref, pooled_ref, keep_ref, send_ref,
+                   pooled_out_ref):
+    pooled_out_ref[...] = pooled_ref[...]
+    member = member_ref[0]
+    n = keep_ref.shape[1] // columns
+    side = member // 2 // n % 2
+    for i in range(n):
+        for ref, j in ((keep_ref, side * n + i), (send_ref, (1 - side) * n + i)):
+            value = term_of(2 * j + member % 2, columns, parts_ref, low_ref, factor_ref)
+            value += away_ref[:, pl.ds(pl.multiple_of(j * columns, LANES), columns)]
+            ref[:, i * columns : (i + 1) * columns] = value.astype(ref.dtype)
+
+
+def sum_chips_body(columns, member_ref, kept_ref, got_ref, keep_ref, send_ref):
+    n = keep_ref.shape[1] // columns
+    side = member_ref[0] // 2 // n % 2
+    for ref, half in ((keep_ref, side), (send_ref, 1 - side)):
+        at = pl.ds(pl.multiple_of(half * n * columns, LANES), n * columns)
+        ref[...] = (kept_ref[:, at] + got_ref[:, at].astype(F32)).astype(ref.dtype)
+
+
+def stats_body(member_ref, kept_ref, got_ref, grads_ref, low_ref, factor_ref, hidden_ref, stats_ref):
+    rank = low_ref.shape[1]
     columns = grads_ref.shape[1]
-    if last:
-        joined_ref, at = out_ref, width
-    else:
-        put_low(low, width, out_ref)
-        (joined_ref,), at = more, 0
-    joined_ref[:, at : at + columns] = grads_ref[...]
-    joined_ref[:, at + columns : at + 2 * columns] = got_grads_ref[...]
-
-
-def direction_body(count, blocks, member_ref, total_ref, low_ref, mine_ref, other_ref, factor_ref, pooled_ref,
-                   direction_ref, spread_ref, packed_ref):
-    member = member_ref[0]
-    width = total_ref.shape[1]
-    columns = width // blocks
-
-    def hidden_block(b):
-        piece = slice(b % blocks * columns, (b % blocks + 1) * columns)
-        return jnp.where(member % 2 == b // blocks, total_ref[:, piece], other_ref[:, piece].astype(F32))
-
-    def grads_block(b):
-        apart = member ^ b
-        piece = pl.ds(pl.multiple_of(width + apart // 2 * columns, LANES), columns)
-        return jnp.where(apart % 2 == 0, mine_ref[:, piece].astype(F32), other_ref[:, piece].astype(F32))
-
-    squares = sum(jnp.sum(hidden_block(b) ** 2, axis=1, keepdims=True) for b in range(2 * blocks))
-    length = jnp.sqrt(squares + EPSILON)
-    along = sum(
-        jnp.sum(grads_block(b) * (hidden_block(b) / length), axis=1, keepdims=True) for b in range(2 * blocks)
-    )
-    for b in range(2 * blocks):
-        value = (grads_block(b) - along * (hidden_block(b) / length)) / length
-        direction_ref[:, b * columns : (b + 1) * columns] = value.astype(BF16)
-    spread = dot(direction_ref[...], factor_ref[...], ((1,), (1,))).astype(BF16)
+    hidden = kept_ref[...] + got_ref[...].astype(F32)
+    hidden_ref[...] = hidden
+    factor = factor_ref[:, pl.ds(pl.multiple_of(member_ref[0] * columns, LANES), columns)]
+    high = hidden.astype(BF16)
+    rest = (hidden - high.astype(F32)).astype(BF16)
+    lanes = ((1,), (1,))
+    stats_ref[...] = jnp.zeros_like(stats_ref)
+    stats_ref[:, :1] = jnp.sum(hidden * hidden, axis=1, keepdims=True)
+    stats_ref[:, 1:2] = jnp.sum(hidden * grads_ref[...].astype(F32), axis=1, keepdims=True)
+    stats_ref[:, rank : 2 * rank] = dot(high, factor, lanes) + dot(rest, factor, lanes)
+    stats_ref[:, 2 * rank : 3 * rank] = dot(grads_ref[...], factor, lanes)
+    stats_ref[:, 3 * rank : 4 * rank] = low_ref[...]
+
+
+def direction_body(count, stats_ref, got_ref, hidden_ref, grads_ref, direction_ref, spread_ref, packed_ref):
+    rank = spread_ref.shape[1]
+    stats = stats_ref[...] + got_ref[...]
+    length = jnp.sqrt(stats[:, :1] + EPSILON)
+    along = stats[:, 1:2] / length
+    direction = ((grads_ref[...].astype(F32) - along * (hidden_ref[...] / length)) / length).astype(BF16)
+    direction_ref[...] = direction
+    spread = (stats[:, 2 * rank : 3 * rank] - along * (stats[:, rank : 2 * rank] / length)) / length
+    spread = spread.astype(BF16)
     spread_ref[...] = spread
-    hidden = pooled_ref.shape[1]
-    scale = ADAPTER_SCALE / count
-    packed_ref[:, :hidden] = (scale * dot(spread, pooled_ref[...], ((0,), (0,)))).astype(BF16)
-    own = direction_ref[:, pl.ds(pl.multiple_of(member * columns, LANES), columns)]
-    packed_ref[:, hidden:] = (scale * dot(low_ref[...].astype(BF16), own, ((0,), (0,)))).astype(BF16)
+    low = stats[:, 3 * rank : 4 * rank].astype(BF16)
+    passes, columns = direction.shape
+    packed_ref[:, :columns] = (ADAPTER_SCALE / count * dot(low, direction, ((0,), (0,)))).astype(BF16)
+    packed_ref[:, columns:] = jnp.zeros_like(packed_ref[:, columns:])
+    same = (iota((passes, passes), 0) == iota((passes, passes), 1)).astype(F32).astype(BF16)
+    packed_ref[:, columns : columns + passes] = dot(spread, same, ((0,), (0,))).astype(BF16)
+
+
+def first_sum_body(count, columns, sides, *refs):
+    packed, pooled, out_ref = refs[:sides], refs[sides : 2 * sides], refs[-1]
+    hidden = out_ref.shape[1] - columns
+    passes = pooled[0].shape[0]
+    first = sum(dot(a[:, columns : columns + passes], b[...]) for a, b in zip(packed, pooled))
+    out_ref[:, :hidden] = (ADAPTER_SCALE / count * first).astype(BF16)
+    out_ref[:, hidden:] = sum(a[:, :columns].astype(F32) for a in packed).astype(BF16)
 
 
 def round_sum_body(own_ref, got_ref, *refs):
@@ -229,26 +224,31 @@
     second_ref[...] = total[:, hidden:]
 
 
-def activation_body(start, stop, direction_ref, spread_ref, input_factor_ref, weight_ref, *refs):
+def activation_body(masks, first, member_ref, weight_ref, *refs):
     *before, out_ref, token_ref = refs
+    pieces = [before.pop() for _ in masks][::-1]
     token_ref[...] = jnp.zeros_like(token_ref)
-    for ref in before:
-        out_ref[:, :start] = ref[:, :start]
+    columns = pieces[0].shape[1]
 
     def part(at, size):
-        columns = pl.ds(at, size)
-        value = ADAPTER_SCALE * dot(spread_ref[...], input_factor_ref[:, columns])
-        value += dot(direction_ref[...], weight_ref[columns, :], ((1,), (1,)))
-        out_ref[:, columns] = value.astype(BF16)
-
-    whole = (stop - start) // ROWS
-
-    @pl.loop(0, whole)
+        rows = pl.ds(at, size)
+        if first:
+            value = ADAPTER_SCALE * dot(before[0][...], before[1][:, rows])
+        else:
+            value = before[0][:, rows]
+        for mask, piece in zip(masks, pieces):
+            block = pl.ds(pl.multiple_of((member_ref[0] ^ mask) * columns, LANES), columns)
+            value += dot(piece[...], weight_ref[rows, block], ((1,), (1,)))
+        out_ref[:, rows] = value.astype(out_ref.dtype)
+
+    total = out_ref.shape[1]
+
+    @pl.loop(0, total // ROWS)
     def _(i):
-        part(pl.multiple_of(start + i * ROWS, ROWS), ROWS)
-
-    if whole * ROWS < stop - start:
-        part(start + whole * ROWS, stop - start - whole * ROWS)
+        part(pl.multiple_of(i * ROWS, ROWS), ROWS)
+
+    if total % ROWS:
+        part(total - total % ROWS, total % ROWS)
 
 
 def local(gradient_table, residual_input_rows, act, down_weight, adapter_input_factor, adapter_output_factor, lengths,
@@ -273,12 +273,6 @@
     def swap(x, axis, size, bit):
         return lax.ppermute(x, axis, [(i, i ^ bit) for i in range(size)])
 
-    steps = []
-    bit = 2
-    while bit < members:
-        steps.append(bit)
-        bit *= 2
-
     index = owning_row_index.reshape(1, -1)
     sent, last, my_index = call(
         functools.partial(route_body, passes, capacity),
@@ -296,62 +290,81 @@
     )
     away, grads = call(
         functools.partial(finish_body, devices, owned, capacity),
-        [((passes, width + LANES), F32), ((passes, columns), BF16)], "finish",
+        [((passes, blocks * columns), F32), ((passes, columns), BF16)], "finish",
         member_at, my_index, routed, terms, low, adapter_output_factor,
     )
     away = swap(away, "tensor", members, 1)
-    sums = [((passes, width), F32), ((passes, rank), F32)]
-    total, low, out = call(
-        sum_cores_body, [*sums, ((passes, width + LANES), BF16)], "sum_cores",
-        member_at, terms, low, away, adapter_output_factor,
-    )
+    n = blocks // 2
+    kept, out, pooled = call(
+        functools.partial(sum_cores_body, columns),
+        [((passes, n * columns), F32), ((passes, n * columns), BF16), (pooled.shape, BF16)],
+        "sum_cores", member_at, terms, low, away, adapter_output_factor, pooled,
+    )
+    paired = devices & (devices - 1) == 0
+    far = [swap(pooled, "dp", devices, devices // 2)] if paired else []
+    got = swap(out, "tensor", members, 2 * n)
+    while n > 1:
+        n //= 2
+        kept, out = call(
+            functools.partial(sum_chips_body, columns), [((passes, n * columns), F32), ((passes, n * columns), BF16)],
+            "sum_chips", member_at, kept, got,
+        )
+        got = swap(out, "tensor", members, 2 * n)
+    hidden_rows, stats = call(
+        stats_body, [((passes, columns), F32), ((passes, LANES), F32)], "stats",
+        member_at, kept, got, grads, low, adapter_output_factor, flops=2 * WAIT,
+    )
+    bit = 1
+    while 2 * bit < members:
+        stats = stats + swap(stats, "tensor", members, bit)
+        bit *= 2
+    got = swap(stats, "tensor", members, bit)
+    direction, spread, packed = call(
+        functools.partial(direction_body, count),
+        [((passes, columns), BF16), ((passes, rank), BF16), ((rank, columns + LANES * -(-passes // LANES)), BF16)],
+        "direction", stats, got, hidden_rows, grads, flops=passes * columns * 64,
+    )
+    directions = {0: direction}
+    bit = 2
+    while bit < members:
+        directions.update({k ^ bit: swap(v, "tensor", members, bit) for k, v in list(directions.items())})
+        bit *= 2
+    directions.update({k ^ 1: swap(v, "tensor", members, 1) for k, v in list(directions.items())})
     weight = pltpu.with_memory_space_constraint(down_weight, pltpu.VMEM)
-    for bit in steps:
-        got, got_grads = swap(out, "tensor", members, bit), swap(grads, "tensor", members, bit)
-        joined = 2 * grads.shape[1]
-        last = bit == steps[-1]
-        outs = [((passes, width + joined), BF16)] if last else [(out.shape, BF16), ((passes, joined), BF16)]
-        total, low, out, *more = call(
-            functools.partial(sum_chips_body, last), [*sums, *outs], "sum_chips",
-            total, low, got, grads, got_grads, flops=WAIT,
-        )
-        grads = more[0] if more else None
-    other = swap(out, "tensor", members, 1)
-    direction, spread, packed = call(
-        functools.partial(direction_body, count, blocks),
-        [((passes, model), BF16), ((passes, rank), BF16), ((rank, hidden + columns), BF16)], "direction",
-        member_at, total, low, out, other, adapter_output_factor, pooled, flops=WAIT,
-    )
-    parts = 3
-    ends = [min(hidden, -(-pieces * (i + 1) // parts) * ROWS) for i in range(parts)]
-    token = []
-    activation = []
+    order = list(range(members))
+    todo = [order[:1], order[1:-1], order[-1:]]
+    token, activation = [], []
 
     def activate():
-        start = ends[len(ends) - len(todo) - 1] if len(todo) < parts else 0
-        stop = todo.pop(0)
+        masks = todo.pop(0)
         out, done = call(
-            functools.partial(activation_body, start, stop), [((passes, hidden), BF16), ((8, LANES), F32)], "activation",
-            direction, spread, input_factor, weight, *activation,
-            flops=passes * (stop - start) * model * 2,
+            functools.partial(activation_body, masks, not activation),
+            [((passes, hidden), F32 if todo else BF16), ((8, LANES), F32)], "activation",
+            member_at, weight, *(activation or (spread, input_factor)), *[directions[k] for k in masks],
+            flops=2 * passes * hidden * columns * len(masks),
         )
         activation[:] = [out]
         token[:] = [done]
 
-    todo = list(ends)
     shapes = [((rank, hidden), F32), ((rank, columns), F32)]
-    if devices & (devices - 1) == 0:
+    both = [((rank, hidden + columns), BF16)]
+    first = functools.partial(first_sum_body, count, columns)
+    if paired:
+        got = swap(packed, "dp", devices, devices // 2)
+        activate()
+        (packed,) = call(functools.partial(first, 2), both, "sum_far", packed, got, pooled, *far, *token, keep=(weight,))
         bit = 1
-        while bit < devices:
+        while bit < devices // 2:
             got = swap(packed, "dp", devices, bit)
             bit *= 2
             if todo:
                 activate()
-            if bit < devices:
-                (packed,) = call(round_sum_body, [(packed.shape, BF16)], "sum_pairs", packed, got, *token, keep=(weight,))
+            if bit < devices // 2:
+                (packed,) = call(round_sum_body, both, "sum_pairs", packed, got, *token, keep=(weight,))
             else:
                 sums = call(last_sum_body, shapes, "sum_last", packed, got, *token)
     else:
+        (packed,) = call(functools.partial(first, 1), both, "sum_own", packed, pooled)
         packed = lax.psum(packed.astype(F32), "dp")
         sums = packed[:, :hidden], packed[:, hidden:]
     while todo:

time: 50.7 us -> 49.4 us (0.974)
  waiting for transfers between devices: 15.6 us -> 7.49 us
  starting transfers between devices: 16.1 us -> 21.3 us
  Pallas kernels: 17.8 us -> 19.5 us
    ppermute x7 -> x11, waiting for transfers between devices: 15.6 us -> 7.48 us  [swap(): return lax.ppermute(x, axis, [(i, i ^ bit) for i in range(size)])]
    ppermute x7 -> x11, starting transfers between devices: 8.82 us -> 14.1 us  [swap(): return lax.ppermute(x, axis, [(i, i ^ bit) for i in range(size)])]
    pallas_call x12, Pallas kernels: 17.8 us -> 19.5 us  [call(): pl.pallas_call(run, out_shape=[jax.ShapeDtypeStruct(*s) if isinstance(s,...]
  transfers between devices with their start and end apart: 8 -> 12, of which waited for: 6 -> 5; matrix products, arithmetic and copies ran while one was open for 0% -> 0% of each run, Pallas kernels for 26% -> 33%
where the time goes in v4:
time: 49.4 us; the launch traced here: 49.1 us
  starting transfers between devices  21.3 us (43%)
  Pallas kernels  19.5 us (39%)
  waiting for transfers between devices  7.49 us (15%)
  between operations  0.78 us (2%)
    pallas_call x12, Pallas kernels, call(): pl.pallas_call(run, out_shape=[jax.ShapeDtypeStruct(*s) if isinstance(s,...  19.5 us
    ppermute x11, starting transfers between devices, swap(): return lax.ppermute(x, axis, [(i, i ^ bit) for i in range(size)])  14.1 us
    ppermute x11, waiting for transfers between devices, swap(): return lax.ppermute(x, axis, [(i, i ^ bit) for i in range(size)])  7.48 us
    all_to_all x1, starting transfers between devices, local(): routed = lax.all_to_all(sent, 'dp', 0, 0, tiled=True)  7.26 us
  transfers between devices with their start and end apart: 12, of which 5 were waited for; matrix products, arithmetic and copies ran while one was open for 0% of the time, Pallas kernels for 33%

profile of v4, /device:TPU:0, one launch (start us, length us, event | category | flops | bytes accessed | tf_op | source)
XLA Modules:
  0.0 49.1 jit_solution(14061530162401799028)
XLA Ops:
  0.6 1.9 %route.1 = (bf16[64,1024]{1,0:T(8,128)(2,1)}, s32[64,1]{1,0:T(8,128)S(1)}, s32[64,1]{1,0:T(8,128)S(1)}) custom-call(s32[1]{0:T(128)} %bitcast.1.refs_0_, s32[1,512]{1,0:T(1,128)} %bitcast.12, s32[1,64]{1,0:T(1,128)} %refs_2_.2, bf16[64,1024]{1,0:T(8,128)(2,1)} %refs_3_.2), custom_call_target="tpu_custom_call" | custom-call | bytes 133380 | tf_op jit(solution)/shard_map/route/pallas_call | solution.py:49
  2.5 7.3 %all-to-all-start = ((bf16[8,8,1024]{2,1,0:T(8,128)(2,1)}), bf16[8,8,1024]{2,1,0:T(8,128)(2,1)S(1)}, u32[]{:S(2)}, u32[]{:S(2)}) async-start(bf16[8,8,1024]{2,1,0:T(8,128)(2,1)} %bitcast.4), calls=%async_computation | async-start | bytes 262144 | tf_op jit(solution)/shard_map/all_to_all | solution.py:282
  9.8 7.4 %project.1 = (f32[64,4096]{1,0:T(8,128)S(1)}, bf16[64,1792]{1,0:T(8,128)(2,1)S(1)}, f32[64,16]{1,0:T(8,128)S(1)}) custom-call(s32[1]{0:T(128)} %bitcast.refs_0_, s32[64,1]{1,0:T(8,128)S(1)} %get-tuple-element.27.refs_1_, bf16[64,1024]{1,0:T(8,128)(2,1)} %refs_2_.3, bf16[16,1792]{1,0:T(8,128)(2,1)} %bitcast.10, bf16[1024,1792]{1,0:T(8,128)(2,1)} %refs_4_.2, ...), custom_call_target="tpu_custom_call" | custom-call | flops 939524096 | bytes 18538756 | tf_op jit(solution)/shard_map/project/pallas_call | solution.py:49
  17.2 0.4 finish.1
  17.7 1.9 %collective-permute-done.refs_3_ = f32[64,2048]{1,0:T(8,128)S(1)} collective-permute-done((f32[64,2048]{1,0:T(8,128)S(1)}, f32[64,2048]{1,0:T(8,128)S(1)}, u32[]{:S(2)}, u32[]{:S(2)}) %collective-permute-start) | collective-permute-done | bytes 524320 | tf_op jit(solution)/shard_map/ppermute | solution.py:274
  19.6 0.2 sum_cores.1
  19.8 1.6 %collective-permute-start.1 = (bf16[64,1024]{1,0:T(8,128)(2,1)S(1)}, bf16[64,1024]{1,0:T(8,128)(2,1)S(1)}, u32[]{:S(2)}, u32[]{:S(2)}) collective-permute-start(bf16[64,1024]{1,0:T(8,128)(2,1)S(1)} %get-tuple-element.35), channel_id=1, source_target_pairs={{0,2},{1,3},{2,0},{3,1},{4,6},{5,7},{6,4},{7,5},{8,10},{9,11},{10,... | collective-permute-start | bytes 393224 | tf_op jit(solution)/shard_map/ppermute | solution.py:274
  21.4 2.9 %collective-permute-start.8 = (bf16[64,1792]{1,0:T(8,128)(2,1)S(1)}, bf16[64,1792]{1,0:T(8,128)(2,1)S(1)}, u32[]{:S(2)}, u32[]{:S(2)}) collective-permute-start(bf16[64,1792]{1,0:T(8,128)(2,1)S(1)} %get-tuple-element.45.refs_2_), channel_id=1, source_target_pairs={{0,16},{4,20},{8,24},{12,28},{16,0},{20,4},{24,8},{28,12},{1,17},{... | collective-permute-start | bytes 688136 | tf_op jit(solution)/shard_map/ppermute | solution.py:274
  24.3 1.1 %collective-permute-done.1.refs_2_ = bf16[64,1024]{1,0:T(8,128)(2,1)S(1)} collective-permute-done((bf16[64,1024]{1,0:T(8,128)(2,1)S(1)}, bf16[64,1024]{1,0:T(8,128)(2,1)S(1)}, u32[]{:S(2)}, u32[]{:S(2)}) %collective-permute-start.1) | collective-permute-done | bytes 131104 | tf_op jit(solution)/shard_map/ppermute | solution.py:274
  25.4 0.3 stats.1
  25.9 1.2 %collective-permute-done.2 = f32[64,128]{1,0:T(8,128)S(1)} collective-permute-done((f32[64,128]{1,0:T(8,128)S(1)}, f32[64,128]{1,0:T(8,128)S(1)}, u32[]{:S(2)}, u32[]{:S(2)}) %collective-permute-start.2) | collective-permute-done | bytes 32800 | tf_op jit(solution)/shard_map/ppermute | solution.py:274
  27.1 1.5 %collective-permute-start.3 = (f32[64,128]{1,0:T(8,128)S(1)}, f32[64,128]{1,0:T(8,128)S(1)}, u32[]{:S(2)}, u32[]{:S(2)}) collective-permute-start(f32[64,128]{1,0:T(8,128)S(1)} %add.3.refs_0_), channel_id=1, source_target_pairs={{0,2},{1,3},{2,0},{3,1},{4,6},{5,7},{6,4},{7,5},{8,10},{9,11},{10,... | collective-permute-start | bytes 98312 | tf_op jit(solution)/shard_map/ppermute | solution.py:274
  28.6 2.4 %collective-permute-done.3.refs_1_ = f32[64,128]{1,0:T(8,128)S(1)} collective-permute-done((f32[64,128]{1,0:T(8,128)S(1)}, f32[64,128]{1,0:T(8,128)S(1)}, u32[]{:S(2)}, u32[]{:S(2)}) %collective-permute-start.3) | collective-permute-done | bytes 32800 | tf_op jit(solution)/shard_map/ppermute | solution.py:274
  31.0 0.4 direction.1
  31.4 1.6 %collective-permute-start.5 = (bf16[64,1024]{1,0:T(8,128)(2,1)S(1)}, bf16[64,1024]{1,0:T(8,128)(2,1)S(1)}, u32[]{:S(2)}, u32[]{:S(2)}) collective-permute-start(bf16[64,1024]{1,0:T(8,128)(2,1)S(1)} %get-tuple-element.40.refs_4_), channel_id=1, source_target_pairs={{0,2},{1,3},{2,0},{3,1},{4,6},{5,7},{6,4},{7,5},{8,10},{9,11},{10,... | collective-permute-start | bytes 393224 | tf_op jit(solution)/shard_map/ppermute | solution.py:274
  33.0 2.9 %collective-permute-start.7 = (bf16[16,1152]{1,0:T(8,128)(2,1)S(1)}, bf16[16,1152]{1,0:T(8,128)(2,1)S(1)}, u32[]{:S(2)}, u32[]{:S(2)}) collective-permute-start(bf16[16,1152]{1,0:T(8,128)(2,1)S(1)} %get-tuple-element.44.refs_0_), channel_id=1, source_target_pairs={{0,16},{4,20},{8,24},{12,28},{16,0},{20,4},{24,8},{28,12},{1,17},{... | collective-permute-start | bytes 110600 | tf_op jit(solution)/shard_map/ppermute | solution.py:274
  35.9 2.1 %activation.3 = (f32[64,1792]{1,0:T(8,128)S(1)}, f32[8,128]{1,0:T(8,128)S(1)}) custom-call(s32[1]{0:T(128)} %bitcast.refs_0_, bf16[1792,4096]{1,0:T(8,128)(2,1)S(1)} %bitcast.8, bf16[64,16]{1,0:T(8,128)(2,1)S(1)} %get-tuple-element.39.refs_2_, bf16[16,1792]{1,0:T(8,128)(2,1)S(1)} %bitcast.11, bf16[64,1024]{1,0:T(8,128)(2,1)S(1)} %get-tuple-element.40.refs_4_), custom_call_target="tpu_custom_call" | custom-call | flops 234881024 | bytes 14870532 | tf_op jit(solution)/shard_map/activation/pallas_call | solution.py:49
  38.1 0.2 sum_far.1.refs_0_
  38.2 1.9 %collective-permute-start.9 = (bf16[16,2816]{1,0:T(8,128)(2,1)S(1)}, bf16[16,2816]{1,0:T(8,128)(2,1)S(1)}, u32[]{:S(2)}, u32[]{:S(2)}) collective-permute-start(bf16[16,2816]{1,0:T(8,128)(2,1)S(1)} %sum_far.1.refs_0_), channel_id=1, source_target_pairs={{0,4},{4,0},{8,12},{12,8},{16,20},{20,16},{24,28},{28,24},{1,5},{5... | collective-permute-start | bytes 270344 | tf_op jit(solution)/shard_map/ppermute | solution.py:274
  40.1 3.2 %activation.4 = (f32[64,1792]{1,0:T(8,128)S(1)}, f32[8,128]{1,0:T(8,128)S(1)}) custom-call(s32[1]{0:T(128)} %bitcast.refs_0_, bf16[1792,4096]{1,0:T(8,128)(2,1)S(1)} %bitcast.8, f32[64,1792]{1,0:T(8,128)S(1)} %get-tuple-element.41.refs_2_, bf16[64,1024]{1,0:T(8,128)(2,1)S(1)} %collective-permute-done.4.refs_3_, ...), custom_call_target="tpu_custom_call" | custom-call | flops 469762048 | bytes 15400964 | tf_op jit(solution)/shard_map/activation/pallas_call | solution.py:49
  43.3 1.5 %collective-permute-start.10 = (bf16[16,2816]{1,0:T(8,128)(2,1)S(1)}, bf16[16,2816]{1,0:T(8,128)(2,1)S(1)}, u32[]{:S(2)}, u32[]{:S(2)}) collective-permute-start(bf16[16,2816]{1,0:T(8,128)(2,1)S(1)} %sum_pairs.1.refs_0_), channel_id=1, source_target_pairs={{0,8},{4,12},{8,0},{12,4},{16,24},{20,28},{24,16},{28,20},{1,9},{5... | collective-permute-start | bytes 270344 | tf_op jit(solution)/shard_map/ppermute | solution.py:274
  44.9 2.7 %activation.5 = (bf16[64,1792]{1,0:T(8,128)(2,1)}, f32[8,128]{1,0:T(8,128)S(1)}) custom-call(s32[1]{0:T(128)} %bitcast.refs_0_, bf16[1792,4096]{1,0:T(8,128)(2,1)S(1)} %bitcast.8, f32[64,1792]{1,0:T(8,128)S(1)} %get-tuple-element.42.refs_2_, bf16[64,1024]{1,0:T(8,128)(2,1)S(1)} %collective-permute-done.6.refs_3_), custom_call_target="tpu_custom_call" | custom-call | flops 234881024 | bytes 15269892 | tf_op jit(solution)/shard_map/activation/pallas_call | solution.py:49
  47.6 0.8 %collective-permute-done.10.refs_1_ = bf16[16,2816]{1,0:T(8,128)(2,1)S(1)} collective-permute-done((bf16[16,2816]{1,0:T(8,128)(2,1)S(1)}, bf16[16,2816]{1,0:T(8,128)(2,1)S(1)}, u32[]{:S(2)}, u32[]{:S(2)}) %collective-permute-start.10) | collective-permute-done | bytes 90144 | tf_op jit(solution)/shard_map/ppermute | solution.py:274
  48.4 0.7 %sum_last.1 = (f32[16,1792]{1,0:T(8,128)}, f32[16,1024]{1,0:T(8,128)}) custom-call(bf16[16,2816]{1,0:T(8,128)(2,1)S(1)} %sum_pairs.1.refs_0_, bf16[16,2816]{1,0:T(8,128)(2,1)S(1)} %collective-permute-done.10.refs_1_, f32[8,128]{1,0:T(8,128)S(1)} %get-tuple-element.48.refs_2_), custom_call_target="tpu_custom_call" | custom-call | bytes 184320 | tf_op jit(solution)/shard_map/sum_last/pallas_call | solution.py:49
  (26 shorter events, 0.3 us)
Async XLA Ops:
  0.6 16.6 %copy-start = (bf16[16,4096]{1,0:T(8,128)(2,1)S(1)}, bf16[16,4096]{1,0:T(8,128)(2,1)}, u32[]{:S(2)}) copy-start(bf16[16,4096]{1,0:T(8,128)(2,1)} %refs_5_.6) | copy-start | bytes 393220
  2.5 14.6 %all-to-all-start = ((bf16[8,8,1024]{2,1,0:T(8,128)(2,1)}), bf16[8,8,1024]{2,1,0:T(8,128)(2,1)S(1)}, u32[]{:S(2)}, u32[]{:S(2)}) async-start(bf16[8,8,1024]{2,1,0:T(8,128)(2,1)} %bitcast.4), calls=%async_computation | async-start | bytes 262144 | tf_op jit(solution)/shard_map/all_to_all | solution.py:282
  17.6 2.0 %collective-permute-start = (f32[64,2048]{1,0:T(8,128)S(1)}, f32[64,2048]{1,0:T(8,128)S(1)}, u32[]{:S(2)}, u32[]{:S(2)}) collective-permute-start(f32[64,2048]{1,0:T(8,128)S(1)} %get-tuple-element.32), channel_id=1, source_target_pairs={{0,1},{1,0},{2,3},{3,2},{4,5},{5,4},{6,7},{7,6},{8,9},{9,8},{10,11... | collective-permute-start | bytes 1572872 | tf_op jit(solution)/shard_map/ppermute | solution.py:274
  19.6 16.3 %slice-start = ((s8[14680064]{0:T(1024)(128)(4,1)}), s8[4194304]{0:T(1024)(128)(4,1)S(1)}, s32[]{:S(2)}) async-start(s8[14680064]{0:T(1024)(128)(4,1)} %bitcast.7), calls=%async_computation.1 | async-start | bytes 8388608
  19.8 5.6 %collective-permute-start.1 = (bf16[64,1024]{1,0:T(8,128)(2,1)S(1)}, bf16[64,1024]{1,0:T(8,128)(2,1)S(1)}, u32[]{:S(2)}, u32[]{:S(2)}) collective-permute-start(bf16[64,1024]{1,0:T(8,128)(2,1)S(1)} %get-tuple-element.35), channel_id=1, source_target_pairs={{0,2},{1,3},{2,0},{3,1},{4,6},{5,7},{6,4},{7,5},{8,10},{9,11},{10,... | collective-permute-start | bytes 393224 | tf_op jit(solution)/shard_map/ppermute | solution.py:274
  21.4 16.6 %collective-permute-start.8 = (bf16[64,1792]{1,0:T(8,128)(2,1)S(1)}, bf16[64,1792]{1,0:T(8,128)(2,1)S(1)}, u32[]{:S(2)}, u32[]{:S(2)}) collective-permute-start(bf16[64,1792]{1,0:T(8,128)(2,1)S(1)} %get-tuple-element.45.refs_2_), channel_id=1, source_target_pairs={{0,16},{4,20},{8,24},{12,28},{16,0},{20,4},{24,8},{28,12},{1,17},{... | collective-permute-start | bytes 688136 | tf_op jit(solution)/shard_map/ppermute | solution.py:274
  25.4 10.5 %slice-start.1 = ((s8[14680064]{0:T(1024)(128)(4,1)}), s8[4194304]{0:T(1024)(128)(4,1)S(1)}, s32[]{:S(2)}) async-start(s8[14680064]{0:T(1024)(128)(4,1)} %bitcast.7), calls=%async_computation.2 | async-start | bytes 8388608
  25.4 10.5 %slice-start.2 = ((s8[14680064]{0:T(1024)(128)(4,1)}), s8[4194304]{0:T(1024)(128)(4,1)S(1)}, s32[]{:S(2)}) async-start(s8[14680064]{0:T(1024)(128)(4,1)} %bitcast.7), calls=%async_computation.3 | async-start | bytes 8388608
  25.4 10.5 %slice-start.3 = ((s8[14680064]{0:T(1024)(128)(4,1)}), s8[2097152]{0:T(1024)(128)(4,1)S(1)}, s32[]{:S(2)}) async-start(s8[14680064]{0:T(1024)(128)(4,1)} %bitcast.7), calls=%async_computation.4 | async-start | bytes 4194304
  25.4 10.5 %copy-start.1 = (bf16[1792,16]{0,1:T(8,128)(2,1)S(1)}, bf16[1792,16]{0,1:T(8,128)(2,1)}, u32[]{:S(2)}) copy-start(bf16[1792,16]{0,1:T(8,128)(2,1)} %param.12) | copy-start | bytes 172036
  25.8 1.3 %collective-permute-start.2 = (f32[64,128]{1,0:T(8,128)S(1)}, f32[64,128]{1,0:T(8,128)S(1)}, u32[]{:S(2)}, u32[]{:S(2)}) collective-permute-start(f32[64,128]{1,0:T(8,128)S(1)} %get-tuple-element.37), channel_id=1, source_target_pairs={{0,1},{1,0},{2,3},{3,2},{4,5},{5,4},{6,7},{7,6},{8,9},{9,8},{10,11... | collective-permute-start | bytes 98312 | tf_op jit(solution)/shard_map/ppermute | solution.py:274
  27.1 3.9 %collective-permute-start.3 = (f32[64,128]{1,0:T(8,128)S(1)}, f32[64,128]{1,0:T(8,128)S(1)}, u32[]{:S(2)}, u32[]{:S(2)}) collective-permute-start(f32[64,128]{1,0:T(8,128)S(1)} %add.3.refs_0_), channel_id=1, source_target_pairs={{0,2},{1,3},{2,0},{3,1},{4,6},{5,7},{6,4},{7,5},{8,10},{9,11},{10,... | collective-permute-start | bytes 98312 | tf_op jit(solution)/shard_map/ppermute | solution.py:274
  31.4 8.7 %collective-permute-start.5 = (bf16[64,1024]{1,0:T(8,128)(2,1)S(1)}, bf16[64,1024]{1,0:T(8,128)(2,1)S(1)}, u32[]{:S(2)}, u32[]{:S(2)}) collective-permute-start(bf16[64,1024]{1,0:T(8,128)(2,1)S(1)} %get-tuple-element.40.refs_4_), channel_id=1, source_target_pairs={{0,2},{1,3},{2,0},{3,1},{4,6},{5,7},{6,4},{7,5},{8,10},{9,11},{10,... | collective-permute-start | bytes 393224 | tf_op jit(solution)/shard_map/ppermute | solution.py:274
  33.0 7.1 %collective-permute-start.4 = (bf16[64,1024]{1,0:T(8,128)(2,1)S(1)}, bf16[64,1024]{1,0:T(8,128)(2,1)S(1)}, u32[]{:S(2)}, u32[]{:S(2)}) collective-permute-start(bf16[64,1024]{1,0:T(8,128)(2,1)S(1)} %get-tuple-element.40.refs_4_), channel_id=1, source_target_pairs={{0,1},{1,0},{2,3},{3,2},{4,5},{5,4},{6,7},{7,6},{8,9},{9,8},{10,11... | collective-permute-start | bytes 393224 | tf_op jit(solution)/shard_map/ppermute | solution.py:274
  33.0 5.1 %collective-permute-start.7 = (bf16[16,1152]{1,0:T(8,128)(2,1)S(1)}, bf16[16,1152]{1,0:T(8,128)(2,1)S(1)}, u32[]{:S(2)}, u32[]{:S(2)}) collective-permute-start(bf16[16,1152]{1,0:T(8,128)(2,1)S(1)} %get-tuple-element.44.refs_0_), channel_id=1, source_target_pairs={{0,16},{4,20},{8,24},{12,28},{16,0},{20,4},{24,8},{28,12},{1,17},{... | collective-permute-start | bytes 110600 | tf_op jit(solution)/shard_map/ppermute | solution.py:274
  38.2 5.1 %collective-permute-start.9 = (bf16[16,2816]{1,0:T(8,128)(2,1)S(1)}, bf16[16,2816]{1,0:T(8,128)(2,1)S(1)}, u32[]{:S(2)}, u32[]{:S(2)}) collective-permute-start(bf16[16,2816]{1,0:T(8,128)(2,1)S(1)} %sum_far.1.refs_0_), channel_id=1, source_target_pairs={{0,4},{4,0},{8,12},{12,8},{16,20},{20,16},{24,28},{28,24},{1,5},{5... | collective-permute-start | bytes 270344 | tf_op jit(solution)/shard_map/ppermute | solution.py:274
  40.1 4.8 %collective-permute-start.6 = (bf16[64,1024]{1,0:T(8,128)(2,1)S(1)}, bf16[64,1024]{1,0:T(8,128)(2,1)S(1)}, u32[]{:S(2)}, u32[]{:S(2)}) collective-permute-start(bf16[64,1024]{1,0:T(8,128)(2,1)S(1)} %collective-permute-done.5.refs_4_), channel_id=1, source_target_pairs={{0,1},{1,0},{2,3},{3,2},{4,5},{5,4},{6,7},{7,6},{8,9},{9,8},{10,11... | collective-permute-start | bytes 393224 | tf_op jit(solution)/shard_map/ppermute | solution.py:274
  43.3 5.1 %collective-permute-start.10 = (bf16[16,2816]{1,0:T(8,128)(2,1)S(1)}, bf16[16,2816]{1,0:T(8,128)(2,1)S(1)}, u32[]{:S(2)}, u32[]{:S(2)}) collective-permute-start(bf16[16,2816]{1,0:T(8,128)(2,1)S(1)} %sum_pairs.1.refs_0_), channel_id=1, source_target_pairs={{0,8},{4,12},{8,0},{12,4},{16,24},{20,28},{24,16},{28,20},{1,9},{5... | collective-permute-start | bytes 270344 | tf_op jit(solution)/shard_map/ppermute | solution.py:274

commit v5 on v4

--- a/solution.py
+++ b/solution.py
@@ -12,6 +12,7 @@
 F32, BF16 = jnp.float32, jnp.bfloat16
 LANES = 128
 ROWS = 256
+STEP = 512
 WAIT = 5_000_000_000
 VMEM = pl.BlockSpec(memory_space=pltpu.VMEM)
 SMEM = pl.BlockSpec(memory_space=pltpu.SMEM)
@@ -71,41 +72,57 @@
     return jnp.sum(jnp.where(iota((n, n), 0) == iota((n, n), 1), column, 0), axis=0, keepdims=True)
 
 
-def route_body(passes, capacity, inputs, out_ref, last_ref, mine_ref):
+def apart(device, other):
+    return device % 2 ^ other % 2, (device // 2) ^ (other // 2)
+
+
+def route_body(passes, capacity, paired, inputs, *refs):
     (device_ref,), (index_ref, lengths_ref, table_ref), copies = inputs
-    rows, slots = table_ref.shape[0], out_ref.shape[0]
+    *out_refs, last_ref, mine_ref = refs
+    rows, slots = table_ref.shape[0], sum(ref.shape[0] for ref in out_refs)
+    device = device_ref[0]
     copies[0].wait()
     index = index_ref[...]
     total = index.shape[1]
-    mine = device_ref[0] * rows + iota((rows, total), 0)
+    mine = device * rows + iota((rows, total), 0)
     packed = iota((rows, total), 1) // passes
     dest = jnp.sum(jnp.where(index == mine, packed, 0), axis=1, keepdims=True)
     earlier = (dest == turned(dest)) & (iota((rows, rows), 1) < iota((rows, rows), 0))
     rank = jnp.sum(earlier.astype(jnp.int32), axis=1, keepdims=True)
-    slot = turned(dest * capacity + rank)
+    place = dest
+    if paired:
+        low, high = apart(dest, device)
+        place = 2 * high + low
+    slot = turned(place * capacity + rank)
     picker = (iota((slots, rows), 0) == slot).astype(F32).astype(BF16)
-    own = iota((passes, total), 1) == device_ref[0] * passes + iota((passes, total), 0)
+    own = iota((passes, total), 1) == device * passes + iota((passes, total), 0)
     mine_ref[...] = jnp.sum(jnp.where(own, index, 0), axis=1, keepdims=True)
     copies[1].wait()
     upto = jnp.where(iota((passes, passes), 1) <= iota((passes, passes), 0), lengths_ref[...], 0)
     last_ref[...] = jnp.sum(upto, axis=1, keepdims=True) - 1
     copies[2].wait()
-    out_ref[...] = dot(picker, table_ref[...]).astype(BF16)
-
-
-def slot_picker(index_ref, owners, owned, capacity):
-    column = index_ref[...]
-    n = column.shape[0]
-    row = turned(column)
-    owner = column // owned
-    earlier = (owner == row // owned) & (row < column)
-    slot = owner * capacity + jnp.sum(earlier.astype(jnp.int32), axis=1, keepdims=True)
-    return (slot == iota((n, owners * capacity), 1)).astype(F32).astype(BF16)
-
-
-def project_body(inputs, out_ref, pooled_ref, low_ref, act_held, weight_held, act_sems, sems):
-    (member_ref, last_ref, act_ref, weight_ref), (residual_ref, input_factor_ref), copies = inputs
-    hidden = weight_held.shape[0]
+    value = dot(picker, table_ref[...]).astype(BF16)
+    size = slots // len(out_refs)
+    for i, ref in enumerate(out_refs):
+        ref[...] = value[i * size : (i + 1) * size]
+
+
+def meet_body(capacity, away_ref, *refs):
+    *blocks, out_ref, keep_ref, send_ref = refs
+    out_ref[...] = away_ref[...].astype(BF16)
+    rows = jnp.concatenate([ref[...] for ref in blocks], axis=0)
+    n, total = keep_ref.shape[0], rows.shape[0]
+    to, at = iota((n, total), 0), iota((n, total), 1)
+    for low, ref in ((0, keep_ref), (1, send_ref)):
+        picker = (at == (2 * (to // capacity) + low) * capacity + to % capacity).astype(F32).astype(BF16)
+        ref[...] = dot(picker, rows).astype(BF16)
+
+
+def project_body(inputs, kept_ref, away_ref, pooled_ref, low_ref, act_held, weight_held, act_sems, sems):
+    (member_ref, last_ref, act_ref, weight_ref), (input_factor_ref, factor_ref, residual_ref), copies = inputs
+    member = member_ref[0]
+    columns = residual_ref.shape[1]
+    hidden = act_ref.shape[1]
     pieces = []
     for i, (at, size) in enumerate(cuts(hidden, ROWS)):
         piece = slice(at, at + size)
@@ -115,49 +132,64 @@
         copy.start()
         pieces.append((piece, act_copy, copy))
     picker = (last_ref[...] == iota((last_ref.shape[0], act_ref.shape[0]), 1)).astype(F32).astype(BF16)
+
+    def places():
+        for ref, core in ((away_ref, 1 - member % 2), (kept_ref, member % 2)):
+            for j in range(ref.shape[1] // columns):
+                start = pl.multiple_of((2 * j + core) * columns, LANES)
+                yield ref, slice(j * columns, (j + 1) * columns), pl.ds(start, columns)
+
     for piece, act_copy, copy in pieces:
         act_copy.wait()
         pooled = dot(picker, act_held[:, piece]).astype(BF16)
         pooled_ref[:, piece] = pooled
         copy.wait()
-        value = dot(pooled, weight_held[piece, :])
-        if piece.start == 0:
-            out_ref[...] = value
-        else:
-            out_ref[...] += value
+        for ref, to, at in places():
+            value = dot(pooled, weight_held[piece, at])
+            if piece.start == 0:
+                ref[:, to] = value
+            else:
+                ref[:, to] += value
     for copy in copies:
         copy.wait()
-    low_ref[...] = dot(pooled_ref[...], input_factor_ref[...], ((1,), (1,)))
-    columns = residual_ref.shape[1]
-    own = pl.ds(pl.multiple_of(member_ref[0] * columns, LANES), columns)
-    out_ref[:, own] += residual_ref[...].astype(F32)
-
-
-def term_of(block, columns, parts_ref, low_ref, factor_ref):
-    at = pl.ds(pl.multiple_of(block * columns, LANES), columns)
-    return parts_ref[:, at] + ADAPTER_SCALE * dot(low_ref[...].astype(BF16), factor_ref[:, at])
-
-
-def finish_body(owners, owned, capacity, member_ref, index_ref, routed_ref, parts_ref, low_ref, factor_ref, away_ref,
-                grads_ref):
-    columns = grads_ref.shape[1]
-    for j in range(away_ref.shape[1] // columns):
-        block = 2 * j + 1 - member_ref[0] % 2
-        away_ref[:, j * columns : (j + 1) * columns] = term_of(block, columns, parts_ref, low_ref, factor_ref)
-    grads_ref[...] = dot(slot_picker(index_ref, owners, owned, capacity), routed_ref[...]).astype(BF16)
-
-
-def sum_cores_body(columns, member_ref, parts_ref, low_ref, away_ref, factor_ref, pooled_ref, keep_ref, send_ref,
-                   pooled_out_ref):
+    low = dot(pooled_ref[...], input_factor_ref[...], ((1,), (1,)))
+    low_ref[...] = low
+    for ref, to, at in places():
+        ref[:, to] += ADAPTER_SCALE * dot(low.astype(BF16), factor_ref[:, at])
+    own = pl.ds(pl.multiple_of(member // 2 * columns, LANES), columns)
+    kept_ref[:, own] += residual_ref[...].astype(F32)
+
+
+def round_body(away_ref, out_ref):
+    out_ref[...] = away_ref[...].astype(BF16)
+
+
+def grads_body(owned, capacity, device_ref, index_ref, *refs):
+    *parts, grads_ref = refs
+    column = index_ref[...]
+    row = turned(column)
+    owner = column // owned
+    earlier = (owner == row // owned) & (row < column)
+    rank = jnp.sum(earlier.astype(jnp.int32), axis=1, keepdims=True)
+    slots = parts[0].shape[0]
+    low = jnp.zeros_like(owner)
+    place = owner
+    if len(parts) == 2:
+        low, place = apart(owner, device_ref[0])
+    total = 0
+    for i, part in enumerate(parts):
+        picker = (low == i) & (place * capacity + rank == iota((column.shape[0], slots), 1))
+        total += dot(picker.astype(F32).astype(BF16), part[...])
+    grads_ref[...] = total.astype(BF16)
+
+
+def sum_cores_body(columns, member_ref, kept_ref, away_ref, pooled_ref, keep_ref, send_ref, pooled_out_ref):
     pooled_out_ref[...] = pooled_ref[...]
-    member = member_ref[0]
     n = keep_ref.shape[1] // columns
-    side = member // 2 // n % 2
-    for i in range(n):
-        for ref, j in ((keep_ref, side * n + i), (send_ref, (1 - side) * n + i)):
-            value = term_of(2 * j + member % 2, columns, parts_ref, low_ref, factor_ref)
-            value += away_ref[:, pl.ds(pl.multiple_of(j * columns, LANES), columns)]
-            ref[:, i * columns : (i + 1) * columns] = value.astype(ref.dtype)
+    side = member_ref[0] // 2 // n % 2
+    for ref, half in ((keep_ref, side), (send_ref, 1 - side)):
+        at = pl.ds(pl.multiple_of(half * n * columns, LANES), n * columns)
+        ref[...] = (kept_ref[:, at] + away_ref[:, at].astype(F32)).astype(ref.dtype)
 
 
 def sum_chips_body(columns, member_ref, kept_ref, got_ref, keep_ref, send_ref):
@@ -274,33 +306,44 @@
         return lax.ppermute(x, axis, [(i, i ^ bit) for i in range(size)])
 
     index = owning_row_index.reshape(1, -1)
-    sent, last, my_index = call(
-        functools.partial(route_body, passes, capacity),
-        [((slots, columns), BF16), ((passes, 1), jnp.int32), ((passes, 1), jnp.int32)], "route",
+    paired = devices & (devices - 1) == 0
+    groups = devices // 2 if paired else 1
+    *sent, last, my_index = call(
+        functools.partial(route_body, passes, capacity, paired),
+        [((slots // groups, columns), BF16)] * groups + [((passes, 1), jnp.int32)] * 2, "route",
         dp_at, near=(index, lengths, gradient_table),
     )
-    routed = lax.all_to_all(sent, "dp", 0, 0, tiled=True)
-    pieces = len(cuts(hidden, ROWS))
-    terms, pooled, low = call(
-        project_body, [((passes, model), F32), ((passes, hidden), BF16), ((passes, rank), F32)], "project",
-        member_at, last, near=(residual_input_rows, input_factor), far=(act, down_weight),
+    if paired:
+        came = [sent[0]] + [swap(sent[k], "dp", devices, 2 * k) for k in range(1, groups)]
+    else:
+        came = [lax.all_to_all(sent[0], "dp", 0, 0, tiled=True)]
+    halves = (passes, blocks * columns)
+    kept, away, pooled, low = call(
+        project_body, [(halves, F32), (halves, F32), ((passes, hidden), BF16), ((passes, rank), F32)], "project",
+        member_at, last, near=(input_factor, adapter_output_factor, residual_input_rows), far=(act, down_weight),
         scratch=[pltpu.VMEM(act.shape, BF16), pltpu.VMEM(down_weight.shape, BF16)]
-        + [pltpu.SemaphoreType.DMA((pieces,))] * 2,
+        + [pltpu.SemaphoreType.DMA((len(cuts(hidden, ROWS)),))] * 2,
         flops=2 * passes * hidden * model,
     )
-    away, grads = call(
-        functools.partial(finish_body, devices, owned, capacity),
-        [((passes, blocks * columns), F32), ((passes, columns), BF16)], "finish",
-        member_at, my_index, routed, terms, low, adapter_output_factor,
+    if paired:
+        half = ((slots // 2, columns), BF16)
+        away, mine, other = call(
+            functools.partial(meet_body, capacity), [(halves, BF16), half, half], "meet", away, *came
+        )
+        came = [mine, swap(other, "dp", devices, 1)]
+    else:
+        (away,) = call(round_body, [(halves, BF16)], "round", away)
+    (grads,) = call(
+        functools.partial(grads_body, owned, capacity), [((passes, columns), BF16)], "grads", dp_at, my_index, *came,
+        flops=2 * WAIT,
     )
     away = swap(away, "tensor", members, 1)
     n = blocks // 2
     kept, out, pooled = call(
         functools.partial(sum_cores_body, columns),
         [((passes, n * columns), F32), ((passes, n * columns), BF16), (pooled.shape, BF16)],
-        "sum_cores", member_at, terms, low, away, adapter_output_factor, pooled,
-    )
-    paired = devices & (devices - 1) == 0
+        "sum_cores", member_at, kept, away, pooled,
+    )
     far = [swap(pooled, "dp", devices, devices // 2)] if paired else []
     got = swap(out, "tensor", members, 2 * n)
     while n > 1:
@@ -312,7 +355,7 @@
         got = swap(out, "tensor", members, 2 * n)
     hidden_rows, stats = call(
         stats_body, [((passes, columns), F32), ((passes, LANES), F32)], "stats",
-        member_at, kept, got, grads, low, adapter_output_factor, flops=2 * WAIT,
+        member_at, kept, got, grads, low, adapter_output_factor,
     )
     bit = 1
     while 2 * bit < members:

time: 49.4 us -> 46.3 us (0.937)
  starting transfers between devices: 21.3 us -> 18.8 us
    all_to_all x1 -> x0, starting transfers between devices: 7.26 us -> none  [local(): routed = lax.all_to_all(sent, 'dp', 0, 0, tiled=True)]
    ppermute x11 -> x15, starting transfers between devices: 14.1 us -> 18.8 us  [swap(): return lax.ppermute(x, axis, [(i, i ^ bit) for i in range(size)])]
    pallas_call x12 -> x13, Pallas kernels: 19.5 us -> 19.2 us  [call(): pl.pallas_call(run, out_shape=[jax.ShapeDtypeStruct(*s) if isinstance(s,...]
    ppermute x11 -> x15, waiting for transfers between devices: 7.48 us -> 7.25 us  [swap(): return lax.ppermute(x, axis, [(i, i ^ bit) for i in range(size)])]
  transfers between devices with their start and end apart: 12 -> 15, of which waited for: 5 -> 5; matrix products, arithmetic and copies ran while one was open for 0% -> 0% of each run, Pallas kernels for 33% -> 37%
where the time goes in v5:
time: 46.3 us; the launch traced here: 46.1 us
  Pallas kernels  19.2 us (41%)
  starting transfers between devices  18.8 us (41%)
  waiting for transfers between devices  7.25 us (16%)
  between operations  0.8 us (2%)
    pallas_call x13, Pallas kernels, call(): pl.pallas_call(run, out_shape=[jax.ShapeDtypeStruct(*s) if isinstance(s,...  19.2 us
    ppermute x15, starting transfers between devices, swap(): return lax.ppermute(x, axis, [(i, i ^ bit) for i in range(size)])  18.8 us
    ppermute x15, waiting for transfers between devices, swap(): return lax.ppermute(x, axis, [(i, i ^ bit) for i in range(size)])  7.25 us
  transfers between devices with their start and end apart: 15, of which 5 were waited for; matrix products, arithmetic and copies ran while one was open for 0% of the time, Pallas kernels for 37%

profile of v5, /device:TPU:0, one launch (start us, length us, event | category | flops | bytes accessed | tf_op | source)
XLA Modules:
  0.0 46.1 jit_solution(13296940317842318429)
XLA Ops:
  0.6 1.2 %route.1 = (bf16[16,1024]{1,0:T(8,128)(2,1)S(1)}, bf16[16,1024]{1,0:T(8,128)(2,1)S(1)}, bf16[16,1024]{1,0:T(8,128)(2,1)S(1)}, bf16[16,1024]{1,0:T(8,128)(2,1)S(1...) custom-call(s32[1]{0:T(128)} %bitcast.1.refs_0_, s32[1,512]{1,0:T(1,128)} %bitcast.9, s32[1,64]{1,0:T(1,128)} %refs_2_.1, ...), custom_call_target="tpu_custom_call" | custom-call | bytes 133380 | tf_op jit(solution)/shard_map/route/pallas_call | solution.py:50
  1.8 3.1 %collective-permute-start = (bf16[16,1024]{1,0:T(8,128)(2,1)S(1)}, bf16[16,1024]{1,0:T(8,128)(2,1)S(1)}, u32[]{:S(2)}, u32[]{:S(2)}) collective-permute-start(bf16[16,1024]{1,0:T(8,128)(2,1)S(1)} %get-tuple-element.36), channel_id=1, source_target_pairs={{0,8},{4,12},{8,0},{12,4},{16,24},{20,28},{24,16},{28,20},{1,9},{5... | collective-permute-start | bytes 98312 | tf_op jit(solution)/shard_map/ppermute | solution.py:306
  4.9 2.6 %collective-permute-start.1 = (bf16[16,1024]{1,0:T(8,128)(2,1)S(1)}, bf16[16,1024]{1,0:T(8,128)(2,1)S(1)}, u32[]{:S(2)}, u32[]{:S(2)}) collective-permute-start(bf16[16,1024]{1,0:T(8,128)(2,1)S(1)} %get-tuple-element.37), channel_id=1, source_target_pairs={{0,16},{4,20},{8,24},{12,28},{16,0},{20,4},{24,8},{28,12},{1,17},{... | collective-permute-start | bytes 98312 | tf_op jit(solution)/shard_map/ppermute | solution.py:306
  7.5 7.7 %project.1 = (f32[64,2048]{1,0:T(8,128)S(1)}, f32[64,2048]{1,0:T(8,128)S(1)}, bf16[64,1792]{1,0:T(8,128)(2,1)S(1)}, f32[64,16]{1,0:T(8,128)S(1)}) custom-call(s32[1]{0:T(128)} %bitcast.refs_0_, s32[64,1]{1,0:T(8,128)S(1)} %get-tuple-element.32.refs_1_, bf16[16,1792]{1,0:T(8,128)(2,1)} %bitcast.7, bf16[16,4096]{1,0:T(8,128)(2,1)} %refs_5_.4, ...), custom_call_target="tpu_custom_call" | custom-call | flops 939524096 | bytes 18669828 | tf_op jit(solution)/shard_map/project/pallas_call | solution.py:50
  15.6 1.8 %collective-permute-start.5 = (bf16[32,1024]{1,0:T(8,128)(2,1)S(1)}, bf16[32,1024]{1,0:T(8,128)(2,1)S(1)}, u32[]{:S(2)}, u32[]{:S(2)}) collective-permute-start(bf16[32,1024]{1,0:T(8,128)(2,1)S(1)} %get-tuple-element.45), channel_id=1, source_target_pairs={{0,4},{4,0},{8,12},{12,8},{16,20},{20,16},{24,28},{28,24},{1,5},{5... | collective-permute-start | bytes 196616 | tf_op jit(solution)/shard_map/ppermute | solution.py:306
  17.4 1.6 %collective-permute-start.4 = (bf16[64,1024]{1,0:T(8,128)(2,1)S(1)}, bf16[64,1024]{1,0:T(8,128)(2,1)S(1)}, u32[]{:S(2)}, u32[]{:S(2)}) collective-permute-start(bf16[64,1024]{1,0:T(8,128)(2,1)S(1)} %get-tuple-element.42), channel_id=1, source_target_pairs={{0,2},{1,3},{2,0},{3,1},{4,6},{5,7},{6,4},{7,5},{8,10},{9,11},{10,... | collective-permute-start | bytes 393224 | tf_op jit(solution)/shard_map/ppermute | solution.py:306
  19.0 1.7 %collective-permute-start.12 = (bf16[64,1792]{1,0:T(8,128)(2,1)S(1)}, bf16[64,1792]{1,0:T(8,128)(2,1)S(1)}, u32[]{:S(2)}, u32[]{:S(2)}) collective-permute-start(bf16[64,1792]{1,0:T(8,128)(2,1)S(1)} %get-tuple-element.55.refs_2_), channel_id=1, source_target_pairs={{0,16},{4,20},{8,24},{12,28},{16,0},{20,4},{24,8},{28,12},{1,17},{... | collective-permute-start | bytes 688136 | tf_op jit(solution)/shard_map/ppermute | solution.py:306
  20.7 0.4 grads.1.refs_3_
  21.2 1.9 %collective-permute-done.4.refs_2_ = bf16[64,1024]{1,0:T(8,128)(2,1)S(1)} collective-permute-done((bf16[64,1024]{1,0:T(8,128)(2,1)S(1)}, bf16[64,1024]{1,0:T(8,128)(2,1)S(1)}, u32[]{:S(2)}, u32[]{:S(2)}) %collective-permute-start.4) | collective-permute-done | bytes 131104 | tf_op jit(solution)/shard_map/ppermute | solution.py:306
  23.0 0.3 stats.1
  23.4 1.2 %collective-permute-done.6 = f32[64,128]{1,0:T(8,128)S(1)} collective-permute-done((f32[64,128]{1,0:T(8,128)S(1)}, f32[64,128]{1,0:T(8,128)S(1)}, u32[]{:S(2)}, u32[]{:S(2)}) %collective-permute-start.6) | collective-permute-done | bytes 32800 | tf_op jit(solution)/shard_map/ppermute | solution.py:306
  24.7 1.5 %collective-permute-start.7 = (f32[64,128]{1,0:T(8,128)S(1)}, f32[64,128]{1,0:T(8,128)S(1)}, u32[]{:S(2)}, u32[]{:S(2)}) collective-permute-start(f32[64,128]{1,0:T(8,128)S(1)} %add.3.refs_0_), channel_id=1, source_target_pairs={{0,2},{1,3},{2,0},{3,1},{4,6},{5,7},{6,4},{7,5},{8,10},{9,11},{10,... | collective-permute-start | bytes 98312 | tf_op jit(solution)/shard_map/ppermute | solution.py:306
  26.2 2.4 %collective-permute-done.7.refs_1_ = f32[64,128]{1,0:T(8,128)S(1)} collective-permute-done((f32[64,128]{1,0:T(8,128)S(1)}, f32[64,128]{1,0:T(8,128)S(1)}, u32[]{:S(2)}, u32[]{:S(2)}) %collective-permute-start.7) | collective-permute-done | bytes 32800 | tf_op jit(solution)/shard_map/ppermute | solution.py:306
  28.6 0.4 direction.1
  29.0 1.6 %collective-permute-start.9 = (bf16[64,1024]{1,0:T(8,128)(2,1)S(1)}, bf16[64,1024]{1,0:T(8,128)(2,1)S(1)}, u32[]{:S(2)}, u32[]{:S(2)}) collective-permute-start(bf16[64,1024]{1,0:T(8,128)(2,1)S(1)} %get-tuple-element.50.refs_4_), channel_id=1, source_target_pairs={{0,2},{1,3},{2,0},{3,1},{4,6},{5,7},{6,4},{7,5},{8,10},{9,11},{10,... | collective-permute-start | bytes 393224 | tf_op jit(solution)/shard_map/ppermute | solution.py:306
  30.6 1.7 %collective-permute-start.11 = (bf16[16,1152]{1,0:T(8,128)(2,1)S(1)}, bf16[16,1152]{1,0:T(8,128)(2,1)S(1)}, u32[]{:S(2)}, u32[]{:S(2)}) collective-permute-start(bf16[16,1152]{1,0:T(8,128)(2,1)S(1)} %get-tuple-element.54.refs_0_), channel_id=1, source_target_pairs={{0,16},{4,20},{8,24},{12,28},{16,0},{20,4},{24,8},{28,12},{1,17},{... | collective-permute-start | bytes 110600 | tf_op jit(solution)/shard_map/ppermute | solution.py:306
  32.3 2.1 %activation.3 = (f32[64,1792]{1,0:T(8,128)S(1)}, f32[8,128]{1,0:T(8,128)S(1)}) custom-call(s32[1]{0:T(128)} %bitcast.refs_0_, bf16[1792,4096]{1,0:T(8,128)(2,1)S(1)} %bitcast.6, bf16[64,16]{1,0:T(8,128)(2,1)S(1)} %get-tuple-element.49.refs_2_, bf16[16,1792]{1,0:T(8,128)(2,1)S(1)} %bitcast.8, bf16[64,1024]{1,0:T(8,128)(2,1)S(1)} %get-tuple-element.50.refs_4_), custom_call_target="tpu_custom_call" | custom-call | flops 234881024 | bytes 14870532 | tf_op jit(solution)/shard_map/activation/pallas_call | solution.py:50
  34.4 1.0 %collective-permute-done.11.refs_1_ = bf16[16,1152]{1,0:T(8,128)(2,1)S(1)} collective-permute-done((bf16[16,1152]{1,0:T(8,128)(2,1)S(1)}, bf16[16,1152]{1,0:T(8,128)(2,1)S(1)}, u32[]{:S(2)}, u32[]{:S(2)}) %collective-permute-start.11) | collective-permute-done | bytes 36896 | tf_op jit(solution)/shard_map/ppermute | solution.py:306
  35.6 1.5 %collective-permute-start.13 = (bf16[16,2816]{1,0:T(8,128)(2,1)S(1)}, bf16[16,2816]{1,0:T(8,128)(2,1)S(1)}, u32[]{:S(2)}, u32[]{:S(2)}) collective-permute-start(bf16[16,2816]{1,0:T(8,128)(2,1)S(1)} %sum_far.1.refs_0_), channel_id=1, source_target_pairs={{0,4},{4,0},{8,12},{12,8},{16,20},{20,16},{24,28},{28,24},{1,5},{5... | collective-permute-start | bytes 270344 | tf_op jit(solution)/shard_map/ppermute | solution.py:306
  37.1 3.2 %activation.4 = (f32[64,1792]{1,0:T(8,128)S(1)}, f32[8,128]{1,0:T(8,128)S(1)}) custom-call(s32[1]{0:T(128)} %bitcast.refs_0_, bf16[1792,4096]{1,0:T(8,128)(2,1)S(1)} %bitcast.6, f32[64,1792]{1,0:T(8,128)S(1)} %get-tuple-element.51.refs_2_, bf16[64,1024]{1,0:T(8,128)(2,1)S(1)} %collective-permute-done.8.refs_3_, ...), custom_call_target="tpu_custom_call" | custom-call | flops 469762048 | bytes 15400964 | tf_op jit(solution)/shard_map/activation/pallas_call | solution.py:50
  40.3 1.7 %collective-permute-start.14 = (bf16[16,2816]{1,0:T(8,128)(2,1)S(1)}, bf16[16,2816]{1,0:T(8,128)(2,1)S(1)}, u32[]{:S(2)}, u32[]{:S(2)}) collective-permute-start(bf16[16,2816]{1,0:T(8,128)(2,1)S(1)} %sum_pairs.1.refs_0_), channel_id=1, source_target_pairs={{0,8},{4,12},{8,0},{12,4},{16,24},{20,28},{24,16},{28,20},{1,9},{5... | collective-permute-start | bytes 270344 | tf_op jit(solution)/shard_map/ppermute | solution.py:306
  42.0 2.7 %activation.5 = (bf16[64,1792]{1,0:T(8,128)(2,1)}, f32[8,128]{1,0:T(8,128)S(1)}) custom-call(s32[1]{0:T(128)} %bitcast.refs_0_, bf16[1792,4096]{1,0:T(8,128)(2,1)S(1)} %bitcast.6, f32[64,1792]{1,0:T(8,128)S(1)} %get-tuple-element.52.refs_2_, bf16[64,1024]{1,0:T(8,128)(2,1)S(1)} %collective-permute-done.10.refs_3_), custom_call_target="tpu_custom_call" | custom-call | flops 234881024 | bytes 15269892 | tf_op jit(solution)/shard_map/activation/pallas_call | solution.py:50
  44.7 0.7 %collective-permute-done.14.refs_1_ = bf16[16,2816]{1,0:T(8,128)(2,1)S(1)} collective-permute-done((bf16[16,2816]{1,0:T(8,128)(2,1)S(1)}, bf16[16,2816]{1,0:T(8,128)(2,1)S(1)}, u32[]{:S(2)}, u32[]{:S(2)}) %collective-permute-start.14) | collective-permute-done | bytes 90144 | tf_op jit(solution)/shard_map/ppermute | solution.py:306
  45.4 0.7 %sum_last.1 = (f32[16,1792]{1,0:T(8,128)}, f32[16,1024]{1,0:T(8,128)}) custom-call(bf16[16,2816]{1,0:T(8,128)(2,1)S(1)} %sum_pairs.1.refs_0_, bf16[16,2816]{1,0:T(8,128)(2,1)S(1)} %collective-permute-done.14.refs_1_, f32[8,128]{1,0:T(8,128)S(1)} %get-tuple-element.58.refs_2_), custom_call_target="tpu_custom_call" | custom-call | bytes 184320 | tf_op jit(solution)/shard_map/sum_last/pallas_call | solution.py:50
  (33 shorter events, 0.7 us)
Async XLA Ops:
  1.8 13.4 %collective-permute-start = (bf16[16,1024]{1,0:T(8,128)(2,1)S(1)}, bf16[16,1024]{1,0:T(8,128)(2,1)S(1)}, u32[]{:S(2)}, u32[]{:S(2)}) collective-permute-start(bf16[16,1024]{1,0:T(8,128)(2,1)S(1)} %get-tuple-element.36), channel_id=1, source_target_pairs={{0,8},{4,12},{8,0},{12,4},{16,24},{20,28},{24,16},{28,20},{1,9},{5... | collective-permute-start | bytes 98312 | tf_op jit(solution)/shard_map/ppermute | solution.py:306
  4.9 10.3 %collective-permute-start.1 = (bf16[16,1024]{1,0:T(8,128)(2,1)S(1)}, bf16[16,1024]{1,0:T(8,128)(2,1)S(1)}, u32[]{:S(2)}, u32[]{:S(2)}) collective-permute-start(bf16[16,1024]{1,0:T(8,128)(2,1)S(1)} %get-tuple-element.37), channel_id=1, source_target_pairs={{0,16},{4,20},{8,24},{12,28},{16,0},{20,4},{24,8},{28,12},{1,17},{... | collective-permute-start | bytes 98312 | tf_op jit(solution)/shard_map/ppermute | solution.py:306
  7.5 7.7 %collective-permute-start.2 = (bf16[16,1024]{1,0:T(8,128)(2,1)S(1)}, bf16[16,1024]{1,0:T(8,128)(2,1)S(1)}, u32[]{:S(2)}, u32[]{:S(2)}) collective-permute-start(bf16[16,1024]{1,0:T(8,128)(2,1)S(1)} %get-tuple-element.38), channel_id=1, source_target_pairs={{0,24},{4,28},{8,16},{12,20},{16,8},{20,12},{24,0},{28,4},{1,25},{... | collective-permute-start | bytes 98312 | tf_op jit(solution)/shard_map/ppermute | solution.py:306
  15.5 1.9 %collective-permute-start.3 = (bf16[64,2048]{1,0:T(8,128)(2,1)S(1)}, bf16[64,2048]{1,0:T(8,128)(2,1)S(1)}, u32[]{:S(2)}, u32[]{:S(2)}) collective-permute-start(bf16[64,2048]{1,0:T(8,128)(2,1)S(1)} %get-tuple-element.39), channel_id=1, source_target_pairs={{0,1},{1,0},{2,3},{3,2},{4,5},{5,4},{6,7},{7,6},{8,9},{9,8},{10,11... | collective-permute-start | bytes 786440 | tf_op jit(solution)/shard_map/ppermute | solution.py:306
  15.6 5.1 %collective-permute-start.5 = (bf16[32,1024]{1,0:T(8,128)(2,1)S(1)}, bf16[32,1024]{1,0:T(8,128)(2,1)S(1)}, u32[]{:S(2)}, u32[]{:S(2)}) collective-permute-start(bf16[32,1024]{1,0:T(8,128)(2,1)S(1)} %get-tuple-element.45), channel_id=1, source_target_pairs={{0,4},{4,0},{8,12},{12,8},{16,20},{20,16},{24,28},{28,24},{1,5},{5... | collective-permute-start | bytes 196616 | tf_op jit(solution)/shard_map/ppermute | solution.py:306
  17.3 14.9 %slice-start = ((s8[14680064]{0:T(1024)(128)(4,1)}), s8[4194304]{0:T(1024)(128)(4,1)S(1)}, s32[]{:S(2)}) async-start(s8[14680064]{0:T(1024)(128)(4,1)} %bitcast.5), calls=%async_computation | async-start | bytes 8388608
  17.4 5.6 %collective-permute-start.4 = (bf16[64,1024]{1,0:T(8,128)(2,1)S(1)}, bf16[64,1024]{1,0:T(8,128)(2,1)S(1)}, u32[]{:S(2)}, u32[]{:S(2)}) collective-permute-start(bf16[64,1024]{1,0:T(8,128)(2,1)S(1)} %get-tuple-element.42), channel_id=1, source_target_pairs={{0,2},{1,3},{2,0},{3,1},{4,6},{5,7},{6,4},{7,5},{8,10},{9,11},{10,... | collective-permute-start | bytes 393224 | tf_op jit(solution)/shard_map/ppermute | solution.py:306
  19.0 15.4 %collective-permute-start.12 = (bf16[64,1792]{1,0:T(8,128)(2,1)S(1)}, bf16[64,1792]{1,0:T(8,128)(2,1)S(1)}, u32[]{:S(2)}, u32[]{:S(2)}) collective-permute-start(bf16[64,1792]{1,0:T(8,128)(2,1)S(1)} %get-tuple-element.55.refs_2_), channel_id=1, source_target_pairs={{0,16},{4,20},{8,24},{12,28},{16,0},{20,4},{24,8},{28,12},{1,17},{... | collective-permute-start | bytes 688136 | tf_op jit(solution)/shard_map/ppermute | solution.py:306
  20.7 2.4 %copy-start = (bf16[16,4096]{1,0:T(8,128)(2,1)S(1)}, bf16[16,4096]{1,0:T(8,128)(2,1)}, u32[]{:S(2)}) copy-start(bf16[16,4096]{1,0:T(8,128)(2,1)} %refs_5_.4) | copy-start | bytes 393220
  20.7 11.6 %slice-start.1 = ((s8[14680064]{0:T(1024)(128)(4,1)}), s8[4194304]{0:T(1024)(128)(4,1)S(1)}, s32[]{:S(2)}) async-start(s8[14680064]{0:T(1024)(128)(4,1)} %bitcast.5), calls=%async_computation.1 | async-start | bytes 8388608
  20.7 11.6 %slice-start.2 = ((s8[14680064]{0:T(1024)(128)(4,1)}), s8[4194304]{0:T(1024)(128)(4,1)S(1)}, s32[]{:S(2)}) async-start(s8[14680064]{0:T(1024)(128)(4,1)} %bitcast.5), calls=%async_computation.2 | async-start | bytes 8388608
  20.7 11.6 %slice-start.3 = ((s8[14680064]{0:T(1024)(128)(4,1)}), s8[2097152]{0:T(1024)(128)(4,1)S(1)}, s32[]{:S(2)}) async-start(s8[14680064]{0:T(1024)(128)(4,1)} %bitcast.5), calls=%async_computation.3 | async-start | bytes 4194304
  20.7 11.6 %copy-start.1 = (bf16[1792,16]{0,1:T(8,128)(2,1)S(1)}, bf16[1792,16]{0,1:T(8,128)(2,1)}, u32[]{:S(2)}) copy-start(bf16[1792,16]{0,1:T(8,128)(2,1)} %param.12) | copy-start | bytes 172036
  23.4 1.3 %collective-permute-start.6 = (f32[64,128]{1,0:T(8,128)S(1)}, f32[64,128]{1,0:T(8,128)S(1)}, u32[]{:S(2)}, u32[]{:S(2)}) collective-permute-start(f32[64,128]{1,0:T(8,128)S(1)} %get-tuple-element.47), channel_id=1, source_target_pairs={{0,1},{1,0},{2,3},{3,2},{4,5},{5,4},{6,7},{7,6},{8,9},{9,8},{10,11... | collective-permute-start | bytes 98312 | tf_op jit(solution)/shard_map/ppermute | solution.py:306
  24.7 3.9 %collective-permute-start.7 = (f32[64,128]{1,0:T(8,128)S(1)}, f32[64,128]{1,0:T(8,128)S(1)}, u32[]{:S(2)}, u32[]{:S(2)}) collective-permute-start(f32[64,128]{1,0:T(8,128)S(1)} %add.3.refs_0_), channel_id=1, source_target_pairs={{0,2},{1,3},{2,0},{3,1},{4,6},{5,7},{6,4},{7,5},{8,10},{9,11},{10,... | collective-permute-start | bytes 98312 | tf_op jit(solution)/shard_map/ppermute | solution.py:306
  29.0 8.1 %collective-permute-start.9 = (bf16[64,1024]{1,0:T(8,128)(2,1)S(1)}, bf16[64,1024]{1,0:T(8,128)(2,1)S(1)}, u32[]{:S(2)}, u32[]{:S(2)}) collective-permute-start(bf16[64,1024]{1,0:T(8,128)(2,1)S(1)} %get-tuple-element.50.refs_4_), channel_id=1, source_target_pairs={{0,2},{1,3},{2,0},{3,1},{4,6},{5,7},{6,4},{7,5},{8,10},{9,11},{10,... | collective-permute-start | bytes 393224 | tf_op jit(solution)/shard_map/ppermute | solution.py:306
  30.6 6.5 %collective-permute-start.8 = (bf16[64,1024]{1,0:T(8,128)(2,1)S(1)}, bf16[64,1024]{1,0:T(8,128)(2,1)S(1)}, u32[]{:S(2)}, u32[]{:S(2)}) collective-permute-start(bf16[64,1024]{1,0:T(8,128)(2,1)S(1)} %get-tuple-element.50.refs_4_), channel_id=1, source_target_pairs={{0,1},{1,0},{2,3},{3,2},{4,5},{5,4},{6,7},{7,6},{8,9},{9,8},{10,11... | collective-permute-start | bytes 393224 | tf_op jit(solution)/shard_map/ppermute | solution.py:306
  30.6 4.9 %collective-permute-start.11 = (bf16[16,1152]{1,0:T(8,128)(2,1)S(1)}, bf16[16,1152]{1,0:T(8,128)(2,1)S(1)}, u32[]{:S(2)}, u32[]{:S(2)}) collective-permute-start(bf16[16,1152]{1,0:T(8,128)(2,1)S(1)} %get-tuple-element.54.refs_0_), channel_id=1, source_target_pairs={{0,16},{4,20},{8,24},{12,28},{16,0},{20,4},{24,8},{28,12},{1,17},{... | collective-permute-start | bytes 110600 | tf_op jit(solution)/shard_map/ppermute | solution.py:306
  35.6 4.7 %collective-permute-start.13 = (bf16[16,2816]{1,0:T(8,128)(2,1)S(1)}, bf16[16,2816]{1,0:T(8,128)(2,1)S(1)}, u32[]{:S(2)}, u32[]{:S(2)}) collective-permute-start(bf16[16,2816]{1,0:T(8,128)(2,1)S(1)} %sum_far.1.refs_0_), channel_id=1, source_target_pairs={{0,4},{4,0},{8,12},{12,8},{16,20},{20,16},{24,28},{28,24},{1,5},{5... | collective-permute-start | bytes 270344 | tf_op jit(solution)/shard_map/ppermute | solution.py:306
  37.1 4.9 %collective-permute-start.10 = (bf16[64,1024]{1,0:T(8,128)(2,1)S(1)}, bf16[64,1024]{1,0:T(8,128)(2,1)S(1)}, u32[]{:S(2)}, u32[]{:S(2)}) collective-permute-start(bf16[64,1024]{1,0:T(8,128)(2,1)S(1)} %collective-permute-done.9.refs_4_), channel_id=1, source_target_pairs={{0,1},{1,0},{2,3},{3,2},{4,5},{5,4},{6,7},{7,6},{8,9},{9,8},{10,11... | collective-permute-start | bytes 393224 | tf_op jit(solution)/shard_map/ppermute | solution.py:306
  40.3 5.1 %collective-permute-start.14 = (bf16[16,2816]{1,0:T(8,128)(2,1)S(1)}, bf16[16,2816]{1,0:T(8,128)(2,1)S(1)}, u32[]{:S(2)}, u32[]{:S(2)}) collective-permute-start(bf16[16,2816]{1,0:T(8,128)(2,1)S(1)} %sum_pairs.1.refs_0_), channel_id=1, source_target_pairs={{0,8},{4,12},{8,0},{12,4},{16,24},{20,28},{24,16},{28,20},{1,9},{5... | collective-permute-start | bytes 270344 | tf_op jit(solution)/shard_map/ppermute | solution.py:306

commit v6 on v5

--- a/solution.py
+++ b/solution.py
@@ -12,6 +12,7 @@
 F32, BF16 = jnp.float32, jnp.bfloat16
 LANES = 128
 ROWS = 256
+WIDE = 896
 STEP = 512
 WAIT = 5_000_000_000
 VMEM = pl.BlockSpec(memory_space=pltpu.VMEM)
@@ -275,12 +276,12 @@
 
     total = out_ref.shape[1]
 
-    @pl.loop(0, total // ROWS)
+    @pl.loop(0, total // WIDE)
     def _(i):
-        part(pl.multiple_of(i * ROWS, ROWS), ROWS)
-
-    if total % ROWS:
-        part(total - total % ROWS, total % ROWS)
+        part(pl.multiple_of(i * WIDE, WIDE), WIDE)
+
+    if total % WIDE:
+        part(total - total % WIDE, total % WIDE)
 
 
 def local(gradient_table, residual_input_rows, act, down_weight, adapter_input_factor, adapter_output_factor, lengths,

time: 46.3 us -> 45.7 us (0.987)
  Pallas kernels: 19.2 us -> 17.2 us
  waiting for transfers between devices: 7.25 us -> 8.84 us
    pallas_call x13, Pallas kernels: 19.2 us -> 17.2 us  [call(): pl.pallas_call(run, out_shape=[jax.ShapeDtypeStruct(*s) if isinstance(s,...]
    ppermute x15, waiting for transfers between devices: 7.25 us -> 8.84 us  [swap(): return lax.ppermute(x, axis, [(i, i ^ bit) for i in range(size)])]
  transfers between devices with their start and end apart: 15 -> 15, of which waited for: 5 -> 6; matrix products, arithmetic and copies ran while one was open for 0% -> 0% of each run, Pallas kernels for 37% -> 33%
where the time goes in v6:
time: 45.7 us; the launch traced here: 45.5 us
  starting transfers between devices  18.7 us (41%)
  Pallas kernels  17.2 us (38%)
  waiting for transfers between devices  8.84 us (19%)
  between operations  0.81 us (2%)
    ppermute x15, starting transfers between devices, swap(): return lax.ppermute(x, axis, [(i, i ^ bit) for i in range(size)])  18.7 us
    pallas_call x13, Pallas kernels, call(): pl.pallas_call(run, out_shape=[jax.ShapeDtypeStruct(*s) if isinstance(s,...  17.2 us
    ppermute x15, waiting for transfers between devices, swap(): return lax.ppermute(x, axis, [(i, i ^ bit) for i in range(size)])  8.84 us
  transfers between devices with their start and end apart: 15, of which 6 were waited for; matrix products, arithmetic and copies ran while one was open for 0% of the time, Pallas kernels for 33%

profile of v6, /device:TPU:0, one launch (start us, length us, event | category | flops | bytes accessed | tf_op | source)
XLA Modules:
  0.0 45.5 jit_solution(2107484304360202189)
XLA Ops:
  0.6 1.2 %route.1 = (bf16[16,1024]{1,0:T(8,128)(2,1)S(1)}, bf16[16,1024]{1,0:T(8,128)(2,1)S(1)}, bf16[16,1024]{1,0:T(8,128)(2,1)S(1)}, bf16[16,1024]{1,0:T(8,128)(2,1)S(1...) custom-call(s32[1]{0:T(128)} %bitcast.1.refs_0_, s32[1,512]{1,0:T(1,128)} %bitcast.9, s32[1,64]{1,0:T(1,128)} %refs_2_.1, ...), custom_call_target="tpu_custom_call" | custom-call | bytes 133380 | tf_op jit(solution)/shard_map/route/pallas_call | solution.py:51
  1.8 3.1 %collective-permute-start = (bf16[16,1024]{1,0:T(8,128)(2,1)S(1)}, bf16[16,1024]{1,0:T(8,128)(2,1)S(1)}, u32[]{:S(2)}, u32[]{:S(2)}) collective-permute-start(bf16[16,1024]{1,0:T(8,128)(2,1)S(1)} %get-tuple-element.36), channel_id=1, source_target_pairs={{0,8},{4,12},{8,0},{12,4},{16,24},{20,28},{24,16},{28,20},{1,9},{5... | collective-permute-start | bytes 98312 | tf_op jit(solution)/shard_map/ppermute | solution.py:307
  4.9 2.6 %collective-permute-start.1 = (bf16[16,1024]{1,0:T(8,128)(2,1)S(1)}, bf16[16,1024]{1,0:T(8,128)(2,1)S(1)}, u32[]{:S(2)}, u32[]{:S(2)}) collective-permute-start(bf16[16,1024]{1,0:T(8,128)(2,1)S(1)} %get-tuple-element.37), channel_id=1, source_target_pairs={{0,16},{4,20},{8,24},{12,28},{16,0},{20,4},{24,8},{28,12},{1,17},{... | collective-permute-start | bytes 98312 | tf_op jit(solution)/shard_map/ppermute | solution.py:307
  7.5 7.7 %project.1 = (f32[64,2048]{1,0:T(8,128)S(1)}, f32[64,2048]{1,0:T(8,128)S(1)}, bf16[64,1792]{1,0:T(8,128)(2,1)S(1)}, f32[64,16]{1,0:T(8,128)S(1)}) custom-call(s32[1]{0:T(128)} %bitcast.refs_0_, s32[64,1]{1,0:T(8,128)S(1)} %get-tuple-element.32.refs_1_, bf16[16,1792]{1,0:T(8,128)(2,1)} %bitcast.7, bf16[16,4096]{1,0:T(8,128)(2,1)} %refs_5_.4, ...), custom_call_target="tpu_custom_call" | custom-call | flops 939524096 | bytes 18669828 | tf_op jit(solution)/shard_map/project/pallas_call | solution.py:51
  15.6 1.8 %collective-permute-start.5 = (bf16[32,1024]{1,0:T(8,128)(2,1)S(1)}, bf16[32,1024]{1,0:T(8,128)(2,1)S(1)}, u32[]{:S(2)}, u32[]{:S(2)}) collective-permute-start(bf16[32,1024]{1,0:T(8,128)(2,1)S(1)} %get-tuple-element.45), channel_id=1, source_target_pairs={{0,4},{4,0},{8,12},{12,8},{16,20},{20,16},{24,28},{28,24},{1,5},{5... | collective-permute-start | bytes 196616 | tf_op jit(solution)/shard_map/ppermute | solution.py:307
  17.4 1.6 %collective-permute-start.4 = (bf16[64,1024]{1,0:T(8,128)(2,1)S(1)}, bf16[64,1024]{1,0:T(8,128)(2,1)S(1)}, u32[]{:S(2)}, u32[]{:S(2)}) collective-permute-start(bf16[64,1024]{1,0:T(8,128)(2,1)S(1)} %get-tuple-element.42), channel_id=1, source_target_pairs={{0,2},{1,3},{2,0},{3,1},{4,6},{5,7},{6,4},{7,5},{8,10},{9,11},{10,... | collective-permute-start | bytes 393224 | tf_op jit(solution)/shard_map/ppermute | solution.py:307
  19.0 1.7 %collective-permute-start.12 = (bf16[64,1792]{1,0:T(8,128)(2,1)S(1)}, bf16[64,1792]{1,0:T(8,128)(2,1)S(1)}, u32[]{:S(2)}, u32[]{:S(2)}) collective-permute-start(bf16[64,1792]{1,0:T(8,128)(2,1)S(1)} %get-tuple-element.55.refs_2_), channel_id=1, source_target_pairs={{0,16},{4,20},{8,24},{12,28},{16,0},{20,4},{24,8},{28,12},{1,17},{... | collective-permute-start | bytes 688136 | tf_op jit(solution)/shard_map/ppermute | solution.py:307
  20.7 0.4 grads.1.refs_3_
  21.2 1.9 %collective-permute-done.4.refs_2_ = bf16[64,1024]{1,0:T(8,128)(2,1)S(1)} collective-permute-done((bf16[64,1024]{1,0:T(8,128)(2,1)S(1)}, bf16[64,1024]{1,0:T(8,128)(2,1)S(1)}, u32[]{:S(2)}, u32[]{:S(2)}) %collective-permute-start.4) | collective-permute-done | bytes 131104 | tf_op jit(solution)/shard_map/ppermute | solution.py:307
  23.4 1.2 %collective-permute-done.6 = f32[64,128]{1,0:T(8,128)S(1)} collective-permute-done((f32[64,128]{1,0:T(8,128)S(1)}, f32[64,128]{1,0:T(8,128)S(1)}, u32[]{:S(2)}, u32[]{:S(2)}) %collective-permute-start.6) | collective-permute-done | bytes 32800 | tf_op jit(solution)/shard_map/ppermute | solution.py:307
  24.7 1.5 %collective-permute-start.7 = (f32[64,128]{1,0:T(8,128)S(1)}, f32[64,128]{1,0:T(8,128)S(1)}, u32[]{:S(2)}, u32[]{:S(2)}) collective-permute-start(f32[64,128]{1,0:T(8,128)S(1)} %add.3.refs_0_), channel_id=1, source_target_pairs={{0,2},{1,3},{2,0},{3,1},{4,6},{5,7},{6,4},{7,5},{8,10},{9,11},{10,... | collective-permute-start | bytes 98312 | tf_op jit(solution)/shard_map/ppermute | solution.py:307
  26.2 2.4 %collective-permute-done.7.refs_1_ = f32[64,128]{1,0:T(8,128)S(1)} collective-permute-done((f32[64,128]{1,0:T(8,128)S(1)}, f32[64,128]{1,0:T(8,128)S(1)}, u32[]{:S(2)}, u32[]{:S(2)}) %collective-permute-start.7) | collective-permute-done | bytes 32800 | tf_op jit(solution)/shard_map/ppermute | solution.py:307
  28.6 0.4 direction.1
  29.0 1.6 %collective-permute-start.9 = (bf16[64,1024]{1,0:T(8,128)(2,1)S(1)}, bf16[64,1024]{1,0:T(8,128)(2,1)S(1)}, u32[]{:S(2)}, u32[]{:S(2)}) collective-permute-start(bf16[64,1024]{1,0:T(8,128)(2,1)S(1)} %get-tuple-element.50.refs_4_), channel_id=1, source_target_pairs={{0,2},{1,3},{2,0},{3,1},{4,6},{5,7},{6,4},{7,5},{8,10},{9,11},{10,... | collective-permute-start | bytes 393224 | tf_op jit(solution)/shard_map/ppermute | solution.py:307
  30.6 1.7 %collective-permute-start.11 = (bf16[16,1152]{1,0:T(8,128)(2,1)S(1)}, bf16[16,1152]{1,0:T(8,128)(2,1)S(1)}, u32[]{:S(2)}, u32[]{:S(2)}) collective-permute-start(bf16[16,1152]{1,0:T(8,128)(2,1)S(1)} %get-tuple-element.54.refs_0_), channel_id=1, source_target_pairs={{0,16},{4,20},{8,24},{12,28},{16,0},{20,4},{24,8},{28,12},{1,17},{... | collective-permute-start | bytes 110600 | tf_op jit(solution)/shard_map/ppermute | solution.py:307
  32.3 1.4 %activation.3 = (f32[64,1792]{1,0:T(8,128)S(1)}, f32[8,128]{1,0:T(8,128)S(1)}) custom-call(s32[1]{0:T(128)} %bitcast.refs_0_, bf16[1792,4096]{1,0:T(8,128)(2,1)S(1)} %bitcast.6, bf16[64,16]{1,0:T(8,128)(2,1)S(1)} %get-tuple-element.49.refs_2_, bf16[16,1792]{1,0:T(8,128)(2,1)S(1)} %bitcast.8, bf16[64,1024]{1,0:T(8,128)(2,1)S(1)} %get-tuple-element.50.refs_4_), custom_call_target="tpu_custom_call" | custom-call | flops 234881024 | bytes 14870532 | tf_op jit(solution)/shard_map/activation/pallas_call | solution.py:51
  33.7 1.7 %collective-permute-done.11.refs_1_ = bf16[16,1152]{1,0:T(8,128)(2,1)S(1)} collective-permute-done((bf16[16,1152]{1,0:T(8,128)(2,1)S(1)}, bf16[16,1152]{1,0:T(8,128)(2,1)S(1)}, u32[]{:S(2)}, u32[]{:S(2)}) %collective-permute-start.11) | collective-permute-done | bytes 36896 | tf_op jit(solution)/shard_map/ppermute | solution.py:307
  35.6 1.5 %collective-permute-start.13 = (bf16[16,2816]{1,0:T(8,128)(2,1)S(1)}, bf16[16,2816]{1,0:T(8,128)(2,1)S(1)}, u32[]{:S(2)}, u32[]{:S(2)}) collective-permute-start(bf16[16,2816]{1,0:T(8,128)(2,1)S(1)} %sum_far.1.refs_0_), channel_id=1, source_target_pairs={{0,4},{4,0},{8,12},{12,8},{16,20},{20,16},{24,28},{28,24},{1,5},{5... | collective-permute-start | bytes 270344 | tf_op jit(solution)/shard_map/ppermute | solution.py:307
  37.1 2.5 %activation.4 = (f32[64,1792]{1,0:T(8,128)S(1)}, f32[8,128]{1,0:T(8,128)S(1)}) custom-call(s32[1]{0:T(128)} %bitcast.refs_0_, bf16[1792,4096]{1,0:T(8,128)(2,1)S(1)} %bitcast.6, f32[64,1792]{1,0:T(8,128)S(1)} %get-tuple-element.51.refs_2_, bf16[64,1024]{1,0:T(8,128)(2,1)S(1)} %collective-permute-done.8.refs_3_, ...), custom_call_target="tpu_custom_call" | custom-call | flops 469762048 | bytes 15400964 | tf_op jit(solution)/shard_map/activation/pallas_call | solution.py:51
  39.6 0.6 %collective-permute-done.13.refs_1_ = bf16[16,2816]{1,0:T(8,128)(2,1)S(1)} collective-permute-done((bf16[16,2816]{1,0:T(8,128)(2,1)S(1)}, bf16[16,2816]{1,0:T(8,128)(2,1)S(1)}, u32[]{:S(2)}, u32[]{:S(2)}) %collective-permute-start.13) | collective-permute-done | bytes 90144 | tf_op jit(solution)/shard_map/ppermute | solution.py:307
  40.2 1.5 %collective-permute-start.14 = (bf16[16,2816]{1,0:T(8,128)(2,1)S(1)}, bf16[16,2816]{1,0:T(8,128)(2,1)S(1)}, u32[]{:S(2)}, u32[]{:S(2)}) collective-permute-start(bf16[16,2816]{1,0:T(8,128)(2,1)S(1)} %sum_pairs.1.refs_0_), channel_id=1, source_target_pairs={{0,8},{4,12},{8,0},{12,4},{16,24},{20,28},{24,16},{28,20},{1,9},{5... | collective-permute-start | bytes 270344 | tf_op jit(solution)/shard_map/ppermute | solution.py:307
  41.8 2.0 %activation.5 = (bf16[64,1792]{1,0:T(8,128)(2,1)}, f32[8,128]{1,0:T(8,128)S(1)}) custom-call(s32[1]{0:T(128)} %bitcast.refs_0_, bf16[1792,4096]{1,0:T(8,128)(2,1)S(1)} %bitcast.6, f32[64,1792]{1,0:T(8,128)S(1)} %get-tuple-element.52.refs_2_, bf16[64,1024]{1,0:T(8,128)(2,1)S(1)} %collective-permute-done.10.refs_3_), custom_call_target="tpu_custom_call" | custom-call | flops 234881024 | bytes 15269892 | tf_op jit(solution)/shard_map/activation/pallas_call | solution.py:51
  43.8 1.0 %collective-permute-done.14.refs_1_ = bf16[16,2816]{1,0:T(8,128)(2,1)S(1)} collective-permute-done((bf16[16,2816]{1,0:T(8,128)(2,1)S(1)}, bf16[16,2816]{1,0:T(8,128)(2,1)S(1)}, u32[]{:S(2)}, u32[]{:S(2)}) %collective-permute-start.14) | collective-permute-done | bytes 90144 | tf_op jit(solution)/shard_map/ppermute | solution.py:307
  44.8 0.7 %sum_last.1 = (f32[16,1792]{1,0:T(8,128)}, f32[16,1024]{1,0:T(8,128)}) custom-call(bf16[16,2816]{1,0:T(8,128)(2,1)S(1)} %sum_pairs.1.refs_0_, bf16[16,2816]{1,0:T(8,128)(2,1)S(1)} %collective-permute-done.14.refs_1_, f32[8,128]{1,0:T(8,128)S(1)} %get-tuple-element.58.refs_2_), custom_call_target="tpu_custom_call" | custom-call | bytes 184320 | tf_op jit(solution)/shard_map/sum_last/pallas_call | solution.py:51
  (33 shorter events, 1.0 us)
Async XLA Ops:
  1.8 13.4 %collective-permute-start = (bf16[16,1024]{1,0:T(8,128)(2,1)S(1)}, bf16[16,1024]{1,0:T(8,128)(2,1)S(1)}, u32[]{:S(2)}, u32[]{:S(2)}) collective-permute-start(bf16[16,1024]{1,0:T(8,128)(2,1)S(1)} %get-tuple-element.36), channel_id=1, source_target_pairs={{0,8},{4,12},{8,0},{12,4},{16,24},{20,28},{24,16},{28,20},{1,9},{5... | collective-permute-start | bytes 98312 | tf_op jit(solution)/shard_map/ppermute | solution.py:307
  4.9 10.3 %collective-permute-start.1 = (bf16[16,1024]{1,0:T(8,128)(2,1)S(1)}, bf16[16,1024]{1,0:T(8,128)(2,1)S(1)}, u32[]{:S(2)}, u32[]{:S(2)}) collective-permute-start(bf16[16,1024]{1,0:T(8,128)(2,1)S(1)} %get-tuple-element.37), channel_id=1, source_target_pairs={{0,16},{4,20},{8,24},{12,28},{16,0},{20,4},{24,8},{28,12},{1,17},{... | collective-permute-start | bytes 98312 | tf_op jit(solution)/shard_map/ppermute | solution.py:307
  7.5 7.7 %collective-permute-start.2 = (bf16[16,1024]{1,0:T(8,128)(2,1)S(1)}, bf16[16,1024]{1,0:T(8,128)(2,1)S(1)}, u32[]{:S(2)}, u32[]{:S(2)}) collective-permute-start(bf16[16,1024]{1,0:T(8,128)(2,1)S(1)} %get-tuple-element.38), channel_id=1, source_target_pairs={{0,24},{4,28},{8,16},{12,20},{16,8},{20,12},{24,0},{28,4},{1,25},{... | collective-permute-start | bytes 98312 | tf_op jit(solution)/shard_map/ppermute | solution.py:307
  15.5 1.9 %collective-permute-start.3 = (bf16[64,2048]{1,0:T(8,128)(2,1)S(1)}, bf16[64,2048]{1,0:T(8,128)(2,1)S(1)}, u32[]{:S(2)}, u32[]{:S(2)}) collective-permute-start(bf16[64,2048]{1,0:T(8,128)(2,1)S(1)} %get-tuple-element.39), channel_id=1, source_target_pairs={{0,1},{1,0},{2,3},{3,2},{4,5},{5,4},{6,7},{7,6},{8,9},{9,8},{10,11... | collective-permute-start | bytes 786440 | tf_op jit(solution)/shard_map/ppermute | solution.py:307
  15.6 5.1 %collective-permute-start.5 = (bf16[32,1024]{1,0:T(8,128)(2,1)S(1)}, bf16[32,1024]{1,0:T(8,128)(2,1)S(1)}, u32[]{:S(2)}, u32[]{:S(2)}) collective-permute-start(bf16[32,1024]{1,0:T(8,128)(2,1)S(1)} %get-tuple-element.45), channel_id=1, source_target_pairs={{0,4},{4,0},{8,12},{12,8},{16,20},{20,16},{24,28},{28,24},{1,5},{5... | collective-permute-start | bytes 196616 | tf_op jit(solution)/shard_map/ppermute | solution.py:307
  17.3 14.9 %slice-start = ((s8[14680064]{0:T(1024)(128)(4,1)}), s8[4194304]{0:T(1024)(128)(4,1)S(1)}, s32[]{:S(2)}) async-start(s8[14680064]{0:T(1024)(128)(4,1)} %bitcast.5), calls=%async_computation | async-start | bytes 8388608
  17.4 5.6 %collective-permute-start.4 = (bf16[64,1024]{1,0:T(8,128)(2,1)S(1)}, bf16[64,1024]{1,0:T(8,128)(2,1)S(1)}, u32[]{:S(2)}, u32[]{:S(2)}) collective-permute-start(bf16[64,1024]{1,0:T(8,128)(2,1)S(1)} %get-tuple-element.42), channel_id=1, source_target_pairs={{0,2},{1,3},{2,0},{3,1},{4,6},{5,7},{6,4},{7,5},{8,10},{9,11},{10,... | collective-permute-start | bytes 393224 | tf_op jit(solution)/shard_map/ppermute | solution.py:307
  19.0 14.7 %collective-permute-start.12 = (bf16[64,1792]{1,0:T(8,128)(2,1)S(1)}, bf16[64,1792]{1,0:T(8,128)(2,1)S(1)}, u32[]{:S(2)}, u32[]{:S(2)}) collective-permute-start(bf16[64,1792]{1,0:T(8,128)(2,1)S(1)} %get-tuple-element.55.refs_2_), channel_id=1, source_target_pairs={{0,16},{4,20},{8,24},{12,28},{16,0},{20,4},{24,8},{28,12},{1,17},{... | collective-permute-start | bytes 688136 | tf_op jit(solution)/shard_map/ppermute | solution.py:307
  20.7 2.4 %copy-start = (bf16[16,4096]{1,0:T(8,128)(2,1)S(1)}, bf16[16,4096]{1,0:T(8,128)(2,1)}, u32[]{:S(2)}) copy-start(bf16[16,4096]{1,0:T(8,128)(2,1)} %refs_5_.4) | copy-start | bytes 393220
  20.7 11.6 %slice-start.1 = ((s8[14680064]{0:T(1024)(128)(4,1)}), s8[4194304]{0:T(1024)(128)(4,1)S(1)}, s32[]{:S(2)}) async-start(s8[14680064]{0:T(1024)(128)(4,1)} %bitcast.5), calls=%async_computation.1 | async-start | bytes 8388608
  20.7 11.6 %slice-start.2 = ((s8[14680064]{0:T(1024)(128)(4,1)}), s8[4194304]{0:T(1024)(128)(4,1)S(1)}, s32[]{:S(2)}) async-start(s8[14680064]{0:T(1024)(128)(4,1)} %bitcast.5), calls=%async_computation.2 | async-start | bytes 8388608
  20.7 11.6 %slice-start.3 = ((s8[14680064]{0:T(1024)(128)(4,1)}), s8[2097152]{0:T(1024)(128)(4,1)S(1)}, s32[]{:S(2)}) async-start(s8[14680064]{0:T(1024)(128)(4,1)} %bitcast.5), calls=%async_computation.3 | async-start | bytes 4194304
  20.7 11.6 %copy-start.1 = (bf16[1792,16]{0,1:T(8,128)(2,1)S(1)}, bf16[1792,16]{0,1:T(8,128)(2,1)}, u32[]{:S(2)}) copy-start(bf16[1792,16]{0,1:T(8,128)(2,1)} %param.12) | copy-start | bytes 172036
  23.4 1.3 %collective-permute-start.6 = (f32[64,128]{1,0:T(8,128)S(1)}, f32[64,128]{1,0:T(8,128)S(1)}, u32[]{:S(2)}, u32[]{:S(2)}) collective-permute-start(f32[64,128]{1,0:T(8,128)S(1)} %get-tuple-element.47), channel_id=1, source_target_pairs={{0,1},{1,0},{2,3},{3,2},{4,5},{5,4},{6,7},{7,6},{8,9},{9,8},{10,11... | collective-permute-start | bytes 98312 | tf_op jit(solution)/shard_map/ppermute | solution.py:307
  24.7 3.9 %collective-permute-start.7 = (f32[64,128]{1,0:T(8,128)S(1)}, f32[64,128]{1,0:T(8,128)S(1)}, u32[]{:S(2)}, u32[]{:S(2)}) collective-permute-start(f32[64,128]{1,0:T(8,128)S(1)} %add.3.refs_0_), channel_id=1, source_target_pairs={{0,2},{1,3},{2,0},{3,1},{4,6},{5,7},{6,4},{7,5},{8,10},{9,11},{10,... | collective-permute-start | bytes 98312 | tf_op jit(solution)/shard_map/ppermute | solution.py:307
  29.0 8.1 %collective-permute-start.9 = (bf16[64,1024]{1,0:T(8,128)(2,1)S(1)}, bf16[64,1024]{1,0:T(8,128)(2,1)S(1)}, u32[]{:S(2)}, u32[]{:S(2)}) collective-permute-start(bf16[64,1024]{1,0:T(8,128)(2,1)S(1)} %get-tuple-element.50.refs_4_), channel_id=1, source_target_pairs={{0,2},{1,3},{2,0},{3,1},{4,6},{5,7},{6,4},{7,5},{8,10},{9,11},{10,... | collective-permute-start | bytes 393224 | tf_op jit(solution)/shard_map/ppermute | solution.py:307
  30.6 6.5 %collective-permute-start.8 = (bf16[64,1024]{1,0:T(8,128)(2,1)S(1)}, bf16[64,1024]{1,0:T(8,128)(2,1)S(1)}, u32[]{:S(2)}, u32[]{:S(2)}) collective-permute-start(bf16[64,1024]{1,0:T(8,128)(2,1)S(1)} %get-tuple-element.50.refs_4_), channel_id=1, source_target_pairs={{0,1},{1,0},{2,3},{3,2},{4,5},{5,4},{6,7},{7,6},{8,9},{9,8},{10,11... | collective-permute-start | bytes 393224 | tf_op jit(solution)/shard_map/ppermute | solution.py:307
  30.6 4.9 %collective-permute-start.11 = (bf16[16,1152]{1,0:T(8,128)(2,1)S(1)}, bf16[16,1152]{1,0:T(8,128)(2,1)S(1)}, u32[]{:S(2)}, u32[]{:S(2)}) collective-permute-start(bf16[16,1152]{1,0:T(8,128)(2,1)S(1)} %get-tuple-element.54.refs_0_), channel_id=1, source_target_pairs={{0,16},{4,20},{8,24},{12,28},{16,0},{20,4},{24,8},{28,12},{1,17},{... | collective-permute-start | bytes 110600 | tf_op jit(solution)/shard_map/ppermute | solution.py:307
  35.6 4.6 %collective-permute-start.13 = (bf16[16,2816]{1,0:T(8,128)(2,1)S(1)}, bf16[16,2816]{1,0:T(8,128)(2,1)S(1)}, u32[]{:S(2)}, u32[]{:S(2)}) collective-permute-start(bf16[16,2816]{1,0:T(8,128)(2,1)S(1)} %sum_far.1.refs_0_), channel_id=1, source_target_pairs={{0,4},{4,0},{8,12},{12,8},{16,20},{20,16},{24,28},{28,24},{1,5},{5... | collective-permute-start | bytes 270344 | tf_op jit(solution)/shard_map/ppermute | solution.py:307
  37.1 4.7 %collective-permute-start.10 = (bf16[64,1024]{1,0:T(8,128)(2,1)S(1)}, bf16[64,1024]{1,0:T(8,128)(2,1)S(1)}, u32[]{:S(2)}, u32[]{:S(2)}) collective-permute-start(bf16[64,1024]{1,0:T(8,128)(2,1)S(1)} %collective-permute-done.9.refs_4_), channel_id=1, source_target_pairs={{0,1},{1,0},{2,3},{3,2},{4,5},{5,4},{6,7},{7,6},{8,9},{9,8},{10,11... | collective-permute-start | bytes 393224 | tf_op jit(solution)/shard_map/ppermute | solution.py:307
  40.2 4.6 %collective-permute-start.14 = (bf16[16,2816]{1,0:T(8,128)(2,1)S(1)}, bf16[16,2816]{1,0:T(8,128)(2,1)S(1)}, u32[]{:S(2)}, u32[]{:S(2)}) collective-permute-start(bf16[16,2816]{1,0:T(8,128)(2,1)S(1)} %sum_pairs.1.refs_0_), channel_id=1, source_target_pairs={{0,8},{4,12},{8,0},{12,4},{16,24},{20,28},{24,16},{28,20},{1,9},{5... | collective-permute-start | bytes 270344 | tf_op jit(solution)/shard_map/ppermute | solution.py:307
